TPU v7x, 256 devices: a whole 4x4x8 slice. The times are simulated.
256 devices in a mesh: rows: 32 (over z, y), dim: 8 (over x, core).
Axes of the slice: x: 4, y: 4, z: 8, core: 2. Of those that a mesh axis runs over, the one named last changes fastest.
Arguments:
- embeddings: bfloat16 [294912, 4096], P('rows', 'dim'), may hold values from -1 to 1
- quality: float32 [294912], P(('rows', 'dim')), may hold values from 0.5 to 4
- picked_rows: int32 [3, 64], replicated, may hold values from 0 to 294911, as said below
Outputs:
- factor_rows: float32 [294912, 192], P(('rows', 'dim'))
- residual_diag: float32 [294912], P(('rows', 'dim'))
Inputs may be any that keep to these rules, and one draw needn't show every extreme that they name: `picked_rows`: all 192 indices are different.
All inputs are finite; a program needn't handle non-finite values.
Results may differ from a plain program's by a relative error of at most 0.0003.
Values may be sent and summed in bfloat16 or wider, within the bound.
No kernel may reach another device: no remote copies, remote signals or barrier semaphores. Data moves between devices by JAX's collectives and lax.ppermute only.
A program may use at most 128 MiB of HBM per device.

v0:
```python
import jax
import jax.numpy as jnp
from jax import lax
from jax.sharding import PartitionSpec as P

ridge_term = 0.5


def per_device(embeddings, quality, picked_rows):
    rows_here, dims_here = embeddings.shape
    rounds_total, pick_count = picked_rows.shape
    total_rank = rounds_total * pick_count
    dim_devices = lax.axis_size("dim")
    portion = rows_here // dim_devices
    block_start = lax.axis_index("rows") * rows_here
    my_part = lax.axis_index("dim")
    first_row = block_start + my_part * portion
    row_global = first_row + jnp.arange(portion, dtype=jnp.int32)
    eye_block = jnp.eye(pick_count, dtype=jnp.float32)
    partial_norms = jnp.einsum(
        "rd,rd->r", embeddings, embeddings, preferred_element_type=jnp.float32
    )
    norms_mine = lax.psum_scatter(partial_norms, "dim", scatter_dimension=0, tiled=True)
    residual_diag = quality * quality * (norms_mine + ridge_term)
    factor_rows = jnp.zeros((portion, total_rank), jnp.float32)
    all_chosen = picked_rows.reshape(total_rank)
    local_index = all_chosen - block_start
    held_here = (local_index >= 0) & (local_index < rows_here)
    safe_index = jnp.clip(local_index, 0, rows_here - 1)
    masked_rows = jnp.where(held_here[:, None], embeddings[safe_index], jnp.zeros((), jnp.bfloat16))
    collected = lax.all_gather(masked_rows, "rows", axis=0, tiled=True)
    pick_all = jnp.sum(collected.reshape(-1, total_rank, dims_here), axis=0, dtype=jnp.bfloat16)
    for counter in range(rounds_total):
        low_col = counter * pick_count
        high_col = (counter + 1) * pick_count
        chosen = picked_rows[counter]
        pick_emb = pick_all[low_col:high_col]
        mine_index = chosen - first_row
        mine_here = (mine_index >= 0) & (mine_index < portion)
        mine_safe = jnp.clip(mine_index, 0, portion - 1)
        factor_masked = jnp.where(mine_here[:, None], factor_rows[mine_safe], 0.0)
        quality_masked = jnp.where(mine_here, quality[mine_safe], 0.0)
        pick_factor, pick_quality = lax.psum((factor_masked, quality_masked), ("rows", "dim"))
        gram_part = jnp.einsum("pd,qd->pq", pick_emb, pick_emb, preferred_element_type=jnp.float32)
        full_rows = jnp.einsum(
            "rd,pd->rp", embeddings, pick_emb, preferred_element_type=jnp.float32
        )
        summed_rows, pick_gram = lax.psum((full_rows, gram_part), "dim")
        kernel_rows = lax.dynamic_slice_in_dim(summed_rows, my_part * portion, portion, 0)
        kernel_rows = kernel_rows + ridge_term * (row_global[:, None] == chosen[None, :]).astype(
            jnp.float32
        )
        schur = quality[:, None] * pick_quality[None, :] * kernel_rows - jnp.dot(
            factor_rows, pick_factor.T, precision=lax.Precision.HIGHEST
        )
        pick_kernel = pick_quality[:, None] * pick_quality[None, :] * (
            pick_gram + ridge_term * eye_block
        ) - jnp.dot(pick_factor, pick_factor.T, precision=lax.Precision.HIGHEST)
        lower_factor = jnp.linalg.cholesky(pick_kernel)
        new_columns = jax.scipy.linalg.solve_triangular(lower_factor, schur.T, lower=True).T
        factor_rows = factor_rows.at[:, low_col:high_col].set(new_columns)
        residual_diag = residual_diag - jnp.sum(new_columns * new_columns, axis=1)
    return (factor_rows, residual_diag)


def solution(mesh):
    return jax.shard_map(
        per_device,
        mesh=mesh,
        in_specs=(P("rows", "dim"), P(("rows", "dim")), P()),
        out_specs=(P(("rows", "dim"), None), P(("rows", "dim"))),
        check_vma=False,
    )
```

profile of v0, /device:TPU:1, one launch (start us, length us, event | category | flops | bytes accessed | tf_op | source)
XLA Modules:
  0.0 482.6 jit_solution(2851351119712041183)
XLA Ops:
  7.2 0.0 all-gather.2.cloned.1.call-start
  7.2 0.7 subtract_clamp_fusion
  7.9 0.7 compare_and_fusion.2
  8.6 0.1 min.37
  8.7 0.1 and.47
  8.8 5.9 %gather_fusion.1 = bf16[192,512]{1,0:T(8,128)(2,1)S(1)} fusion(bf16[9216,512]{1,0:T(8,128)(2,1)} %param.12, s32[1024]{0:T(1024)S(1)} %pad_clamp_fusion.2), kind=kCustom, calls=%fused_computation.1 | custom fusion | bytes 393984 | tf_op jit(solution)/shard_map/gather | solution.py:30
  14.7 0.8 broadcast_select_fusion
  15.5 0.0 all-reduce.11.cloned.1.call-start
  15.6 5.9 %fusion = f32[9216]{0:T(1024)} fusion(bf16[9216,512]{1,0:T(8,128)(2,1)} %param.12), kind=kLoop, calls=%fused_computation.8 | loop fusion | flops 14146560 | bytes 9474048 | tf_op jit(solution)/shard_map/rd,rd->r/dot_general | solution.py:20
  21.5 86.4 %all-gather.2.cloned.1.call-done = bf16[6144,512]{1,0:T(8,128)(2,1)} async-done(((bf16[192,512]{1,0:T(8,128)(2,1)}), bf16[6144,512]{1,0:T(8,128)(2,1)}) %all-gather.2.cloned.1.call-update) | async-done | bytes 6291472 | tf_op jit(solution)/shard_map/all_gather | solution.py:31
  107.8 3.7 reduce_sum.36
  111.6 0.8 fusion.21
  112.3 0.8 fusion.24
  113.1 0.8 fusion.27
  113.9 8.0 %convolution_bitcast_fusion = f32[9216,64]{0,1:T(8,128)} fusion(bf16[9216,512]{1,0:T(8,128)(2,1)} %param.12, bf16[192,512]{1,0:T(8,128)(2,1)S(1)} %reduce_sum.36), kind=kOutput, calls=%fused_computation.9 | convolution fusion | flops 603979776 | bytes 11862016 | tf_op jit(solution)/shard_map/rd,pd->rp/dot_general | solution.py:45
  121.9 8.0 %convolution_bitcast_fusion.1 = f32[9216,64]{0,1:T(8,128)} fusion(bf16[9216,512]{1,0:T(8,128)(2,1)} %param.12, bf16[192,512]{1,0:T(8,128)(2,1)S(1)} %reduce_sum.36), kind=kOutput, calls=%fused_computation.10 | convolution fusion | flops 603979776 | bytes 11862016 | tf_op jit(solution)/shard_map/rd,pd->rp/dot_general | solution.py:45
  129.9 0.0 all-reduce.13.cloned.1.call-start
  130.0 8.1 %convolution_bitcast_fusion.2 = f32[9216,64]{0,1:T(8,128)} fusion(bf16[9216,512]{1,0:T(8,128)(2,1)} %param.12, bf16[192,512]{1,0:T(8,128)(2,1)S(1)} %reduce_sum.36), kind=kOutput, calls=%fused_computation.11 | convolution fusion | flops 603979776 | bytes 11862016 | tf_op jit(solution)/shard_map/rd,pd->rp/dot_general | solution.py:45
  138.2 0.6 copy-done.2
  138.8 0.8 gather_fusion.3
  139.6 0.8 gather_fusion.5
  140.4 0.8 gather_fusion
  141.2 0.1 broadcast_in_dim.76
  141.2 0.7 gather_fusion.2
  141.9 0.6 dynamic-slice.26
  143.2 0.6 compare_reduce_fusion.4
  143.8 0.7 compare_reduce_fusion.3
  144.5 0.1 broadcast_select_fusion.2
  144.6 75.8 %all-reduce.5 = (f32[64,192]{1,0:T(8,128)S(1)}, f32[64]{0:T(128)S(1)}) all-reduce(f32[64,192]{1,0:T(8,128)S(1)} %broadcast_select_fusion.2, f32[64]{0:T(128)S(1)} %get-tuple-element.68), channel_id=1, replica_groups=mesh['rows'=32,'dim'=8] {'rows','dim'}, use_global_device_ids=true, to_apply=%region_4.5 | all-reduce | flops 12352 | bytes 98816 | tf_op jit(solution)/shard_map/psum | solution.py:43
  220.4 0.1 multiply_reduce_fusion.3
  220.6 1.0 convolution_subtract_fusion.4
  221.6 0.1 copy.29
  221.7 5.8 %cholesky.59 = f32[64,64]{1,0:T(8,128)S(1)} custom-call(f32[64,64]{1,0:T(8,128)S(1)} %fusion.41), custom_call_target="Cholesky" | custom-call | tf_op jit(solution)/shard_map/jit(cholesky)/cholesky | solution.py:59
  227.5 0.6 compare_reduce_fusion.2
  228.2 0.7 fusion.29
  228.8 4.9 %custom-call.7 = f32[1,64,64]{1,2,0:T(8,128)S(1)} custom-call(f32[1,64,64]{2,1,0:T(8,128)S(1)} %fusion.29), custom_call_target="InvertDiagBlocksLowerTriangular" | custom-call | tf_op jit(solution)/shard_map/jit(_solve_triangular)/triangular_solve | solution.py:60
  233.7 55.9 %all-reduce.13.cloned.1.call-done = (f32[9216,64]{0,1:T(8,128)}, f32[9216,64]{0,1:T(8,128)}, f32[9216,64]{0,1:T(8,128)}) async-done(((f32[9216,64]{0,1:T(8,128)}, f32[9216,64]{0,1:T(8,128)}, f32[9216,64]{0,1:T(8,128)}), (f32[9216,64]{0,1:T(8,128)}, f32[9216,64]{0,1:T(8,128)}, f32[9216,64]{0,1:T(8,128)})) %all-reduce.13.cloned.1.call-update) | async-done | bytes 7077904 | tf_op jit(solution)/shard_map/psum | solution.py:48
  289.6 2.1 multiply_reduce_fusion.2
  291.8 0.2 copy.31
  292.0 0.1 scatter.10
  292.1 0.6 gather_fusion.4
  292.7 0.1 pad_select_fusion
  292.7 77.2 %all-reduce.4 = (f32[64,192]{1,0:T(8,128)S(1)}, f32[64]{0:T(128)S(1)}) all-reduce(f32[64,192]{1,0:T(8,128)S(1)} %pad_select_fusion, f32[64]{0:T(128)S(1)} %get-tuple-element.66), channel_id=1, replica_groups=mesh['rows'=32,'dim'=8] {'rows','dim'}, use_global_device_ids=true, to_apply=%region_12.15 | all-reduce | flops 12352 | bytes 98816 | tf_op jit(solution)/shard_map/psum | solution.py:43
  369.9 0.2 convolution_subtract_fusion.3
  370.1 0.1 copy.33
  370.2 5.8 %cholesky.70 = f32[64,64]{1,0:T(8,128)S(1)} custom-call(f32[64,64]{1,0:T(8,128)S(1)} %fusion.39), custom_call_target="Cholesky" | custom-call | tf_op jit(solution)/shard_map/jit(cholesky)/cholesky | solution.py:59
  376.1 0.6 compare_reduce_fusion.1
  376.7 0.7 fusion.30
  377.4 4.9 %custom-call.8 = f32[1,64,64]{1,2,0:T(8,128)S(1)} custom-call(f32[1,64,64]{2,1,0:T(8,128)S(1)} %fusion.30), custom_call_target="InvertDiagBlocksLowerTriangular" | custom-call | tf_op jit(solution)/shard_map/jit(_solve_triangular)/triangular_solve | solution.py:60
  382.3 1.4 fusion.1
  383.7 1.1 bitcast_dynamic-update-slice_fusion
  384.9 0.4 copy.35
  385.2 0.7 gather_fusion.6
  385.9 0.1 broadcast_select_fusion.1
  386.0 74.1 %all-reduce.3 = (f32[64,192]{1,0:T(8,128)S(1)}, f32[64]{0:T(128)S(1)}) all-reduce(f32[64,192]{1,0:T(8,128)S(1)} %broadcast_select_fusion.1, f32[64]{0:T(128)S(1)} %get-tuple-element.53), channel_id=1, replica_groups=mesh['rows'=32,'dim'=8] {'rows','dim'}, use_global_device_ids=true, to_apply=%region_16.19 | all-reduce | flops 12352 | bytes 98816 | tf_op jit(solution)/shard_map/psum | solution.py:43
  460.0 0.2 convolution_subtract_fusion.2
  460.3 0.1 copy.37
  460.3 5.8 %cholesky.81 = f32[64,64]{1,0:T(8,128)S(1)} custom-call(f32[64,64]{1,0:T(8,128)S(1)} %fusion.36), custom_call_target="Cholesky" | custom-call | tf_op jit(solution)/shard_map/jit(cholesky)/cholesky | solution.py:59
  466.2 0.6 compare_reduce_fusion
  466.9 0.7 fusion.31
  467.5 4.9 %custom-call.9 = f32[1,64,64]{1,2,0:T(8,128)S(1)} custom-call(f32[1,64,64]{2,1,0:T(8,128)S(1)} %fusion.31), custom_call_target="InvertDiagBlocksLowerTriangular" | custom-call | tf_op jit(solution)/shard_map/jit(_solve_triangular)/triangular_solve | solution.py:60
  472.5 1.7 fusion.2
  474.1 0.5 multiply_reduce_fusion
  474.6 1.4 fusion.45
  (30 shorter events, 0.3 us)
Async XLA Ops:
  7.2 100.7 %all-gather.2.cloned.1.call-start = ((), (), s32[]{:S(2)}) async-start(), calls=%async_computation | async-start | bytes 6488064 | tf_op jit(solution)/shard_map/all_gather | solution.py:31
  15.5 205.0 %all-reduce.11.cloned.1.call-start = ((), (), s32[]{:S(2)}) async-start(), calls=%async_computation.1 | async-start | bytes 270336 | tf_op jit(solution)/shard_map/psum | solution.py:48
  129.9 159.7 %all-reduce.13.cloned.1.call-start = ((), (), s32[]{:S(2)}) async-start(), calls=%async_computation.2 | async-start | bytes 14155776 | tf_op jit(solution)/shard_map/psum | solution.py:48
  138.1 0.7 copy-start.2
  138.1 0.7 copy-start
  138.1 3.8 copy-start.5
  220.6 149.3 %copy-start.4 = (f32[64,64]{0,1:T(8,128)S(1)}, f32[64,64]{0,1:T(8,128)}, u32[]{:S(2)}) copy-start(f32[64,64]{0,1:T(8,128)} %get-tuple-element.47) | copy-start | bytes 49156
  382.3 77.7 %copy-start.3 = (f32[64,64]{0,1:T(8,128)S(1)}, f32[64,64]{0,1:T(8,128)}, u32[]{:S(2)}) copy-start(f32[64,64]{0,1:T(8,128)} %get-tuple-element.48) | copy-start | bytes 49156
  474.6 1.5 copy-start.1
Sparse Core Ops, SparseCore 0:
  15.6 92.1 all-gather.1
  130.1 58.6 all-reduce.10
  191.5 98.0 all-reduce.12
where the time goes:
time: 483 us
  blocking collectives  227 us (47%)
  waiting for transfers between devices  142 us (29%)
  other arithmetic  51.2 us (11%)
  matrix products  34.6 us (7%)
  between operations  14.7 us (3%)
  local copies, waits for them, and re-layouts  12.5 us (3%)
    psum x3, blocking collectives, per_device(): lax.psum((factor_masked, quality_masked), ('rows', 'dim'))  227 us
    all_gather x1, waiting for transfers between devices, per_device(): collected = lax.all_gather(masked_rows, 'rows', axis=0, tiled=True)  86.4 us
    psum x2, waiting for transfers between devices, per_device(): summed_rows, pick_gram = lax.psum((full_rows, gram_part), 'dim')  55.9 us
    dot_general x3, matrix products, per_device(): jnp.einsum('rd,pd->rp', embeddings, pick_emb, preferred_element_type=jnp....  24.2 us
    another operation x9, other arithmetic, per_device(): lower_factor = jnp.linalg.cholesky(pick_kernel)  19.6 us
    another operation x6, other arithmetic, per_device(): jax.scipy.linalg.solve_triangular(lower_factor, schur.T, lower=True)  16.6 us
  transfers between devices with their start and end apart: 3, of which 2 were waited for; matrix products, arithmetic and copies ran while one was open for 7% of the time, Pallas kernels for 0%

commit v1 on v0

v1 whole, which is shorter than its diff:
```python
import functools

import jax
import jax.numpy as jnp
from jax import lax
from jax.experimental import pallas as pl
from jax.experimental.pallas import tpu as pltpu
from jax.sharding import PartitionSpec as P

ridge_term = 0.5
pack = 1152
Y, Z, X = 4, 8, 4
HIGHEST = lax.Precision.HIGHEST
NT = (((1,), (1,)), ((), ()))
TN = (((0,), (0,)), ((), ()))
f32, bf16, i32, i16 = jnp.float32, jnp.bfloat16, jnp.int32, jnp.int16
VMEM = pl.BlockSpec(memory_space=pltpu.VMEM)
levels = 32767.0


def params(mib):
    return pltpu.CompilerParams(vmem_limit_bytes=mib << 20)


def cost(flops, nbytes):
    return pl.CostEstimate(flops=int(flops), bytes_accessed=int(nbytes), transcendentals=0)


def shape(dims, dtype):
    return jax.ShapeDtypeStruct(dims, dtype)


def as_column(row):
    n = row.shape[1]
    eye = lax.broadcasted_iota(i32, (n, n), 0) == lax.broadcasted_iota(i32, (n, n), 1)
    wide = jnp.broadcast_to(row.astype(f32), (n, n))
    return jnp.sum(jnp.where(eye, wide, 0.0), axis=1, keepdims=True).astype(i32)


def pick_kernel(picks_ref, e_ref, *rest):
    outs, (idx_ref, acc_ref) = rest[:Y], rest[Y:]
    step = pl.program_id(0)
    tile = e_ref.shape[0]
    rounds, count = picks_ref.shape
    total = rounds * count
    row_start = lax.axis_index("rows") * (tile * pl.num_programs(0))

    @pl.when(step == 0)
    def _():
        for r in range(rounds):
            column = as_column(picks_ref[r : r + 1, :]) - row_start
            idx_ref[r * count : (r + 1) * count, :] = jnp.broadcast_to(column, (count, 128))
        acc_ref[...] = jnp.zeros_like(acc_ref)

    here = idx_ref[...] - step * tile
    lane = lax.broadcasted_iota(i32, (total, 128), 1)
    hot = jnp.concatenate(
        [jnp.where(here == lane + 128 * j, 1.0, 0.0).astype(bf16) for j in range(tile // 128)], axis=1
    )
    acc_ref[...] += jnp.dot(hot, e_ref[...], preferred_element_type=f32)

    @pl.when(step == pl.num_programs(0) - 1)
    def _():
        y = lax.rem(lax.axis_index("rows"), Y)
        group = total // Y
        for j in range(Y):
            g = lax.rem(y + j, Y)
            outs[j][...] = acc_ref[pl.ds(pl.multiple_of(g * group, 16), group), :].astype(bf16)


def local_picks(picks, embeddings):
    rows, dims = embeddings.shape
    total = picks.size
    tile = 1024
    return pl.pallas_call(
        pick_kernel,
        grid=(rows // tile,),
        in_specs=[VMEM, pl.BlockSpec((tile, dims), lambda i: (i, 0))],
        out_specs=[pl.BlockSpec((total // Y, dims), lambda i: (0, 0))] * Y,
        out_shape=[shape((total // Y, dims), bf16)] * Y,
        scratch_shapes=[pltpu.VMEM((total, 128), i32), pltpu.VMEM((total, dims), f32)],
        compiler_params=params(48),
        cost_estimate=cost(2 * rows * dims * total, rows * dims * 2),
        name="local_picks",
    )(picks, embeddings)


def gram_kernel(s0, s1, s2, s3, mine_ref, other_ref, gram_ref):
    y = lax.rem(lax.axis_index("rows"), Y)
    group = s0.shape[0] // 2
    for j, ref in enumerate((s0, s1, s2, s3)):
        g = pl.multiple_of(lax.rem(y + (Y - j), Y) * group, 16)
        mine_ref[pl.ds(g, group), :] = ref[:group, :]
        other_ref[pl.ds(g, group), :] = ref[group:, :]
    mine, other = mine_ref[...], other_ref[...]
    gram = lax.dot_general(mine, mine, NT, preferred_element_type=f32)
    gram += lax.dot_general(other, other, NT, preferred_element_type=f32)
    core = lax.rem(lax.axis_index("dim"), 2)

    @pl.when(core == 0)
    def _():
        gram_ref[...] = gram[:128, :128]

    @pl.when(core == 1)
    def _():
        gram_ref[...] = jnp.zeros_like(gram_ref)
        gram_ref[:64, :] = gram[128:, :128]
        gram_ref[64:, :64] = gram[128:, 128:]


def picks_and_gram(parts):
    both, dims = parts[0].shape
    total = both // 2 * Y
    return pl.pallas_call(
        gram_kernel,
        in_specs=[VMEM] * Y,
        out_specs=[VMEM] * 3,
        out_shape=[shape((total, dims), bf16), shape((total, dims), bf16), shape((128, 128), f32)],
        compiler_params=params(16),
        cost_estimate=cost(4 * total * total * dims, 4 * total * dims),
        name="gram",
    )(*parts)


panel = 32


def factor_kernel(mine_ref, other_ref, inverse_ref, m_ref):
    n = inverse_ref.shape[0]
    core = lax.rem(lax.axis_index("dim"), 2)
    first = jnp.where(core == 0, mine_ref[...], other_ref[...])
    last = jnp.where(core == 0, other_ref[...], mine_ref[...])
    width = m_ref.shape[1]
    sub = lax.broadcasted_iota(i32, (n, width - 128), 0)
    lane = lax.broadcasted_iota(i32, (n, width - 128), 1) + 128
    m_ref[:, 128:] = jnp.where(lane - n == sub, 1.0, 0.0)
    diag = lax.broadcasted_iota(i32, (128, 128), 0) == lax.broadcasted_iota(i32, (128, 128), 1)
    ridge = jnp.where(diag, ridge_term, 0.0)
    m_ref[:128, :128] = first + ridge
    m_ref[128:, :128] = last[:64, :]
    m_ref[128:, 128:n] = last[64:, :64] + ridge[:64, :64]
    m_ref[:128, 128:n] = last[:64, :].T
    below = lax.broadcasted_iota(i32, (panel, 1), 0)
    at = lax.broadcasted_iota(i32, (panel, width), 1) - lax.broadcasted_iota(i32, (panel, width), 0)
    for low in range(0, n, panel):
        rows = m_ref[low : low + panel, :]
        for t in range(0, panel, 2):
            c1, c2 = rows[:, low + t : low + t + 1], rows[:, low + t + 1 : low + t + 2]
            r1, r2 = rows[t : t + 1, :], rows[t + 1 : t + 2, :]
            a, b, d = c1[t : t + 1], c2[t : t + 1], c2[t + 1 : t + 2]
            over_a = 1.0 / a
            l = b * over_a
            over_d = 1.0 / (d - l * b)
            m1 = jnp.where(below > t, c1 * over_a, 0.0)
            m2 = jnp.where(below > t + 1, (c2 - l * c1) * over_d, 0.0)
            rows = rows - m1 * r1 - m2 * (r2 - l * r1)
        pivots = jnp.sum(jnp.where(at == low, rows, 0.0), axis=1, keepdims=True)
        rows = rows * (1.0 / jnp.sqrt(pivots))
        inverse_ref[low : low + panel, :] = rows[:, n:]
        if low + panel < n:
            update = lax.dot_general(rows[:, :n], rows, TN, precision=HIGHEST, preferred_element_type=f32)
            m_ref[low + panel :, :] -= update[low + panel :, :]


def factor_inverse(mine, other, n):
    return pl.pallas_call(
        factor_kernel,
        in_specs=[VMEM] * 2,
        out_specs=VMEM,
        out_shape=shape((n, n), f32),
        scratch_shapes=[pltpu.VMEM((n, 2 * n), f32)],
        compiler_params=params(16),
        cost_estimate=cost(1e10, 1 << 20),
        name="factor",
    )(mine, other)


def block_products(e_ref, r_ref, mine_ref, other_ref):
    e, r = e_ref[...], r_ref[...]
    part = lax.dot_general(mine_ref[...], e, NT, preferred_element_type=f32)
    part += lax.dot_general(other_ref[...], r, NT, preferred_element_type=f32)
    squares = jnp.zeros((e.shape[0], 128), f32)
    for j in range(0, e.shape[1], 128):
        ej, rj = e[:, j : j + 128].astype(f32), r[:, j : j + 128].astype(f32)
        squares += ej * ej + rj * rj
    norm = lax.dot_general(jnp.ones((8, 128), f32), squares, NT, precision=HIGHEST, preferred_element_type=f32)
    return part, norm


def split(value):
    scaled = value * 16.0
    high = jnp.floor(scaled)
    return high, jnp.floor((scaled - high) * 32768.0)


def join(high, low):
    return (high + low * (1.0 / 32768.0)) * (1.0 / 16.0)


def send_kernel(place_ref, e_ref, r_ref, mine_ref, other_ref, out_ref):
    part, norm = block_products(e_ref, r_ref, mine_ref, other_ref)
    norm_high, norm_low = split(norm[:1])
    top_high, top_low = split(jnp.max(jnp.abs(part), axis=0, keepdims=True))
    scale = join(top_high, top_low + 1.0)
    coded = jnp.floor(part * (levels / scale) + 0.5)
    row = lax.broadcasted_iota(i32, (8, part.shape[1]), 0)
    extra = jnp.where(row == 0, norm_high, jnp.where(row == 1, norm_low, jnp.where(row == 2, top_high, top_low)))
    out_ref[...] = jnp.concatenate([coded, extra], axis=0).astype(i32).astype(i16)


def keep_kernel(place_ref, e_ref, r_ref, mine_ref, other_ref, out_ref, norm_ref):
    part, norm = block_products(e_ref, r_ref, mine_ref, other_ref)
    out_ref[...] = part
    norm_ref[...] = norm


def products(hop, place, embeddings, received, mine, other, tile=384):
    total, dims = mine.shape
    steps = pack // tile

    def own(i, place):
        return (lax.rem(place[0] + hop, X) * 2 + place[1]) * steps + i, 0

    def got(i, place):
        return lax.rem(place[0] + hop, X) * steps + i, 0

    def fixed(i, place):
        return 0, 0

    def along(i, place):
        return 0, i

    send = hop > 0
    out_shape = [shape((total + 8, pack), i16)] if send else [shape((total, pack), f32), shape((8, pack), f32)]
    return pl.pallas_call(
        send_kernel if send else keep_kernel,
        grid_spec=pltpu.PrefetchScalarGridSpec(
            num_scalar_prefetch=1,
            grid=(steps,),
            in_specs=[
                pl.BlockSpec((tile, dims), own),
                pl.BlockSpec((tile, dims), got),
                pl.BlockSpec((total, dims), fixed),
                pl.BlockSpec((total, dims), fixed),
            ],
            out_specs=[pl.BlockSpec((s.shape[0], tile), along) for s in out_shape],
        ),
        out_shape=out_shape,
        compiler_params=params(32),
        cost_estimate=cost(4 * pack * dims * total, 4 * pack * dims),
        name="products_%d" % hop,
    )(place, embeddings, received, mine, other)


def finish_kernel(picks_ref, quality_ref, own_ref, norm_ref, g1, g2, g3, inverse_ref, out_ref, resid_ref):
    total, width = own_ref.shape
    rounds, count = picks_ref.shape
    first_row = (lax.axis_index("rows") * (2 * X) + lax.axis_index("dim")) * width
    chosen = jnp.concatenate([as_column(picks_ref[r : r + 1, :]) for r in range(rounds)], axis=0) - first_row
    inverse = inverse_ref[...]
    tile = 384
    for low in range(0, width, tile):
        here = pl.ds(low, tile)
        values, norm = own_ref[:, here], norm_ref[:1, here]
        for ref in (g1, g2, g3):
            got = ref[:, here].astype(i32).astype(f32)
            scale = join(got[total + 2 : total + 3], got[total + 3 : total + 4] + 1.0)
            values = values + got[:total] * (scale * (1.0 / levels))
            norm = norm + join(got[total : total + 1], got[total + 1 : total + 2] + 0.5)
        lane = lax.broadcasted_iota(i32, (total, tile), 1) + low
        values = jnp.where(chosen == lane, values + ridge_term, values)
        columns = jnp.dot(inverse, values, precision=HIGHEST, preferred_element_type=f32)
        score = quality_ref[here].reshape(1, tile)
        out_ref[:, here] = columns * score
        left = norm + ridge_term - jnp.sum(columns * columns, axis=0, keepdims=True)
        resid_ref[here] = (score * score * left).reshape(tile)


def finish(picks, quality, own, norm, got, inverse):
    total, width = own.shape
    return pl.pallas_call(
        finish_kernel,
        in_specs=[VMEM] * 8,
        out_specs=[VMEM] * 2,
        out_shape=[shape((total, width), f32), shape((width,), f32)],
        compiler_params=params(32),
        cost_estimate=cost(12 * total * total * width, 4 << 20),
        name="finish",
    )(picks, quality, own, norm, *got, inverse)


def along_y(k):
    return [(r, r // Y * Y + (r % Y + k) % Y) for r in range(Y * Z)]


def along_z(k):
    return [(r, (r // Y + k) % Z * Y + r % Y) for r in range(Y * Z)]


def along_x(k):
    return [(d, (d // 2 + k) % X * 2 + d % 2) for d in range(2 * X)]


def both_ways_z(k):
    pairs = []
    for r in range(Y * Z):
        for d in range(2 * X):
            z = (r // Y + (k if d % 2 == 0 else -k)) % Z
            pairs.append((r * 2 * X + d, (z * Y + r % Y) * 2 * X + d))
    return pairs


swap = [(d, d ^ 1) for d in range(2 * X)]


def per_device(embeddings, quality, picked_rows):
    rows_here, dims_here = embeddings.shape
    total = picked_rows.size
    group = total // Y
    d = lax.axis_index("dim")
    place = jnp.stack([d // 2, d % 2]).astype(i32)

    with jax.named_scope("swap_rows"):
        halves = embeddings.reshape(X, 2, pack, dims_here)
        away = lax.dynamic_index_in_dim(halves, 1 - d % 2, 1, keepdims=False)
        received = lax.ppermute(away.reshape(X * pack, dims_here), "dim", swap)

    with jax.named_scope("gather_picks"):
        parts = local_picks(picked_rows, embeddings)
        mine = parts[0]
        for k in range(1, Y):
            mine = mine + lax.ppermute(parts[k], "rows", along_y(k))
        both = jnp.concatenate([mine, lax.ppermute(mine, "dim", swap)], axis=0)
        arrived = [lax.ppermute(both, ("rows", "dim"), both_ways_z(k)) for k in (1, 2, 3)]
        far = lax.ppermute(mine, "rows", along_z(4))
        near = arrived[0] + arrived[1] + arrived[2]
        partial = jnp.concatenate([near[:group] + mine + far, near[group:]], axis=0)
        turned = lax.ppermute(partial, "dim", swap)
        full = partial + jnp.concatenate([turned[group:], turned[:group]], axis=0)
        groups = [full] + [lax.ppermute(full, "rows", along_y(k)) for k in range(1, Y)]

    pick_mine, pick_other, gram = picks_and_gram(groups)
    with jax.named_scope("sum_gram"):
        for_sum = [lax.ppermute(gram, "dim", along_x(k)) for k in (1, 2, 3)]
        gram = gram + for_sum[0] + for_sum[1] + for_sum[2]
        gram_other = lax.ppermute(gram, "dim", swap)

    got = []
    for hop in (2, 1, 3):
        coded = products(hop, place, embeddings, received, pick_mine, pick_other)[0]
        got.append(lax.ppermute(coded, "dim", along_x(hop)))
    own, norm = products(0, place, embeddings, received, pick_mine, pick_other)
    inverse = factor_inverse(gram, gram_other, total)
    columns, residual = finish(picked_rows, quality, own, norm, got, inverse)
    return columns.T, residual


def solution(mesh):
    return jax.shard_map(
        per_device,
        mesh=mesh,
        in_specs=(P("rows", "dim"), P(("rows", "dim")), P()),
        out_specs=(P(("rows", "dim"), None), P(("rows", "dim"))),
        check_vma=False,
    )
```

time: 483 us -> 109 us (0.23)
  blocking collectives: 227 us -> 0 us
  waiting for transfers between devices: 142 us -> 20.1 us
  other arithmetic: 51.2 us -> 0.17 us
  Pallas kernels: 0 us -> 44.8 us
  matrix products: 34.6 us -> 0 us
  starting transfers between devices: 0.12 us -> 33.7 us
  between operations: 14.7 us -> 0.78 us
    psum x3 -> x0, blocking collectives: 227 us -> none  [per_device(): lax.psum((factor_masked, quality_masked), ('rows', 'dim'))]
    all_gather x1 -> x0, waiting for transfers between devices: 86.4 us -> none  [per_device(): collected = lax.all_gather(masked_rows, 'rows', axis=0, tiled=True)]
    psum x2 -> x0, waiting for transfers between devices: 55.9 us -> none  [per_device(): summed_rows, pick_gram = lax.psum((full_rows, gram_part), 'dim')]
    pallas_call x0 -> x8, Pallas kernels: none -> 44.8 us  [the longest x1 18.6 us: factor_inverse(): pl.pallas_call(factor_kernel, in_specs=[VMEM] * 2, out_specs=VMEM, out_sh...]
    another operation x18 -> x1, other arithmetic: 37.7 us -> 0.07 us  [per_device(): place = jnp.stack([d // 2, d % 2]).astype(i32)]
    ppermute x0 -> x20, starting transfers between devices: none -> 33.7 us  [the longest x3 7.23 us: per_device(): lax.ppermute(both, ('rows', 'dim'), both_ways_z(k))]
    dot_general x11 -> x0, matrix products: 30.9 us -> none  [the longest x3 24.2 us: per_device(): jnp.einsum('rd,pd->rp', embeddings, pick_emb, preferred_element_type=jnp....]
    ppermute x0 -> x20, waiting for transfers between devices: none -> 20.1 us  [the longest x3 5.02 us: per_device(): mine = mine + lax.ppermute(parts[k], 'rows', along_y(k))]
  transfers between devices with their start and end apart: 3 -> 20, of which waited for: 2 -> 12; matrix products, arithmetic and copies ran while one was open for 7% -> 0% of each run, Pallas kernels for 0% -> 39%
where the time goes in v1:
time: 109 us; the launch traced here: 108 us
  Pallas kernels  44.8 us (41%)
  starting transfers between devices  33.7 us (31%)
  waiting for transfers between devices  20.1 us (18%)
  local copies, waits for them, and re-layouts  8.5 us (8%)
    pallas_call x1, Pallas kernels, factor_inverse(): pl.pallas_call(factor_kernel, in_specs=[VMEM] * 2, out_specs=VMEM, out_sh...  18.6 us
    pallas_call x4, Pallas kernels, products(): pl.pallas_call(send_kernel if send else keep_kernel, grid_spec=pltpu.Pref...  15.1 us
    pallas_call x1, Pallas kernels, local_picks(): pl.pallas_call(pick_kernel, grid=(rows // tile,), in_specs=[VMEM, pl.Bloc...  8.31 us
    ppermute x3, starting transfers between devices, per_device(): lax.ppermute(both, ('rows', 'dim'), both_ways_z(k))  7.23 us
    ppermute x3, waiting for transfers between devices, per_device(): mine = mine + lax.ppermute(parts[k], 'rows', along_y(k))  5.02 us
    dynamic_slice x1, local copies, waits for them, and re-layouts, per_device(): away = lax.dynamic_index_in_dim(halves, 1 - d % 2, 1, keepdims=False)  4.8 us
    ppermute x3, waiting for transfers between devices, per_device(): lax.ppermute(full, 'rows', along_y(k))  4.6 us
    ppermute x1, starting transfers between devices, per_device(): far = lax.ppermute(mine, 'rows', along_z(4))  4.49 us
  transfers between devices with their start and end apart: 20, of which 12 were waited for; matrix products, arithmetic and copies ran while one was open for 0% of the time, Pallas kernels for 39%

profile of v1, /device:TPU:1, one launch (start us, length us, event | category | flops | bytes accessed | tf_op | source)
XLA Modules:
  0.0 108.0 jit_solution(8253649502585822982)
XLA Ops:
  0.6 0.0 copy-start.2
  0.7 4.8 %constant_dynamic-slice_fusion = bf16[4,1,1152,512]{3,2,1,0:T(8,128)(2,1)} fusion(bf16[4,2,1152,512]{3,2,1,0:T(8,128)(2,1)} %bitcast.7, s32[]{:T(128)S(6)} %select_n.19), kind=kLoop, calls=%fused_computation.9 | loop fusion | bytes 9437188 | tf_op jit(solution)/shard_map/swap_rows/jit(dynamic_index_in_dim)/dynamic_slice | solution.py:325
  5.5 3.2 %collective-permute-start = (bf16[4608,512]{1,0:T(8,128)(2,1)}, bf16[4608,512]{1,0:T(8,128)(2,1)}, u32[]{:S(2)}, u32[]{:S(2)}) collective-permute-start(bf16[4608,512]{1,0:T(8,128)(2,1)} %bitcast.3), channel_id=1, source_target_pairs={{0,1},{1,0},{2,3},{3,2},{4,5},{5,4},{6,7},{7,6},{8,9},{9,8},{10,11... | collective-permute-start | bytes 14155784 | tf_op jit(solution)/shard_map/swap_rows/ppermute | solution.py:326
  8.7 0.0 copy-done.2
  8.7 8.3 %local_picks.1 = (bf16[48,512]{1,0:T(8,128)(2,1)S(1)}, bf16[48,512]{1,0:T(8,128)(2,1)S(1)}, bf16[48,512]{1,0:T(8,128)(2,1)S(1)}, bf16[48,512]{1,0:T(8,128)(2,1)S(1)}) custom-call(s32[3,64]{1,0:T(4,128)S(1)} %copy-done.2, bf16[9216,512]{1,0:T(8,128)(2,1)} %e_ref.9), custom_call_target="tpu_custom_call" | custom-call | flops 1811939328 | bytes 9437184 | tf_op jit(solution)/shard_map/gather_picks/local_picks/pallas_call | solution.py:75
  17.0 1.1 collective-permute-start.3
  18.1 0.3 collective-permute-start.2
  18.4 0.7 collective-permute-start.1
  19.1 1.3 %collective-permute-done.3 = bf16[48,512]{1,0:T(8,128)(2,1)S(1)} collective-permute-done((bf16[48,512]{1,0:T(8,128)(2,1)S(1)}, bf16[48,512]{1,0:T(8,128)(2,1)S(1)}, u32[]{:S(2)}, u32[]{:S(2)}) %collective-permute-start.3) | collective-permute-done | bytes 49184 | tf_op jit(solution)/shard_map/gather_picks/ppermute | solution.py:332
  20.5 2.1 %collective-permute-done.2 = bf16[48,512]{1,0:T(8,128)(2,1)S(1)} collective-permute-done((bf16[48,512]{1,0:T(8,128)(2,1)S(1)}, bf16[48,512]{1,0:T(8,128)(2,1)S(1)}, u32[]{:S(2)}, u32[]{:S(2)}) %collective-permute-start.2) | collective-permute-done | bytes 49184 | tf_op jit(solution)/shard_map/gather_picks/ppermute | solution.py:332
  22.6 1.6 %collective-permute-done.1 = bf16[48,512]{1,0:T(8,128)(2,1)S(1)} collective-permute-done((bf16[48,512]{1,0:T(8,128)(2,1)S(1)}, bf16[48,512]{1,0:T(8,128)(2,1)S(1)}, u32[]{:S(2)}, u32[]{:S(2)}) %collective-permute-start.1) | collective-permute-done | bytes 49184 | tf_op jit(solution)/shard_map/gather_picks/ppermute | solution.py:332
  24.2 0.7 collective-permute-start.4
  24.9 0.9 collective-permute-done.4
  25.8 6.5 %collective-permute-start.7 = (bf16[96,512]{1,0:T(8,128)(2,1)S(1)}, bf16[96,512]{1,0:T(8,128)(2,1)S(1)}, u32[]{:S(2)}, u32[]{:S(2)}) collective-permute-start(bf16[96,512]{1,0:T(8,128)(2,1)S(1)} %pad_maximum_fusion), channel_id=1, source_target_pairs={{0,96},{1,161},{2,98},{3,163},{4,100},{5,165},{6,102},{7,167},{8,1... | collective-permute-start | bytes 294920 | tf_op jit(solution)/shard_map/gather_picks/ppermute | solution.py:334
  32.3 0.7 collective-permute-start.5
  33.0 0.0 collective-permute-start.6
  33.0 4.5 %collective-permute-start.8 = (bf16[48,512]{1,0:T(8,128)(2,1)S(1)}, bf16[48,512]{1,0:T(8,128)(2,1)S(1)}, u32[]{:S(2)}, u32[]{:S(2)}) collective-permute-start(bf16[48,512]{1,0:T(8,128)(2,1)S(1)} %add_add_fusion.2), channel_id=1, source_target_pairs={{0,128},{8,136},{16,144},{24,152},{32,160},{40,168},{48,176},{56,1... | collective-permute-start | bytes 147464 | tf_op jit(solution)/shard_map/gather_picks/ppermute | solution.py:335
  37.5 0.0 collective-permute-done.7
  37.5 1.0 collective-permute-done.5
  38.5 2.2 %collective-permute-done.6 = bf16[96,512]{1,0:T(8,128)(2,1)S(1)} collective-permute-done((bf16[96,512]{1,0:T(8,128)(2,1)S(1)}, bf16[96,512]{1,0:T(8,128)(2,1)S(1)}, u32[]{:S(2)}, u32[]{:S(2)}) %collective-permute-start.6) | collective-permute-done | bytes 98336 | tf_op jit(solution)/shard_map/gather_picks/ppermute | solution.py:334
  40.7 1.2 %collective-permute-done.8 = bf16[48,512]{1,0:T(8,128)(2,1)S(1)} collective-permute-done((bf16[48,512]{1,0:T(8,128)(2,1)S(1)}, bf16[48,512]{1,0:T(8,128)(2,1)S(1)}, u32[]{:S(2)}, u32[]{:S(2)}) %collective-permute-start.8) | collective-permute-done | bytes 49184 | tf_op jit(solution)/shard_map/gather_picks/ppermute | solution.py:335
  42.0 2.0 %collective-permute-start.9 = (bf16[96,512]{1,0:T(8,128)(2,1)S(1)}, bf16[96,512]{1,0:T(8,128)(2,1)S(1)}, u32[]{:S(2)}, u32[]{:S(2)}) collective-permute-start(bf16[96,512]{1,0:T(8,128)(2,1)S(1)} %pad_maximum_fusion.1), channel_id=1, source_target_pairs={{0,1},{1,0},{2,3},{3,2},{4,5},{5,4},{6,7},{7,6},{8,9},{9,8},{10,11... | collective-permute-start | bytes 294920 | tf_op jit(solution)/shard_map/gather_picks/ppermute | solution.py:338
  44.0 0.9 collective-permute-done.9
  45.0 0.1 collective-permute-start.10
  45.1 1.5 %collective-permute-start.11 = (bf16[96,512]{1,0:T(8,128)(2,1)S(1)}, bf16[96,512]{1,0:T(8,128)(2,1)S(1)}, u32[]{:S(2)}, u32[]{:S(2)}) collective-permute-start(bf16[96,512]{1,0:T(8,128)(2,1)S(1)} %maximum_add_fusion.s0), channel_id=1, source_target_pairs={{0,16},{8,24},{16,0},{24,8},{32,48},{40,56},{48,32},{56,40},{64,80... | collective-permute-start | bytes 294920 | tf_op jit(solution)/shard_map/gather_picks/ppermute | solution.py:340
  46.5 1.5 %collective-permute-start.12 = (bf16[96,512]{1,0:T(8,128)(2,1)S(1)}, bf16[96,512]{1,0:T(8,128)(2,1)S(1)}, u32[]{:S(2)}, u32[]{:S(2)}) collective-permute-start(bf16[96,512]{1,0:T(8,128)(2,1)S(1)} %maximum_add_fusion.s0), channel_id=1, source_target_pairs={{0,24},{8,0},{16,8},{24,16},{32,56},{40,32},{48,40},{56,48},{64,88... | collective-permute-start | bytes 294920 | tf_op jit(solution)/shard_map/gather_picks/ppermute | solution.py:340
  48.0 4.6 %collective-permute-done.10.s1 = bf16[96,512]{1,0:T(8,128)(2,1)S(1)} collective-permute-done((bf16[96,512]{1,0:T(8,128)(2,1)S(1)}, bf16[96,512]{1,0:T(8,128)(2,1)S(1)}, u32[]{:S(2)}, u32[]{:S(2)}) %collective-permute-start.10) | collective-permute-done | bytes 98336 | tf_op jit(solution)/shard_map/gather_picks/ppermute | solution.py:340
  52.6 0.0 collective-permute-done.11.s2
  52.6 0.0 collective-permute-done.12.s3
  52.6 0.3 gram.1
  53.0 2.7 %collective-permute-start.18 = (f32[128,128]{1,0:T(8,128)S(1)}, f32[128,128]{1,0:T(8,128)S(1)}, u32[]{:S(2)}, u32[]{:S(2)}) collective-permute-start(f32[128,128]{1,0:T(8,128)S(1)} %get-tuple-element.21), channel_id=1, source_target_pairs={{0,6},{1,7},{2,0},{3,1},{4,2},{5,3},{6,4},{7,5},{8,14},{9,15},{10,... | collective-permute-start | bytes 196616 | tf_op jit(solution)/shard_map/sum_gram/ppermute | solution.py:344
  55.6 0.4 collective-permute-start.17
  56.0 0.6 collective-permute-start.16
  56.7 0.1 pad_add_fusion.place_ref
  56.7 0.2 collective-permute-done.18
  57.0 3.3 %collective-permute-done.17 = f32[128,128]{1,0:T(8,128)S(1)} collective-permute-done((f32[128,128]{1,0:T(8,128)S(1)}, f32[128,128]{1,0:T(8,128)S(1)}, u32[]{:S(2)}, u32[]{:S(2)}) %collective-permute-start.17) | collective-permute-done | bytes 65568 | tf_op jit(solution)/shard_map/sum_gram/ppermute | solution.py:344
  60.3 0.6 collective-permute-done.16
  61.0 3.2 %collective-permute-start.19 = (f32[128,128]{1,0:T(8,128)S(1)}, f32[128,128]{1,0:T(8,128)S(1)}, u32[]{:S(2)}, u32[]{:S(2)}) collective-permute-start(f32[128,128]{1,0:T(8,128)S(1)} %add_add_fusion.1.mine_ref), channel_id=1, source_target_pairs={{0,1},{1,0},{2,3},{3,2},{4,5},{5,4},{6,7},{7,6},{8,9},{9,8},{10,11... | collective-permute-start | bytes 196616 | tf_op jit(solution)/shard_map/sum_gram/ppermute | solution.py:346
  64.1 0.0 collective-permute-done.r_ref
  64.1 0.0 copy-start
  64.1 3.7 %copy-done = bf16[9216,512]{1,0:T(8,128)(2,1)S(1)} copy-done((bf16[9216,512]{1,0:T(8,128)(2,1)S(1)}, bf16[9216,512]{1,0:T(8,128)(2,1)}, u32[]{:S(2)}) %copy-start) | copy-done | bytes 9437208
  67.8 3.8 %products_2.1 = s16[200,1152]{1,0:T(8,128)(2,1)S(1)} custom-call(s32[2]{0:T(128)S(1)} %pad_add_fusion.place_ref, bf16[9216,512]{1,0:T(8,128)(2,1)S(1)} %copy-done, bf16[4608,512]{1,0:T(8,128)(2,1)} %collective-permute-done.r_ref, bf16[192,512]{1,0:T(8,128)(2,1)S(1)} %get-tuple-element.17.mine_ref, bf16[192,512]{1,0:T(8,128)(2,1)S(1)} %get-tuple-element.18.other_ref), custom_call_target="tpu_custom_call" | custom-call | flops 452984832 | bytes 2359296 | tf_op jit(solution)/shard_map/products_2/pallas_call | solution.py:235
  71.6 1.1 %collective-permute-start.13 = (s16[200,1152]{1,0:T(8,128)(2,1)S(1)}, s16[200,1152]{1,0:T(8,128)(2,1)S(1)}, u32[]{:S(2)}, u32[]{:S(2)}) collective-permute-start(s16[200,1152]{1,0:T(8,128)(2,1)S(1)} %products_2.1), channel_id=1, source_target_pairs={{0,4},{1,5},{2,6},{3,7},{4,0},{5,1},{6,2},{7,3},{8,12},{9,13},{10,... | collective-permute-start | bytes 1382408 | tf_op jit(solution)/shard_map/ppermute | solution.py:351
  72.8 3.8 %products_1.1 = s16[200,1152]{1,0:T(8,128)(2,1)S(1)} custom-call(s32[2]{0:T(128)S(1)} %pad_add_fusion.place_ref, bf16[9216,512]{1,0:T(8,128)(2,1)S(1)} %copy-done, bf16[4608,512]{1,0:T(8,128)(2,1)} %collective-permute-done.r_ref, bf16[192,512]{1,0:T(8,128)(2,1)S(1)} %get-tuple-element.17.mine_ref, bf16[192,512]{1,0:T(8,128)(2,1)S(1)} %get-tuple-element.18.other_ref), custom_call_target="tpu_custom_call" | custom-call | flops 452984832 | bytes 2359296 | tf_op jit(solution)/shard_map/products_1/pallas_call | solution.py:235
  76.6 0.1 collective-permute-start.14
  76.7 3.8 %products_3.1 = s16[200,1152]{1,0:T(8,128)(2,1)S(1)} custom-call(s32[2]{0:T(128)S(1)} %pad_add_fusion.place_ref, bf16[9216,512]{1,0:T(8,128)(2,1)S(1)} %copy-done, bf16[4608,512]{1,0:T(8,128)(2,1)} %collective-permute-done.r_ref, bf16[192,512]{1,0:T(8,128)(2,1)S(1)} %get-tuple-element.17.mine_ref, bf16[192,512]{1,0:T(8,128)(2,1)S(1)} %get-tuple-element.18.other_ref), custom_call_target="tpu_custom_call" | custom-call | flops 452984832 | bytes 2359296 | tf_op jit(solution)/shard_map/products_3/pallas_call | solution.py:235
  80.5 2.7 %collective-permute-start.15 = (s16[200,1152]{1,0:T(8,128)(2,1)S(1)}, s16[200,1152]{1,0:T(8,128)(2,1)S(1)}, u32[]{:S(2)}, u32[]{:S(2)}) collective-permute-start(s16[200,1152]{1,0:T(8,128)(2,1)S(1)} %products_3.1), channel_id=1, source_target_pairs={{0,6},{1,7},{2,0},{3,1},{4,2},{5,3},{6,4},{7,5},{8,14},{9,15},{10,... | collective-permute-start | bytes 1382408 | tf_op jit(solution)/shard_map/ppermute | solution.py:351
  83.2 0.0 collective-permute-done.19.other_ref
  83.2 18.6 %factor.1.inverse_ref = f32[192,192]{1,0:T(8,128)S(1)} custom-call(f32[128,128]{1,0:T(8,128)S(1)} %add_add_fusion.1.mine_ref, f32[128,128]{1,0:T(8,128)S(1)} %collective-permute-done.19.other_ref), custom_call_target="tpu_custom_call" | custom-call | flops 10000000000 | bytes 1048576 | tf_op jit(solution)/shard_map/factor/pallas_call | solution.py:166
  101.8 0.0 copy-start.1
  101.8 3.8 %products_0.1 = (f32[192,1152]{1,0:T(8,128)S(1)}, f32[8,1152]{1,0:T(8,128)S(1)}) custom-call(s32[2]{0:T(128)S(1)} %pad_add_fusion.place_ref, bf16[9216,512]{1,0:T(8,128)(2,1)S(1)} %copy-done, bf16[4608,512]{1,0:T(8,128)(2,1)} %collective-permute-done.r_ref, bf16[192,512]{1,0:T(8,128)(2,1)S(1)} %get-tuple-element.17.mine_ref, ...), custom_call_target="tpu_custom_call" | custom-call | flops 452984832 | bytes 2359296 | tf_op jit(solution)/shard_map/products_0/pallas_call | solution.py:235
  105.5 0.0 collective-permute-done.13.g1
  105.5 0.0 collective-permute-done.14.g2
  105.6 0.0 collective-permute-done.15.g3
  105.6 0.0 copy-done.1
  105.6 2.4 %finish.1 = (f32[192,1152]{1,0:T(8,128)}, f32[1152]{0:T(1024)}) custom-call(s32[3,64]{1,0:T(4,128)S(1)} %copy-done.2, f32[1152]{0:T(1024)S(1)} %copy-done.1, f32[192,1152]{1,0:T(8,128)S(1)} %get-tuple-element.19.own_ref, f32[8,1152]{1,0:T(8,128)S(1)} %get-tuple-element.20.norm_ref, s16[200,1152]{1,0:T(8,128)(2,1)S(1)} %collective-permute-done.13.g1, ...), custom_call_target="tpu_custom_call" | custom-call | flops 509607936 | bytes 4194304 | tf_op jit(solution)/shard_map/finish/pallas_call | solution.py:281
  (8 shorter events, 0.1 us)
Async XLA Ops:
  0.6 8.1 %copy-start.2 = (s32[3,64]{1,0:T(4,128)S(1)}, s32[3,64]{1,0:T(4,128)}, u32[]{:S(2)}) copy-start(s32[3,64]{1,0:T(4,128)} %picks_ref.3) | copy-start | bytes 2308
  5.5 58.7 %collective-permute-start = (bf16[4608,512]{1,0:T(8,128)(2,1)}, bf16[4608,512]{1,0:T(8,128)(2,1)}, u32[]{:S(2)}, u32[]{:S(2)}) collective-permute-start(bf16[4608,512]{1,0:T(8,128)(2,1)} %bitcast.3), channel_id=1, source_target_pairs={{0,1},{1,0},{2,3},{3,2},{4,5},{5,4},{6,7},{7,6},{8,9},{9,8},{10,11... | collective-permute-start | bytes 14155784 | tf_op jit(solution)/shard_map/swap_rows/ppermute | solution.py:326
  17.0 3.5 %collective-permute-start.3 = (bf16[48,512]{1,0:T(8,128)(2,1)S(1)}, bf16[48,512]{1,0:T(8,128)(2,1)S(1)}, u32[]{:S(2)}, u32[]{:S(2)}) collective-permute-start(bf16[48,512]{1,0:T(8,128)(2,1)S(1)} %get-tuple-element.16), channel_id=1, source_target_pairs={{0,24},{8,0},{16,8},{24,16},{32,56},{40,32},{48,40},{56,48},{64,88... | collective-permute-start | bytes 147464 | tf_op jit(solution)/shard_map/gather_picks/ppermute | solution.py:332
  18.1 4.5 %collective-permute-start.2 = (bf16[48,512]{1,0:T(8,128)(2,1)S(1)}, bf16[48,512]{1,0:T(8,128)(2,1)S(1)}, u32[]{:S(2)}, u32[]{:S(2)}) collective-permute-start(bf16[48,512]{1,0:T(8,128)(2,1)S(1)} %get-tuple-element.15), channel_id=1, source_target_pairs={{0,16},{8,24},{16,0},{24,8},{32,48},{40,56},{48,32},{56,40},{64,80... | collective-permute-start | bytes 147464 | tf_op jit(solution)/shard_map/gather_picks/ppermute | solution.py:332
  18.4 5.7 %collective-permute-start.1 = (bf16[48,512]{1,0:T(8,128)(2,1)S(1)}, bf16[48,512]{1,0:T(8,128)(2,1)S(1)}, u32[]{:S(2)}, u32[]{:S(2)}) collective-permute-start(bf16[48,512]{1,0:T(8,128)(2,1)S(1)} %get-tuple-element.14), channel_id=1, source_target_pairs={{0,8},{8,16},{16,24},{24,0},{32,40},{40,48},{48,56},{56,32},{64,72... | collective-permute-start | bytes 147464 | tf_op jit(solution)/shard_map/gather_picks/ppermute | solution.py:332
  24.2 1.6 %collective-permute-start.4 = (bf16[48,512]{1,0:T(8,128)(2,1)S(1)}, bf16[48,512]{1,0:T(8,128)(2,1)S(1)}, u32[]{:S(2)}, u32[]{:S(2)}) collective-permute-start(bf16[48,512]{1,0:T(8,128)(2,1)S(1)} %add_add_fusion.2), channel_id=1, source_target_pairs={{0,1},{1,0},{2,3},{3,2},{4,5},{5,4},{6,7},{7,6},{8,9},{9,8},{10,11... | collective-permute-start | bytes 147464 | tf_op jit(solution)/shard_map/gather_picks/ppermute | solution.py:333
  25.8 11.7 %collective-permute-start.7 = (bf16[96,512]{1,0:T(8,128)(2,1)S(1)}, bf16[96,512]{1,0:T(8,128)(2,1)S(1)}, u32[]{:S(2)}, u32[]{:S(2)}) collective-permute-start(bf16[96,512]{1,0:T(8,128)(2,1)S(1)} %pad_maximum_fusion), channel_id=1, source_target_pairs={{0,96},{1,161},{2,98},{3,163},{4,100},{5,165},{6,102},{7,167},{8,1... | collective-permute-start | bytes 294920 | tf_op jit(solution)/shard_map/gather_picks/ppermute | solution.py:334
  32.3 6.2 %collective-permute-start.5 = (bf16[96,512]{1,0:T(8,128)(2,1)S(1)}, bf16[96,512]{1,0:T(8,128)(2,1)S(1)}, u32[]{:S(2)}, u32[]{:S(2)}) collective-permute-start(bf16[96,512]{1,0:T(8,128)(2,1)S(1)} %pad_maximum_fusion), channel_id=1, source_target_pairs={{0,32},{1,225},{2,34},{3,227},{4,36},{5,229},{6,38},{7,231},{8,40}... | collective-permute-start | bytes 294920 | tf_op jit(solution)/shard_map/gather_picks/ppermute | solution.py:334
  33.0 7.7 %collective-permute-start.6 = (bf16[96,512]{1,0:T(8,128)(2,1)S(1)}, bf16[96,512]{1,0:T(8,128)(2,1)S(1)}, u32[]{:S(2)}, u32[]{:S(2)}) collective-permute-start(bf16[96,512]{1,0:T(8,128)(2,1)S(1)} %pad_maximum_fusion), channel_id=1, source_target_pairs={{0,64},{1,193},{2,66},{3,195},{4,68},{5,197},{6,70},{7,199},{8,72}... | collective-permute-start | bytes 294920 | tf_op jit(solution)/shard_map/gather_picks/ppermute | solution.py:334
  33.0 8.9 %collective-permute-start.8 = (bf16[48,512]{1,0:T(8,128)(2,1)S(1)}, bf16[48,512]{1,0:T(8,128)(2,1)S(1)}, u32[]{:S(2)}, u32[]{:S(2)}) collective-permute-start(bf16[48,512]{1,0:T(8,128)(2,1)S(1)} %add_add_fusion.2), channel_id=1, source_target_pairs={{0,128},{8,136},{16,144},{24,152},{32,160},{40,168},{48,176},{56,1... | collective-permute-start | bytes 147464 | tf_op jit(solution)/shard_map/gather_picks/ppermute | solution.py:335
  42.0 3.0 %collective-permute-start.9 = (bf16[96,512]{1,0:T(8,128)(2,1)S(1)}, bf16[96,512]{1,0:T(8,128)(2,1)S(1)}, u32[]{:S(2)}, u32[]{:S(2)}) collective-permute-start(bf16[96,512]{1,0:T(8,128)(2,1)S(1)} %pad_maximum_fusion.1), channel_id=1, source_target_pairs={{0,1},{1,0},{2,3},{3,2},{4,5},{5,4},{6,7},{7,6},{8,9},{9,8},{10,11... | collective-permute-start | bytes 294920 | tf_op jit(solution)/shard_map/gather_picks/ppermute | solution.py:338
  45.0 7.6 %collective-permute-start.10 = (bf16[96,512]{1,0:T(8,128)(2,1)S(1)}, bf16[96,512]{1,0:T(8,128)(2,1)S(1)}, u32[]{:S(2)}, u32[]{:S(2)}) collective-permute-start(bf16[96,512]{1,0:T(8,128)(2,1)S(1)} %maximum_add_fusion.s0), channel_id=1, source_target_pairs={{0,8},{8,16},{16,24},{24,0},{32,40},{40,48},{48,56},{56,32},{64,72... | collective-permute-start | bytes 294920 | tf_op jit(solution)/shard_map/gather_picks/ppermute | solution.py:340
  45.1 7.6 %collective-permute-start.11 = (bf16[96,512]{1,0:T(8,128)(2,1)S(1)}, bf16[96,512]{1,0:T(8,128)(2,1)S(1)}, u32[]{:S(2)}, u32[]{:S(2)}) collective-permute-start(bf16[96,512]{1,0:T(8,128)(2,1)S(1)} %maximum_add_fusion.s0), channel_id=1, source_target_pairs={{0,16},{8,24},{16,0},{24,8},{32,48},{40,56},{48,32},{56,40},{64,80... | collective-permute-start | bytes 294920 | tf_op jit(solution)/shard_map/gather_picks/ppermute | solution.py:340
  46.5 6.1 %collective-permute-start.12 = (bf16[96,512]{1,0:T(8,128)(2,1)S(1)}, bf16[96,512]{1,0:T(8,128)(2,1)S(1)}, u32[]{:S(2)}, u32[]{:S(2)}) collective-permute-start(bf16[96,512]{1,0:T(8,128)(2,1)S(1)} %maximum_add_fusion.s0), channel_id=1, source_target_pairs={{0,24},{8,0},{16,8},{24,16},{32,56},{40,32},{48,40},{56,48},{64,88... | collective-permute-start | bytes 294920 | tf_op jit(solution)/shard_map/gather_picks/ppermute | solution.py:340
  53.0 4.0 %collective-permute-start.18 = (f32[128,128]{1,0:T(8,128)S(1)}, f32[128,128]{1,0:T(8,128)S(1)}, u32[]{:S(2)}, u32[]{:S(2)}) collective-permute-start(f32[128,128]{1,0:T(8,128)S(1)} %get-tuple-element.21), channel_id=1, source_target_pairs={{0,6},{1,7},{2,0},{3,1},{4,2},{5,3},{6,4},{7,5},{8,14},{9,15},{10,... | collective-permute-start | bytes 196616 | tf_op jit(solution)/shard_map/sum_gram/ppermute | solution.py:344
  55.6 4.7 %collective-permute-start.17 = (f32[128,128]{1,0:T(8,128)S(1)}, f32[128,128]{1,0:T(8,128)S(1)}, u32[]{:S(2)}, u32[]{:S(2)}) collective-permute-start(f32[128,128]{1,0:T(8,128)S(1)} %get-tuple-element.21), channel_id=1, source_target_pairs={{0,4},{1,5},{2,6},{3,7},{4,0},{5,1},{6,2},{7,3},{8,12},{9,13},{10,... | collective-permute-start | bytes 196616 | tf_op jit(solution)/shard_map/sum_gram/ppermute | solution.py:344
  56.0 4.9 %collective-permute-start.16 = (f32[128,128]{1,0:T(8,128)S(1)}, f32[128,128]{1,0:T(8,128)S(1)}, u32[]{:S(2)}, u32[]{:S(2)}) collective-permute-start(f32[128,128]{1,0:T(8,128)S(1)} %get-tuple-element.21), channel_id=1, source_target_pairs={{0,2},{1,3},{2,4},{3,5},{4,6},{5,7},{6,0},{7,1},{8,10},{9,11},{10,... | collective-permute-start | bytes 196616 | tf_op jit(solution)/shard_map/sum_gram/ppermute | solution.py:344
  61.0 22.2 %collective-permute-start.19 = (f32[128,128]{1,0:T(8,128)S(1)}, f32[128,128]{1,0:T(8,128)S(1)}, u32[]{:S(2)}, u32[]{:S(2)}) collective-permute-start(f32[128,128]{1,0:T(8,128)S(1)} %add_add_fusion.1.mine_ref), channel_id=1, source_target_pairs={{0,1},{1,0},{2,3},{3,2},{4,5},{5,4},{6,7},{7,6},{8,9},{9,8},{10,11... | collective-permute-start | bytes 196616 | tf_op jit(solution)/shard_map/sum_gram/ppermute | solution.py:346
  64.1 3.7 %copy-start = (bf16[9216,512]{1,0:T(8,128)(2,1)S(1)}, bf16[9216,512]{1,0:T(8,128)(2,1)}, u32[]{:S(2)}) copy-start(bf16[9216,512]{1,0:T(8,128)(2,1)} %e_ref.9) | copy-start | bytes 28311556
  71.6 33.9 %collective-permute-start.13 = (s16[200,1152]{1,0:T(8,128)(2,1)S(1)}, s16[200,1152]{1,0:T(8,128)(2,1)S(1)}, u32[]{:S(2)}, u32[]{:S(2)}) collective-permute-start(s16[200,1152]{1,0:T(8,128)(2,1)S(1)} %products_2.1), channel_id=1, source_target_pairs={{0,4},{1,5},{2,6},{3,7},{4,0},{5,1},{6,2},{7,3},{8,12},{9,13},{10,... | collective-permute-start | bytes 1382408 | tf_op jit(solution)/shard_map/ppermute | solution.py:351
  76.6 29.0 %collective-permute-start.14 = (s16[200,1152]{1,0:T(8,128)(2,1)S(1)}, s16[200,1152]{1,0:T(8,128)(2,1)S(1)}, u32[]{:S(2)}, u32[]{:S(2)}) collective-permute-start(s16[200,1152]{1,0:T(8,128)(2,1)S(1)} %products_1.1), channel_id=1, source_target_pairs={{0,2},{1,3},{2,4},{3,5},{4,6},{5,7},{6,0},{7,1},{8,10},{9,11},{10,... | collective-permute-start | bytes 1382408 | tf_op jit(solution)/shard_map/ppermute | solution.py:351
  80.5 25.1 %collective-permute-start.15 = (s16[200,1152]{1,0:T(8,128)(2,1)S(1)}, s16[200,1152]{1,0:T(8,128)(2,1)S(1)}, u32[]{:S(2)}, u32[]{:S(2)}) collective-permute-start(s16[200,1152]{1,0:T(8,128)(2,1)S(1)} %products_3.1), channel_id=1, source_target_pairs={{0,6},{1,7},{2,0},{3,1},{4,2},{5,3},{6,4},{7,5},{8,14},{9,15},{10,... | collective-permute-start | bytes 1382408 | tf_op jit(solution)/shard_map/ppermute | solution.py:351
  101.8 3.8 %copy-start.1 = (f32[1152]{0:T(1024)S(1)}, f32[1152]{0:T(1024)}, u32[]{:S(2)}) copy-start(f32[1152]{0:T(1024)} %quality_ref.1) | copy-start | bytes 13828

commit v2 on v0

v2 whole, which is shorter than its diff:
```python
import functools

import jax
import jax.numpy as jnp
from jax import lax
from jax.experimental import pallas as pl
from jax.experimental.pallas import tpu as pltpu
from jax.sharding import PartitionSpec as P

ridge_term = 0.5
pack = 1152
Y, Z, X = 4, 8, 4
HIGHEST = lax.Precision.HIGHEST
NT = (((1,), (1,)), ((), ()))
TN = (((0,), (0,)), ((), ()))
f32, bf16, i32, i16 = jnp.float32, jnp.bfloat16, jnp.int32, jnp.int16
VMEM = pl.BlockSpec(memory_space=pltpu.VMEM)
ANY = pl.BlockSpec(memory_space=pl.ANY)
levels = 32767.0


def params(mib):
    return pltpu.CompilerParams(vmem_limit_bytes=mib << 20)


def cost(flops, nbytes):
    return pl.CostEstimate(flops=int(flops), bytes_accessed=int(nbytes), transcendentals=0)


def shape(dims, dtype):
    return jax.ShapeDtypeStruct(dims, dtype)


def as_column(row):
    n = row.shape[1]
    eye = lax.broadcasted_iota(i32, (n, n), 0) == lax.broadcasted_iota(i32, (n, n), 1)
    wide = jnp.broadcast_to(row.astype(f32), (n, n))
    return jnp.sum(jnp.where(eye, wide, 0.0), axis=1, keepdims=True).astype(i32)


def pick_kernel(picks_ref, e_ref, *rest):
    outs, (list_ref, tiles_ref, rows_ref, arrived) = rest[:Y], rest[Y:]
    rounds, count = picks_ref.shape
    total = rounds * count
    height = tiles_ref.shape[1]
    rows_here = e_ref.shape[0]
    row_start = lax.axis_index("rows") * rows_here
    held = jnp.int32(0)
    for p in range(total):
        local = picks_ref[p // count, p % count] - row_start
        list_ref[held] = local * 256 + p
        held = held + jnp.where((local >= 0) & (local < rows_here), 1, 0)

    def fetch(i):
        tile = pl.multiple_of(lax.div(list_ref[i], 256 * height) * height, height)
        return pltpu.make_async_copy(e_ref.at[pl.ds(tile, height), :], tiles_ref.at[i], arrived.at[i])

    def begin(i, carry):
        fetch(i).start()
        return carry

    def end(i, carry):
        fetch(i).wait()
        sub = lax.broadcasted_iota(i32, tiles_ref.shape[1:], 0)
        place, p = lax.div(list_ref[i], 256), lax.rem(list_ref[i], 256)
        one = jnp.where(sub == lax.rem(place, height), tiles_ref[i].astype(f32), 0.0)
        rows_ref[pl.ds(p, 1), :] = jnp.sum(one, axis=0, keepdims=True)
        return carry

    lax.fori_loop(0, held, begin, 0)
    rows_ref[...] = jnp.zeros_like(rows_ref)
    lax.fori_loop(0, held, end, 0)
    y = lax.rem(lax.axis_index("rows"), Y)
    group = total // Y
    for j in range(Y):
        g = lax.rem(y + j, Y)
        outs[j][...] = rows_ref[pl.ds(pl.multiple_of(g * group, 16), group), :].astype(bf16)


def local_picks(picks, embeddings):
    dims = embeddings.shape[1]
    total = picks.size
    return pl.pallas_call(
        pick_kernel,
        in_specs=[pl.BlockSpec(memory_space=pltpu.SMEM), ANY],
        out_specs=[VMEM] * Y,
        out_shape=[shape((total // Y, dims), bf16)] * Y,
        scratch_shapes=[
            pltpu.SMEM((256,), i32),
            pltpu.VMEM((total, 16, dims), bf16),
            pltpu.VMEM((total, dims), f32),
            pltpu.SemaphoreType.DMA((total,)),
        ],
        compiler_params=params(50),
        cost_estimate=cost(0, 10 << 20),
        name="local_picks",
    )(picks, embeddings)


def stage_kernel(hop, e_ref, r_ref, through_ref, mine_ref, other_ref, norm_ref, passed_ref, arrived):
    d = lax.axis_index("dim")
    chip, core = lax.div(d, 2), lax.rem(d, 2)
    first = (lax.rem(chip + hop, X) * 2 + core) * pack
    tile = pack // 3
    copies = []
    for i in range(3):
        there, here = pl.ds(pl.multiple_of(first + i * tile, 128), tile), pl.ds(i * tile, tile)
        copies.append(
            (
                pltpu.make_async_copy(e_ref.at[there, :], mine_ref.at[here, :], arrived.at[2 * i]),
                pltpu.make_async_copy(r_ref.at[there, :], other_ref.at[here, :], arrived.at[2 * i + 1]),
            )
        )
    for pair in copies:
        for copy in pair:
            copy.start()
    passed_ref[...] = through_ref[...]
    for i in range(3):
        for copy in copies[i]:
            copy.wait()
        squares = jnp.zeros((tile, 128), f32)
        for ref in (mine_ref, other_ref):
            for j in range(0, ref.shape[1], 128):
                part = ref[i * tile : (i + 1) * tile, j : j + 128].astype(f32)
                squares += part * part
        high = squares.astype(bf16)
        low = (squares - high.astype(f32)).astype(bf16)
        ones = jnp.ones((8, 128), bf16)
        norm = lax.dot_general(ones, high, NT, preferred_element_type=f32)
        norm_ref[:, i * tile : (i + 1) * tile] = norm + lax.dot_general(ones, low, NT, preferred_element_type=f32)


def stage(hop, embeddings, received, through):
    dims = embeddings.shape[1]
    return pl.pallas_call(
        functools.partial(stage_kernel, hop),
        in_specs=[ANY, ANY, VMEM],
        out_specs=[VMEM] * 4,
        out_shape=[
            shape((pack, dims), bf16),
            shape((pack, dims), bf16),
            shape((8, pack), f32),
            shape(through.shape, through.dtype),
        ],
        scratch_shapes=[pltpu.SemaphoreType.DMA((6,))],
        compiler_params=params(52),
        cost_estimate=cost(0, 4 * pack * dims),
        name="stage_%d" % hop,
    )(embeddings, received, through)


def order_kernel(s0, s1, s2, s3, out_ref):
    y = lax.rem(lax.axis_index("rows"), Y)
    group = s0.shape[0]
    for j, ref in enumerate((s0, s1, s2, s3)):
        g = pl.multiple_of(lax.rem(y + (Y - j), Y) * group, 16)
        out_ref[pl.ds(g, group), :] = ref[...]


def in_order(groups):
    group, dims = groups[0].shape
    return pl.pallas_call(
        order_kernel,
        in_specs=[VMEM] * Y,
        out_specs=VMEM,
        out_shape=shape((group * Y, dims), bf16),
        compiler_params=params(16),
        cost_estimate=cost(0, 4 * Y * group * dims),
        name="order",
    )(*groups)


def gram_kernel(mine_ref, other_ref, full_ref, half_ref, keep_ref):
    mine, other = mine_ref[...], other_ref[...]
    gram = lax.dot_general(mine, mine, NT, preferred_element_type=f32)
    gram += lax.dot_general(other, other, NT, preferred_element_type=f32)
    core = lax.rem(lax.axis_index("dim"), 2)
    top = gram[:128, :128]
    corner = jnp.concatenate([gram[128:, 128:], jnp.zeros((64, 64), f32)], axis=1)
    low = jnp.concatenate([gram[128:, :128], corner], axis=0)
    a, b = jnp.where(core == 0, top, low), jnp.where(core == 0, low, top)
    half_ref[...] = a
    full_ref[:128, :], full_ref[128:, :] = a, b
    keep_ref[:128, :], keep_ref[128:, :] = jnp.where(core == 0, a, 0.0), jnp.where(core == 0, b, 0.0)


def picks_gram(mine, other):
    total, dims = mine.shape
    return pl.pallas_call(
        gram_kernel,
        in_specs=[VMEM] * 2,
        out_specs=[VMEM] * 3,
        out_shape=[shape((256, 128), f32), shape((128, 128), f32), shape((256, 128), f32)],
        compiler_params=params(16),
        cost_estimate=cost(4 * total * total * dims, 4 * total * dims),
        name="gram",
    )(mine, other)


panel, together = 64, 8


def factor_kernel(sum_ref, swapped_ref, inverse_ref, m_ref):
    n = inverse_ref.shape[0]
    core = lax.rem(lax.axis_index("dim"), 2)
    a = sum_ref[:128, :] + swapped_ref[128:, :]
    b = sum_ref[128:, :] + swapped_ref[:128, :]
    first, last = jnp.where(core == 0, a, b), jnp.where(core == 0, b, a)
    width = m_ref.shape[1]
    sub = lax.broadcasted_iota(i32, (n, width - 128), 0)
    lane = lax.broadcasted_iota(i32, (n, width - 128), 1) + 128
    m_ref[:, 128:] = jnp.where(lane - n == sub, 1.0, 0.0)
    diag = lax.broadcasted_iota(i32, (128, 128), 0) == lax.broadcasted_iota(i32, (128, 128), 1)
    ridge = jnp.where(diag, ridge_term, 0.0)
    m_ref[:128, :128] = first + ridge
    m_ref[128:, :128] = last[:64, :]
    m_ref[128:, 128:n] = last[64:, :64] + ridge[:64, :64]
    m_ref[:128, 128:n] = last[:64, :].T
    below = lax.broadcasted_iota(i32, (panel, 128), 0)
    at = lax.broadcasted_iota(i32, (panel, 128), 1) - below
    for low in range(0, n, panel):
        left = low // 128 * 128
        off = low - left
        tiles = [m_ref[low : low + panel, j : j + 128] for j in range(left, width, 128)]
        for g in range(0, panel, together):
            cols = [
                jnp.broadcast_to(tiles[0][:, off + g + i : off + g + i + 1], (panel, 128)) for i in range(together)
            ]
            heads = [[t[g + i : g + i + 1, :] for t in tiles] for i in range(together)]
            for i in range(together):
                factors = jnp.where(below > g + i, cols[i] * (1.0 / cols[i][g + i : g + i + 1, :]), 0.0)
                for j in range(i + 1, together):
                    cols[j] = cols[j] - factors * cols[j][g + i : g + i + 1, :]
                    by = factors[g + j : g + j + 1, :]
                    heads[j] = [x - by * y for x, y in zip(heads[j], heads[i])]
                tiles = [t - factors * y for t, y in zip(tiles, heads[i])]
        pivots = jnp.sum(jnp.where(at == off, tiles[0], 0.0), axis=1, keepdims=True)
        rows = jnp.concatenate(tiles, axis=1) * (1.0 / jnp.sqrt(pivots))
        inverse_ref[low : low + panel, :] = rows[:, n - left :]
        if low + panel < n:
            update = lax.dot_general(rows[:, : n - left], rows, TN, precision=HIGHEST, preferred_element_type=f32)
            m_ref[low + panel :, left:] -= update[low + panel - left :, :]


def factor_inverse(total, swapped, n):
    return pl.pallas_call(
        factor_kernel,
        in_specs=[VMEM] * 2,
        out_specs=VMEM,
        out_shape=shape((n, n), f32),
        scratch_shapes=[pltpu.VMEM((n, 2 * n), f32)],
        compiler_params=params(16),
        cost_estimate=cost(1e6, 1 << 16),
        name="factor",
    )(total, swapped)


def split(value):
    scaled = value * 16.0
    high = jnp.floor(scaled)
    return high, jnp.floor((scaled - high) * 32768.0)


def join(high, low):
    return (high + low * (1.0 / 32768.0)) * (1.0 / 16.0)


def block_products(at, e_ref, r_ref, mine_ref, other_ref):
    part = lax.dot_general(mine_ref[...], e_ref[at, :], NT, preferred_element_type=f32)
    return part + lax.dot_general(other_ref[...], r_ref[at, :], NT, preferred_element_type=f32)


def send_kernel(e_ref, r_ref, norm_ref, mine_ref, other_ref, through_ref, out_ref, passed_ref):
    tile = pack // 3
    passed_ref[...] = through_ref[...]
    for low in range(0, pack, tile):
        at = pl.ds(low, tile)
        part = block_products(at, e_ref, r_ref, mine_ref, other_ref)
        norm_high, norm_low = split(norm_ref[:1, at])
        top_high, top_low = split(jnp.max(jnp.abs(part), axis=0, keepdims=True))
        scale = join(top_high, top_low + 1.0)
        coded = jnp.floor(part * (levels / scale) + 0.5)
        row = lax.broadcasted_iota(i32, (8, tile), 0)
        extra = jnp.where(row == 0, norm_high, jnp.where(row == 1, norm_low, jnp.where(row == 2, top_high, top_low)))
        out_ref[:, at] = jnp.concatenate([coded, extra], axis=0).astype(i32).astype(i16)


def keep_kernel(e_ref, r_ref, mine_ref, other_ref, out_ref):
    tile = pack // 3
    for low in range(0, pack, tile):
        out_ref[:, low : low + tile] = block_products(pl.ds(low, tile), e_ref, r_ref, mine_ref, other_ref)


def products(hop, staged, mine, other, through=None):
    total, dims = mine.shape
    if hop:
        operands = (*staged, mine, other, through)
        out_shape = [shape((total + 8, pack), i16), shape(through.shape, through.dtype)]
    else:
        operands = (*staged[:2], mine, other)
        out_shape = [shape((total, pack), f32)]
    return pl.pallas_call(
        send_kernel if hop else keep_kernel,
        in_specs=[VMEM] * len(operands),
        out_specs=[VMEM] * len(out_shape),
        out_shape=out_shape,
        compiler_params=params(16),
        cost_estimate=cost(1e6, 1 << 16),
        name="products_%d" % hop,
    )(*operands)


def finish_kernel(picks_ref, quality_ref, own_ref, norm_ref, g1, g2, g3, inverse_ref, out_ref, resid_ref, stage_ref, sent):
    total, width = own_ref.shape
    rounds, count = picks_ref.shape
    first_row = (lax.axis_index("rows") * (2 * X) + lax.axis_index("dim")) * width
    chosen = jnp.concatenate([as_column(picks_ref[r : r + 1, :]) for r in range(rounds)], axis=0) - first_row
    inverse = inverse_ref[...]
    tile = width // 3
    copies = []
    for i in range(3):
        here = pl.ds(i * tile, tile)
        values, norm = own_ref[:, here], norm_ref[:1, here]
        for ref in (g1, g2, g3):
            got = ref[:, here].astype(i32).astype(f32)
            scale = join(got[total + 2 : total + 3], got[total + 3 : total + 4] + 1.0)
            values = values + got[:total] * (scale * (1.0 / levels))
            norm = norm + join(got[total : total + 1], got[total + 1 : total + 2] + 0.5)
        lane = lax.broadcasted_iota(i32, (total, tile), 1) + i * tile
        values = jnp.where(chosen == lane, values + ridge_term, values)
        columns = jnp.dot(inverse, values, precision=HIGHEST, preferred_element_type=f32)
        score = quality_ref[here].reshape(1, tile)
        stage_ref[:, here] = columns * score
        copies.append(pltpu.make_async_copy(stage_ref.at[:, here], out_ref.at[:, here], sent.at[i]))
        copies[-1].start()
        left = norm + ridge_term - jnp.sum(columns * columns, axis=0, keepdims=True)
        resid_ref[here] = (score * score * left).reshape(tile)
    for copy in copies:
        copy.wait()


def finish(picks, quality, own, norm, got, inverse):
    total, width = own.shape
    return pl.pallas_call(
        finish_kernel,
        in_specs=[VMEM] * 8,
        out_specs=[ANY, VMEM],
        out_shape=[shape((total, width), f32), shape((width,), f32)],
        scratch_shapes=[pltpu.VMEM((total, width), f32), pltpu.SemaphoreType.DMA((3,))],
        compiler_params=params(16),
        cost_estimate=cost(12 * total * total * width, 4 << 20),
        name="finish",
    )(picks, quality, own, norm, *got, inverse)


def along_y(k):
    return [(r, r // Y * Y + (r % Y + k) % Y) for r in range(Y * Z)]


def along_z(partner):
    return [(r, partner(r // Y) * Y + r % Y) for r in range(Y * Z)]


def along_x(k):
    return [(d, (d // 2 + k) % X * 2 + d % 2) for d in range(2 * X)]


swap = [(d, d ^ 1) for d in range(2 * X)]
both_ways = [(d, (d // 2 + (1 if d % 2 == 0 else -1)) % X * 2 + d % 2) for d in range(2 * X)]


def per_device(embeddings, quality, picked_rows):
    total = picked_rows.size
    with jax.named_scope("swap_rows"):
        received = lax.ppermute(embeddings, "dim", swap)

    with jax.named_scope("gather_picks"):
        parts = local_picks(picked_rows, embeddings)
        mine = parts[0]
        for k in range(1, Y):
            mine = mine + lax.ppermute(parts[k], "rows", along_y(k))
        staged = {}
        mine = mine + lax.ppermute(mine, "rows", along_z(lambda z: z ^ 1))
        arrived = lax.ppermute(mine, "rows", along_z(lambda z: z ^ 2))
        *staged[2], mine = stage(2, embeddings, received, mine)
        mine = mine + arrived
        arrived = lax.ppermute(mine, "rows", along_z(lambda z: Z - 1 - z))
        *staged[1], mine = stage(1, embeddings, received, mine)
        mine = mine + arrived
        groups = [mine] + [lax.ppermute(mine, "rows", along_y(k)) for k in range(1, Y)]
        *staged[3], mine = stage(3, embeddings, received, mine)
        *staged[0], mine = stage(0, embeddings, received, mine)
        groups[0] = mine
        pick_mine = in_order(groups)
        pick_other = lax.ppermute(pick_mine, "dim", swap)

    full, half, keep = picks_gram(pick_mine, pick_other)
    got = {}
    with jax.named_scope("sum_gram"):
        near = lax.ppermute(full, "dim", both_ways)
        far = lax.ppermute(half, "dim", along_x(2))
        for hop in (2, 1):
            coded, keep = products(hop, staged[hop], pick_mine, pick_other, keep)
            got[hop] = lax.ppermute(coded, "dim", along_x(hop))
        gram = jnp.concatenate([keep[:128] + near[:128] + far, keep[128:] + near[128:]], axis=0)
        gram_other = lax.ppermute(gram, "dim", swap)
        coded, gram = products(3, staged[3], pick_mine, pick_other, gram)
        got[3] = lax.ppermute(coded, "dim", along_x(3))
    inverse = factor_inverse(gram, gram_other, total)
    own = products(0, staged[0], pick_mine, pick_other)[0]
    columns, residual = finish(picked_rows, quality, own, staged[0][2], [got[k] for k in (2, 1, 3)], inverse)
    return columns.T, residual


def solution(mesh):
    return jax.shard_map(
        per_device,
        mesh=mesh,
        in_specs=(P("rows", "dim"), P(("rows", "dim")), P()),
        out_specs=(P(("rows", "dim"), None), P(("rows", "dim"))),
        check_vma=False,
    )
```

time: 483 us -> 78.9 us (0.16)
  the two profiles are of different devices: /device:TPU:1 before, /device:TPU:11 now
where the time goes in v2:
time: 78.9 us; the launch traced here: 78.2 us
  starting transfers between devices  31.3 us (40%)
  Pallas kernels  29.7 us (38%)
  waiting for transfers between devices  15.3 us (19%)
  between operations  1 us (1%)
  local copies, waits for them, and re-layouts  0.93 us (1%)
    pallas_call x4, Pallas kernels, stage(): pl.pallas_call(functools.partial(stage_kernel, hop), in_specs=[ANY, ANY,...  12.2 us
    ppermute x1, waiting for transfers between devices, per_device(): got[3] = lax.ppermute(coded, 'dim', along_x(3))  10.1 us
    pallas_call x1, Pallas kernels, factor_inverse(): pl.pallas_call(factor_kernel, in_specs=[VMEM] * 2, out_specs=VMEM, out_sh...  6.56 us
    ppermute x3, starting transfers between devices, per_device(): lax.ppermute(mine, 'rows', along_y(k))  4.78 us
    ppermute x1, starting transfers between devices, per_device(): pick_other = lax.ppermute(pick_mine, 'dim', swap)  4.76 us
    ppermute x3, starting transfers between devices, per_device(): mine = mine + lax.ppermute(parts[k], 'rows', along_y(k))  4.08 us
    pallas_call x4, Pallas kernels, products(): pl.pallas_call(send_kernel if hop else keep_kernel, in_specs=[VMEM] * len...  3.99 us
    pallas_call x1, Pallas kernels, local_picks(): pl.pallas_call(pick_kernel, in_specs=[pl.BlockSpec(memory_space=pltpu.SME...  3.8 us
  transfers between devices with their start and end apart: 17, of which 6 were waited for; matrix products, arithmetic and copies ran while one was open for 0% of the time, Pallas kernels for 34%

profile of v2, /device:TPU:11, one launch (start us, length us, event | category | flops | bytes accessed | tf_op | source)
XLA Modules:
  0.0 78.2 jit_solution(11414009481891288618)
XLA Ops:
  0.6 0.8 collective-permute-start
  1.4 0.0 copy-start.5
  1.4 0.7 copy-done.5
  2.1 3.8 %local_picks.1 = (bf16[48,512]{1,0:T(8,128)(2,1)S(1)}, bf16[48,512]{1,0:T(8,128)(2,1)S(1)}, bf16[48,512]{1,0:T(8,128)(2,1)S(1)}, bf16[48,512]{1,0:T(8,128)(2,1)S(1)}) custom-call(s32[3,64]{1,0:T(4,128)S(1)} %copy-done.5, bf16[9216,512]{1,0:T(8,128)(2,1)} %e_ref.9), custom_call_target="tpu_custom_call" | custom-call | bytes 10485760 | tf_op jit(solution)/shard_map/gather_picks/local_picks/pallas_call | solution.py:83
  5.9 1.3 %collective-permute-start.1 = (bf16[48,512]{1,0:T(8,128)(2,1)S(1)}, bf16[48,512]{1,0:T(8,128)(2,1)S(1)}, u32[]{:S(2)}, u32[]{:S(2)}) collective-permute-start(bf16[48,512]{1,0:T(8,128)(2,1)S(1)} %get-tuple-element.34), channel_id=1, source_target_pairs={{0,8},{8,16},{16,24},{24,0},{32,40},{40,48},{48,56},{56,32},{64,72... | collective-permute-start | bytes 147464 | tf_op jit(solution)/shard_map/gather_picks/ppermute | solution.py:381
  7.1 0.9 %collective-permute-start.2 = (bf16[48,512]{1,0:T(8,128)(2,1)S(1)}, bf16[48,512]{1,0:T(8,128)(2,1)S(1)}, u32[]{:S(2)}, u32[]{:S(2)}) collective-permute-start(bf16[48,512]{1,0:T(8,128)(2,1)S(1)} %get-tuple-element.35), channel_id=1, source_target_pairs={{0,16},{8,24},{16,0},{24,8},{32,48},{40,56},{48,32},{56,40},{64,80... | collective-permute-start | bytes 147464 | tf_op jit(solution)/shard_map/gather_picks/ppermute | solution.py:381
  8.0 2.0 %collective-permute-start.3 = (bf16[48,512]{1,0:T(8,128)(2,1)S(1)}, bf16[48,512]{1,0:T(8,128)(2,1)S(1)}, u32[]{:S(2)}, u32[]{:S(2)}) collective-permute-start(bf16[48,512]{1,0:T(8,128)(2,1)S(1)} %get-tuple-element.36), channel_id=1, source_target_pairs={{0,24},{8,0},{16,8},{24,16},{32,56},{40,32},{48,40},{56,48},{64,88... | collective-permute-start | bytes 147464 | tf_op jit(solution)/shard_map/gather_picks/ppermute | solution.py:381
  10.0 0.0 collective-permute-done.1
  10.0 1.6 %collective-permute-done.2 = bf16[48,512]{1,0:T(8,128)(2,1)S(1)} collective-permute-done((bf16[48,512]{1,0:T(8,128)(2,1)S(1)}, bf16[48,512]{1,0:T(8,128)(2,1)S(1)}, u32[]{:S(2)}, u32[]{:S(2)}) %collective-permute-start.2) | collective-permute-done | bytes 49184 | tf_op jit(solution)/shard_map/gather_picks/ppermute | solution.py:381
  11.6 0.0 collective-permute-done.3
  11.6 1.8 %collective-permute-start.4 = (bf16[48,512]{1,0:T(8,128)(2,1)S(1)}, bf16[48,512]{1,0:T(8,128)(2,1)S(1)}, u32[]{:S(2)}, u32[]{:S(2)}) collective-permute-start(bf16[48,512]{1,0:T(8,128)(2,1)S(1)} %add_add_fusion), channel_id=1, source_target_pairs={{0,32},{8,40},{16,48},{24,56},{32,0},{40,8},{48,16},{56,24},{64,96... | collective-permute-start | bytes 147464 | tf_op jit(solution)/shard_map/gather_picks/ppermute | solution.py:383
  13.4 1.5 %collective-permute-done.4 = bf16[48,512]{1,0:T(8,128)(2,1)S(1)} collective-permute-done((bf16[48,512]{1,0:T(8,128)(2,1)S(1)}, bf16[48,512]{1,0:T(8,128)(2,1)S(1)}, u32[]{:S(2)}, u32[]{:S(2)}) %collective-permute-start.4) | collective-permute-done | bytes 49184 | tf_op jit(solution)/shard_map/gather_picks/ppermute | solution.py:383
  14.9 3.1 %collective-permute-start.5 = (bf16[48,512]{1,0:T(8,128)(2,1)S(1)}, bf16[48,512]{1,0:T(8,128)(2,1)S(1)}, u32[]{:S(2)}, u32[]{:S(2)}) collective-permute-start(bf16[48,512]{1,0:T(8,128)(2,1)S(1)} %add.30.through_ref), channel_id=1, source_target_pairs={{0,64},{8,72},{16,80},{24,88},{32,96},{40,104},{48,112},{56,120},{... | collective-permute-start | bytes 147464 | tf_op jit(solution)/shard_map/gather_picks/ppermute | solution.py:384
  18.1 0.0 collective-permute-done.r_ref
  18.1 3.0 %stage_2.1 = (bf16[1152,512]{1,0:T(8,128)(2,1)S(1)}, bf16[1152,512]{1,0:T(8,128)(2,1)}, f32[8,1152]{1,0:T(8,128)S(1)}, bf16[48,512]{1,0:T(8,128)(2,1)S(1)}) custom-call(bf16[9216,512]{1,0:T(8,128)(2,1)} %e_ref.9, bf16[9216,512]{1,0:T(8,128)(2,1)} %collective-permute-done.r_ref, bf16[48,512]{1,0:T(8,128)(2,1)S(1)} %add.30.through_ref), custom_call_target="tpu_custom_call" | custom-call | bytes 2359296 | tf_op jit(solution)/shard_map/gather_picks/stage_2/pallas_call | solution.py:135
  21.1 0.0 collective-permute-done.5
  21.1 3.7 %collective-permute-start.6 = (bf16[48,512]{1,0:T(8,128)(2,1)S(1)}, bf16[48,512]{1,0:T(8,128)(2,1)S(1)}, u32[]{:S(2)}, u32[]{:S(2)}) collective-permute-start(bf16[48,512]{1,0:T(8,128)(2,1)S(1)} %add.31.through_ref), channel_id=1, source_target_pairs={{0,224},{8,232},{16,240},{24,248},{32,192},{40,200},{48,208},{56,2... | collective-permute-start | bytes 147464 | tf_op jit(solution)/shard_map/gather_picks/ppermute | solution.py:387
  24.8 3.0 %stage_1.1 = (bf16[1152,512]{1,0:T(8,128)(2,1)S(1)}, bf16[1152,512]{1,0:T(8,128)(2,1)}, f32[8,1152]{1,0:T(8,128)S(1)}, bf16[48,512]{1,0:T(8,128)(2,1)S(1)}) custom-call(bf16[9216,512]{1,0:T(8,128)(2,1)} %e_ref.9, bf16[9216,512]{1,0:T(8,128)(2,1)} %collective-permute-done.r_ref, bf16[48,512]{1,0:T(8,128)(2,1)S(1)} %add.31.through_ref), custom_call_target="tpu_custom_call" | custom-call | bytes 2359296 | tf_op jit(solution)/shard_map/gather_picks/stage_1/pallas_call | solution.py:135
  27.8 0.0 collective-permute-done.6
  27.8 1.5 %collective-permute-start.7 = (bf16[48,512]{1,0:T(8,128)(2,1)S(1)}, bf16[48,512]{1,0:T(8,128)(2,1)S(1)}, u32[]{:S(2)}, u32[]{:S(2)}) collective-permute-start(bf16[48,512]{1,0:T(8,128)(2,1)S(1)} %add.32.through_ref), channel_id=1, source_target_pairs={{0,8},{8,16},{16,24},{24,0},{32,40},{40,48},{48,56},{56,32},{64,72... | collective-permute-start | bytes 147464 | tf_op jit(solution)/shard_map/gather_picks/ppermute | solution.py:390
  29.3 1.8 %collective-permute-start.8 = (bf16[48,512]{1,0:T(8,128)(2,1)S(1)}, bf16[48,512]{1,0:T(8,128)(2,1)S(1)}, u32[]{:S(2)}, u32[]{:S(2)}) collective-permute-start(bf16[48,512]{1,0:T(8,128)(2,1)S(1)} %add.32.through_ref), channel_id=1, source_target_pairs={{0,16},{8,24},{16,0},{24,8},{32,48},{40,56},{48,32},{56,40},{64,80... | collective-permute-start | bytes 147464 | tf_op jit(solution)/shard_map/gather_picks/ppermute | solution.py:390
  31.1 1.5 %collective-permute-start.9 = (bf16[48,512]{1,0:T(8,128)(2,1)S(1)}, bf16[48,512]{1,0:T(8,128)(2,1)S(1)}, u32[]{:S(2)}, u32[]{:S(2)}) collective-permute-start(bf16[48,512]{1,0:T(8,128)(2,1)S(1)} %add.32.through_ref), channel_id=1, source_target_pairs={{0,24},{8,0},{16,8},{24,16},{32,56},{40,32},{48,40},{56,48},{64,88... | collective-permute-start | bytes 147464 | tf_op jit(solution)/shard_map/gather_picks/ppermute | solution.py:390
  32.6 3.1 %stage_3.1 = (bf16[1152,512]{1,0:T(8,128)(2,1)S(1)}, bf16[1152,512]{1,0:T(8,128)(2,1)}, f32[8,1152]{1,0:T(8,128)S(1)}, bf16[48,512]{1,0:T(8,128)(2,1)S(1)}) custom-call(bf16[9216,512]{1,0:T(8,128)(2,1)} %e_ref.9, bf16[9216,512]{1,0:T(8,128)(2,1)} %collective-permute-done.r_ref, bf16[48,512]{1,0:T(8,128)(2,1)S(1)} %add.32.through_ref), custom_call_target="tpu_custom_call" | custom-call | bytes 2359296 | tf_op jit(solution)/shard_map/gather_picks/stage_3/pallas_call | solution.py:135
  35.7 0.0 copy-start.2
  35.7 3.1 %stage_0.1 = (bf16[1152,512]{1,0:T(8,128)(2,1)S(1)}, bf16[1152,512]{1,0:T(8,128)(2,1)}, f32[8,1152]{1,0:T(8,128)S(1)}, bf16[48,512]{1,0:T(8,128)(2,1)S(1)}) custom-call(bf16[9216,512]{1,0:T(8,128)(2,1)} %e_ref.9, bf16[9216,512]{1,0:T(8,128)(2,1)} %collective-permute-done.r_ref, bf16[48,512]{1,0:T(8,128)(2,1)S(1)} %get-tuple-element.39.through_ref), custom_call_target="tpu_custom_call" | custom-call | bytes 2359296 | tf_op jit(solution)/shard_map/gather_picks/stage_0/pallas_call | solution.py:135
  38.8 0.0 collective-permute-done.7.s1
  38.8 0.0 collective-permute-done.8.s2
  38.8 0.0 collective-permute-done.9.s3
  38.9 4.8 %collective-permute-start.10 = (bf16[192,512]{1,0:T(8,128)(2,1)S(1)}, bf16[192,512]{1,0:T(8,128)(2,1)S(1)}, u32[]{:S(2)}, u32[]{:S(2)}) collective-permute-start(bf16[192,512]{1,0:T(8,128)(2,1)S(1)} %order.1.mine_ref), channel_id=1, source_target_pairs={{0,1},{1,0},{2,3},{3,2},{4,5},{5,4},{6,7},{7,6},{8,9},{9,8},{10,11... | collective-permute-start | bytes 589832 | tf_op jit(solution)/shard_map/gather_picks/ppermute | solution.py:395
  43.6 1.1 %collective-permute-done.10.other_ref = bf16[192,512]{1,0:T(8,128)(2,1)S(1)} collective-permute-done((bf16[192,512]{1,0:T(8,128)(2,1)S(1)}, bf16[192,512]{1,0:T(8,128)(2,1)S(1)}, u32[]{:S(2)}, u32[]{:S(2)}) %collective-permute-start.10) | collective-permute-done | bytes 196640 | tf_op jit(solution)/shard_map/gather_picks/ppermute | solution.py:395
  44.7 0.3 gram.1
  45.0 0.3 collective-permute-start.13
  45.3 2.1 %collective-permute-start.14 = (f32[128,128]{1,0:T(8,128)S(1)}, f32[128,128]{1,0:T(8,128)S(1)}, u32[]{:S(2)}, u32[]{:S(2)}) collective-permute-start(f32[128,128]{1,0:T(8,128)S(1)} %get-tuple-element.59), channel_id=1, source_target_pairs={{0,4},{1,5},{2,6},{3,7},{4,0},{5,1},{6,2},{7,3},{8,12},{9,13},{10,... | collective-permute-start | bytes 196616 | tf_op jit(solution)/shard_map/sum_gram/ppermute | solution.py:401
  47.5 0.0 copy-done.2
  47.5 0.0 copy-start.3
  47.5 1.0 %products_2.1 = (s16[200,1152]{1,0:T(8,128)(2,1)S(1)}, f32[256,128]{1,0:T(8,128)S(1)}) custom-call(bf16[1152,512]{1,0:T(8,128)(2,1)S(1)} %get-tuple-element.44.e_ref, bf16[1152,512]{1,0:T(8,128)(2,1)S(1)} %copy-done.2, f32[8,1152]{1,0:T(8,128)S(1)} %get-tuple-element.46.norm_ref, bf16[192,512]{1,0:T(8,128)(2,1)S(1)} %order.1.mine_ref, ...), custom_call_target="tpu_custom_call" | custom-call | flops 1000000 | bytes 65536 | tf_op jit(solution)/shard_map/sum_gram/products_2/pallas_call | solution.py:302
  48.5 0.2 copy-done.3
  48.8 0.0 copy-start.1
  48.8 1.0 %products_1.1 = (s16[200,1152]{1,0:T(8,128)(2,1)S(1)}, f32[256,128]{1,0:T(8,128)S(1)}) custom-call(bf16[1152,512]{1,0:T(8,128)(2,1)S(1)} %get-tuple-element.49.e_ref, bf16[1152,512]{1,0:T(8,128)(2,1)S(1)} %copy-done.3, f32[8,1152]{1,0:T(8,128)S(1)} %get-tuple-element.51.norm_ref, bf16[192,512]{1,0:T(8,128)(2,1)S(1)} %order.1.mine_ref, ...), custom_call_target="tpu_custom_call" | custom-call | flops 1000000 | bytes 65536 | tf_op jit(solution)/shard_map/sum_gram/products_1/pallas_call | solution.py:302
  49.8 1.6 %collective-permute-start.12 = (s16[200,1152]{1,0:T(8,128)(2,1)S(1)}, s16[200,1152]{1,0:T(8,128)(2,1)S(1)}, u32[]{:S(2)}, u32[]{:S(2)}) collective-permute-start(s16[200,1152]{1,0:T(8,128)(2,1)S(1)} %get-tuple-element.53), channel_id=1, source_target_pairs={{0,2},{1,3},{2,4},{3,5},{4,6},{5,7},{6,0},{7,1},{8,10},{9,11},{10,... | collective-permute-start | bytes 1382408 | tf_op jit(solution)/shard_map/sum_gram/ppermute | solution.py:404
  51.4 1.2 %collective-permute-start.11 = (s16[200,1152]{1,0:T(8,128)(2,1)S(1)}, s16[200,1152]{1,0:T(8,128)(2,1)S(1)}, u32[]{:S(2)}, u32[]{:S(2)}) collective-permute-start(s16[200,1152]{1,0:T(8,128)(2,1)S(1)} %get-tuple-element.48), channel_id=1, source_target_pairs={{0,4},{1,5},{2,6},{3,7},{4,0},{5,1},{6,2},{7,3},{8,12},{9,13},{10,... | collective-permute-start | bytes 1382408 | tf_op jit(solution)/shard_map/sum_gram/ppermute | solution.py:404
  52.5 0.0 collective-permute-done.14
  52.5 0.0 collective-permute-done.13
  52.6 0.0 copy-done.1
  52.6 0.0 copy-start
  52.6 1.0 %products_3.1 = (s16[200,1152]{1,0:T(8,128)(2,1)S(1)}, f32[256,128]{1,0:T(8,128)S(1)}) custom-call(bf16[1152,512]{1,0:T(8,128)(2,1)S(1)} %get-tuple-element.54.e_ref, bf16[1152,512]{1,0:T(8,128)(2,1)S(1)} %copy-done.1, f32[8,1152]{1,0:T(8,128)S(1)} %get-tuple-element.56.norm_ref, bf16[192,512]{1,0:T(8,128)(2,1)S(1)} %order.1.mine_ref, ...), custom_call_target="tpu_custom_call" | custom-call | flops 1000000 | bytes 65536 | tf_op jit(solution)/shard_map/sum_gram/products_3/pallas_call | solution.py:302
  53.6 1.0 %collective-permute-start.15 = (s16[200,1152]{1,0:T(8,128)(2,1)S(1)}, s16[200,1152]{1,0:T(8,128)(2,1)S(1)}, u32[]{:S(2)}, u32[]{:S(2)}) collective-permute-start(s16[200,1152]{1,0:T(8,128)(2,1)S(1)} %get-tuple-element.60), channel_id=1, source_target_pairs={{0,6},{1,7},{2,0},{3,1},{4,2},{5,3},{6,4},{7,5},{8,14},{9,15},{10,... | collective-permute-start | bytes 1382408 | tf_op jit(solution)/shard_map/sum_gram/ppermute | solution.py:408
  54.6 2.1 %collective-permute-start.16 = (f32[256,128]{1,0:T(8,128)S(1)}, f32[256,128]{1,0:T(8,128)S(1)}, u32[]{:S(2)}, u32[]{:S(2)}) collective-permute-start(f32[256,128]{1,0:T(8,128)S(1)} %pad_maximum_fusion.through_ref), channel_id=1, source_target_pairs={{0,1},{1,0},{2,3},{3,2},{4,5},{5,4},{6,7},{7,6},{8,9},{9,8},{10,11... | collective-permute-start | bytes 393224 | tf_op jit(solution)/shard_map/sum_gram/ppermute | solution.py:406
  56.7 0.0 copy-done
  56.7 0.0 copy-start.4
  56.7 0.0 copy-start.6
  56.7 0.9 %products_0.1.own_ref = f32[192,1152]{1,0:T(8,128)S(1)} custom-call(bf16[1152,512]{1,0:T(8,128)(2,1)S(1)} %get-tuple-element.40.e_ref, bf16[1152,512]{1,0:T(8,128)(2,1)S(1)} %copy-done, bf16[192,512]{1,0:T(8,128)(2,1)S(1)} %order.1.mine_ref, bf16[192,512]{1,0:T(8,128)(2,1)S(1)} %collective-permute-done.10.other_ref), custom_call_target="tpu_custom_call" | custom-call | flops 1000000 | bytes 65536 | tf_op jit(solution)/shard_map/products_0/pallas_call | solution.py:302
  57.6 0.1 collective-permute-done.16.swapped_ref
  57.7 6.6 %factor.1.inverse_ref = f32[192,192]{1,0:T(8,128)S(1)} custom-call(f32[256,128]{1,0:T(8,128)S(1)} %get-tuple-element.61.sum_ref, f32[256,128]{1,0:T(8,128)S(1)} %collective-permute-done.16.swapped_ref), custom_call_target="tpu_custom_call" | custom-call | flops 1000000 | bytes 65536 | tf_op jit(solution)/shard_map/factor/pallas_call | solution.py:246
  64.2 0.0 collective-permute-done.12.g2
  64.2 1.0 %collective-permute-done.11.g1 = s16[200,1152]{1,0:T(8,128)(2,1)S(1)} collective-permute-done((s16[200,1152]{1,0:T(8,128)(2,1)S(1)}, s16[200,1152]{1,0:T(8,128)(2,1)S(1)}, u32[]{:S(2)}, u32[]{:S(2)}) %collective-permute-start.11) | collective-permute-done | bytes 460832 | tf_op jit(solution)/shard_map/sum_gram/ppermute | solution.py:404
  65.2 10.1 %collective-permute-done.15.g3 = s16[200,1152]{1,0:T(8,128)(2,1)S(1)} collective-permute-done((s16[200,1152]{1,0:T(8,128)(2,1)S(1)}, s16[200,1152]{1,0:T(8,128)(2,1)S(1)}, u32[]{:S(2)}, u32[]{:S(2)}) %collective-permute-start.15) | collective-permute-done | bytes 460832 | tf_op jit(solution)/shard_map/sum_gram/ppermute | solution.py:408
  75.3 0.0 copy-done.4
  75.3 0.0 copy-done.6
  75.3 2.8 %finish.1 = (f32[192,1152]{1,0:T(8,128)}, f32[1152]{0:T(1024)}) custom-call(s32[3,64]{1,0:T(4,128)S(1)} %copy-done.6, f32[1152]{0:T(1024)S(1)} %copy-done.4, f32[192,1152]{1,0:T(8,128)S(1)} %products_0.1.own_ref, f32[8,1152]{1,0:T(8,128)S(1)} %get-tuple-element.43.norm_ref, s16[200,1152]{1,0:T(8,128)(2,1)S(1)} %collective-permute-done.11.g1, ...), custom_call_target="tpu_custom_call" | custom-call | flops 509607936 | bytes 4194304 | tf_op jit(solution)/shard_map/finish/pallas_call | solution.py:344
  (7 shorter events, 0.1 us)
Async XLA Ops:
  0.6 17.4 %collective-permute-start = (bf16[9216,512]{1,0:T(8,128)(2,1)}, bf16[9216,512]{1,0:T(8,128)(2,1)}, u32[]{:S(2)}, u32[]{:S(2)}) collective-permute-start(bf16[9216,512]{1,0:T(8,128)(2,1)} %e_ref.9), channel_id=1, source_target_pairs={{0,1},{1,0},{2,3},{3,2},{4,5},{5,4},{6,7},{7,6},{8,9},{9,8},{10,11... | collective-permute-start | bytes 28311560 | tf_op jit(solution)/shard_map/swap_rows/ppermute | solution.py:375
  1.4 0.7 copy-start.5
  5.9 4.1 %collective-permute-start.1 = (bf16[48,512]{1,0:T(8,128)(2,1)S(1)}, bf16[48,512]{1,0:T(8,128)(2,1)S(1)}, u32[]{:S(2)}, u32[]{:S(2)}) collective-permute-start(bf16[48,512]{1,0:T(8,128)(2,1)S(1)} %get-tuple-element.34), channel_id=1, source_target_pairs={{0,8},{8,16},{16,24},{24,0},{32,40},{40,48},{48,56},{56,32},{64,72... | collective-permute-start | bytes 147464 | tf_op jit(solution)/shard_map/gather_picks/ppermute | solution.py:381
  7.1 4.5 %collective-permute-start.2 = (bf16[48,512]{1,0:T(8,128)(2,1)S(1)}, bf16[48,512]{1,0:T(8,128)(2,1)S(1)}, u32[]{:S(2)}, u32[]{:S(2)}) collective-permute-start(bf16[48,512]{1,0:T(8,128)(2,1)S(1)} %get-tuple-element.35), channel_id=1, source_target_pairs={{0,16},{8,24},{16,0},{24,8},{32,48},{40,56},{48,32},{56,40},{64,80... | collective-permute-start | bytes 147464 | tf_op jit(solution)/shard_map/gather_picks/ppermute | solution.py:381
  8.0 3.6 %collective-permute-start.3 = (bf16[48,512]{1,0:T(8,128)(2,1)S(1)}, bf16[48,512]{1,0:T(8,128)(2,1)S(1)}, u32[]{:S(2)}, u32[]{:S(2)}) collective-permute-start(bf16[48,512]{1,0:T(8,128)(2,1)S(1)} %get-tuple-element.36), channel_id=1, source_target_pairs={{0,24},{8,0},{16,8},{24,16},{32,56},{40,32},{48,40},{56,48},{64,88... | collective-permute-start | bytes 147464 | tf_op jit(solution)/shard_map/gather_picks/ppermute | solution.py:381
  11.6 3.3 %collective-permute-start.4 = (bf16[48,512]{1,0:T(8,128)(2,1)S(1)}, bf16[48,512]{1,0:T(8,128)(2,1)S(1)}, u32[]{:S(2)}, u32[]{:S(2)}) collective-permute-start(bf16[48,512]{1,0:T(8,128)(2,1)S(1)} %add_add_fusion), channel_id=1, source_target_pairs={{0,32},{8,40},{16,48},{24,56},{32,0},{40,8},{48,16},{56,24},{64,96... | collective-permute-start | bytes 147464 | tf_op jit(solution)/shard_map/gather_picks/ppermute | solution.py:383
  14.9 6.1 %collective-permute-start.5 = (bf16[48,512]{1,0:T(8,128)(2,1)S(1)}, bf16[48,512]{1,0:T(8,128)(2,1)S(1)}, u32[]{:S(2)}, u32[]{:S(2)}) collective-permute-start(bf16[48,512]{1,0:T(8,128)(2,1)S(1)} %add.30.through_ref), channel_id=1, source_target_pairs={{0,64},{8,72},{16,80},{24,88},{32,96},{40,104},{48,112},{56,120},{... | collective-permute-start | bytes 147464 | tf_op jit(solution)/shard_map/gather_picks/ppermute | solution.py:384
  21.1 6.7 %collective-permute-start.6 = (bf16[48,512]{1,0:T(8,128)(2,1)S(1)}, bf16[48,512]{1,0:T(8,128)(2,1)S(1)}, u32[]{:S(2)}, u32[]{:S(2)}) collective-permute-start(bf16[48,512]{1,0:T(8,128)(2,1)S(1)} %add.31.through_ref), channel_id=1, source_target_pairs={{0,224},{8,232},{16,240},{24,248},{32,192},{40,200},{48,208},{56,2... | collective-permute-start | bytes 147464 | tf_op jit(solution)/shard_map/gather_picks/ppermute | solution.py:387
  27.8 11.0 %collective-permute-start.7 = (bf16[48,512]{1,0:T(8,128)(2,1)S(1)}, bf16[48,512]{1,0:T(8,128)(2,1)S(1)}, u32[]{:S(2)}, u32[]{:S(2)}) collective-permute-start(bf16[48,512]{1,0:T(8,128)(2,1)S(1)} %add.32.through_ref), channel_id=1, source_target_pairs={{0,8},{8,16},{16,24},{24,0},{32,40},{40,48},{48,56},{56,32},{64,72... | collective-permute-start | bytes 147464 | tf_op jit(solution)/shard_map/gather_picks/ppermute | solution.py:390
  29.3 9.5 %collective-permute-start.8 = (bf16[48,512]{1,0:T(8,128)(2,1)S(1)}, bf16[48,512]{1,0:T(8,128)(2,1)S(1)}, u32[]{:S(2)}, u32[]{:S(2)}) collective-permute-start(bf16[48,512]{1,0:T(8,128)(2,1)S(1)} %add.32.through_ref), channel_id=1, source_target_pairs={{0,16},{8,24},{16,0},{24,8},{32,48},{40,56},{48,32},{56,40},{64,80... | collective-permute-start | bytes 147464 | tf_op jit(solution)/shard_map/gather_picks/ppermute | solution.py:390
  31.1 7.8 %collective-permute-start.9 = (bf16[48,512]{1,0:T(8,128)(2,1)S(1)}, bf16[48,512]{1,0:T(8,128)(2,1)S(1)}, u32[]{:S(2)}, u32[]{:S(2)}) collective-permute-start(bf16[48,512]{1,0:T(8,128)(2,1)S(1)} %add.32.through_ref), channel_id=1, source_target_pairs={{0,24},{8,0},{16,8},{24,16},{32,56},{40,32},{48,40},{56,48},{64,88... | collective-permute-start | bytes 147464 | tf_op jit(solution)/shard_map/gather_picks/ppermute | solution.py:390
  35.7 11.8 %copy-start.2 = (bf16[1152,512]{1,0:T(8,128)(2,1)S(1)}, bf16[1152,512]{1,0:T(8,128)(2,1)}, u32[]{:S(2)}) copy-start(bf16[1152,512]{1,0:T(8,128)(2,1)} %get-tuple-element.45.r_ref) | copy-start | bytes 3538948
  38.9 5.8 %collective-permute-start.10 = (bf16[192,512]{1,0:T(8,128)(2,1)S(1)}, bf16[192,512]{1,0:T(8,128)(2,1)S(1)}, u32[]{:S(2)}, u32[]{:S(2)}) collective-permute-start(bf16[192,512]{1,0:T(8,128)(2,1)S(1)} %order.1.mine_ref), channel_id=1, source_target_pairs={{0,1},{1,0},{2,3},{3,2},{4,5},{5,4},{6,7},{7,6},{8,9},{9,8},{10,11... | collective-permute-start | bytes 589832 | tf_op jit(solution)/shard_map/gather_picks/ppermute | solution.py:395
  45.0 7.5 %collective-permute-start.13 = (f32[256,128]{1,0:T(8,128)S(1)}, f32[256,128]{1,0:T(8,128)S(1)}, u32[]{:S(2)}, u32[]{:S(2)}) collective-permute-start(f32[256,128]{1,0:T(8,128)S(1)} %get-tuple-element.58), channel_id=1, source_target_pairs={{0,2},{1,7},{2,4},{3,1},{4,6},{5,3},{6,0},{7,5},{8,10},{9,15},{10,... | collective-permute-start | bytes 393224 | tf_op jit(solution)/shard_map/sum_gram/ppermute | solution.py:400
  45.3 7.2 %collective-permute-start.14 = (f32[128,128]{1,0:T(8,128)S(1)}, f32[128,128]{1,0:T(8,128)S(1)}, u32[]{:S(2)}, u32[]{:S(2)}) collective-permute-start(f32[128,128]{1,0:T(8,128)S(1)} %get-tuple-element.59), channel_id=1, source_target_pairs={{0,4},{1,5},{2,6},{3,7},{4,0},{5,1},{6,2},{7,3},{8,12},{9,13},{10,... | collective-permute-start | bytes 196616 | tf_op jit(solution)/shard_map/sum_gram/ppermute | solution.py:401
  47.5 1.3 %copy-start.3 = (bf16[1152,512]{1,0:T(8,128)(2,1)S(1)}, bf16[1152,512]{1,0:T(8,128)(2,1)}, u32[]{:S(2)}) copy-start(bf16[1152,512]{1,0:T(8,128)(2,1)} %get-tuple-element.50.r_ref) | copy-start | bytes 3538948
  48.8 3.8 %copy-start.1 = (bf16[1152,512]{1,0:T(8,128)(2,1)S(1)}, bf16[1152,512]{1,0:T(8,128)(2,1)}, u32[]{:S(2)}) copy-start(bf16[1152,512]{1,0:T(8,128)(2,1)} %get-tuple-element.55.r_ref) | copy-start | bytes 3538948
  49.8 14.4 %collective-permute-start.12 = (s16[200,1152]{1,0:T(8,128)(2,1)S(1)}, s16[200,1152]{1,0:T(8,128)(2,1)S(1)}, u32[]{:S(2)}, u32[]{:S(2)}) collective-permute-start(s16[200,1152]{1,0:T(8,128)(2,1)S(1)} %get-tuple-element.53), channel_id=1, source_target_pairs={{0,2},{1,3},{2,4},{3,5},{4,6},{5,7},{6,0},{7,1},{8,10},{9,11},{10,... | collective-permute-start | bytes 1382408 | tf_op jit(solution)/shard_map/sum_gram/ppermute | solution.py:404
  51.4 13.8 %collective-permute-start.11 = (s16[200,1152]{1,0:T(8,128)(2,1)S(1)}, s16[200,1152]{1,0:T(8,128)(2,1)S(1)}, u32[]{:S(2)}, u32[]{:S(2)}) collective-permute-start(s16[200,1152]{1,0:T(8,128)(2,1)S(1)} %get-tuple-element.48), channel_id=1, source_target_pairs={{0,4},{1,5},{2,6},{3,7},{4,0},{5,1},{6,2},{7,3},{8,12},{9,13},{10,... | collective-permute-start | bytes 1382408 | tf_op jit(solution)/shard_map/sum_gram/ppermute | solution.py:404
  52.6 4.1 %copy-start = (bf16[1152,512]{1,0:T(8,128)(2,1)S(1)}, bf16[1152,512]{1,0:T(8,128)(2,1)}, u32[]{:S(2)}) copy-start(bf16[1152,512]{1,0:T(8,128)(2,1)} %get-tuple-element.41.r_ref) | copy-start | bytes 3538948
  53.6 21.6 %collective-permute-start.15 = (s16[200,1152]{1,0:T(8,128)(2,1)S(1)}, s16[200,1152]{1,0:T(8,128)(2,1)S(1)}, u32[]{:S(2)}, u32[]{:S(2)}) collective-permute-start(s16[200,1152]{1,0:T(8,128)(2,1)S(1)} %get-tuple-element.60), channel_id=1, source_target_pairs={{0,6},{1,7},{2,0},{3,1},{4,2},{5,3},{6,4},{7,5},{8,14},{9,15},{10,... | collective-permute-start | bytes 1382408 | tf_op jit(solution)/shard_map/sum_gram/ppermute | solution.py:408
  54.6 3.1 %collective-permute-start.16 = (f32[256,128]{1,0:T(8,128)S(1)}, f32[256,128]{1,0:T(8,128)S(1)}, u32[]{:S(2)}, u32[]{:S(2)}) collective-permute-start(f32[256,128]{1,0:T(8,128)S(1)} %pad_maximum_fusion.through_ref), channel_id=1, source_target_pairs={{0,1},{1,0},{2,3},{3,2},{4,5},{5,4},{6,7},{7,6},{8,9},{9,8},{10,11... | collective-permute-start | bytes 393224 | tf_op jit(solution)/shard_map/sum_gram/ppermute | solution.py:406
  56.7 18.6 %copy-start.4 = (f32[1152]{0:T(1024)S(1)}, f32[1152]{0:T(1024)}, u32[]{:S(2)}) copy-start(f32[1152]{0:T(1024)} %quality_ref.1) | copy-start | bytes 13828
  56.7 18.6 %copy-start.6 = (s32[3,64]{1,0:T(4,128)S(1)}, s32[3,64]{1,0:T(4,128)}, u32[]{:S(2)}) copy-start(s32[3,64]{1,0:T(4,128)} %picks_ref.3) | copy-start | bytes 2308

commit v3 on v2

--- a/solution.py
+++ b/solution.py
@@ -73,7 +73,7 @@
     y = lax.rem(lax.axis_index("rows"), Y)
     group = total // Y
     for j in range(Y):
-        g = lax.rem(y + j, Y)
+        g = lax.bitwise_xor(y, j)
         outs[j][...] = rows_ref[pl.ds(pl.multiple_of(g * group, 16), group), :].astype(bf16)
 
 
@@ -97,7 +97,7 @@
     )(picks, embeddings)
 
 
-def stage_kernel(hop, e_ref, r_ref, through_ref, mine_ref, other_ref, norm_ref, passed_ref, arrived):
+def fetch_rows(hop, e_ref, r_ref, mine_ref, other_ref, arrived):
     d = lax.axis_index("dim")
     chip, core = lax.div(d, 2), lax.rem(d, 2)
     first = (lax.rem(chip + hop, X) * 2 + core) * pack
@@ -114,20 +114,31 @@
     for pair in copies:
         for copy in pair:
             copy.start()
+    return copies
+
+
+def squared_norms(i, mine_ref, other_ref):
+    tile = pack // 3
+    squares = jnp.zeros((tile, 128), f32)
+    for ref in (mine_ref, other_ref):
+        for j in range(0, ref.shape[1], 128):
+            part = ref[i * tile : (i + 1) * tile, j : j + 128].astype(f32)
+            squares += part * part
+    high = squares.astype(bf16)
+    low = (squares - high.astype(f32)).astype(bf16)
+    ones = jnp.ones((8, 128), bf16)
+    norm = lax.dot_general(ones, high, NT, preferred_element_type=f32)
+    return norm + lax.dot_general(ones, low, NT, preferred_element_type=f32)
+
+
+def stage_kernel(hop, e_ref, r_ref, through_ref, mine_ref, other_ref, norm_ref, passed_ref, arrived):
+    copies = fetch_rows(hop, e_ref, r_ref, mine_ref, other_ref, arrived)
     passed_ref[...] = through_ref[...]
+    tile = pack // 3
     for i in range(3):
         for copy in copies[i]:
             copy.wait()
-        squares = jnp.zeros((tile, 128), f32)
-        for ref in (mine_ref, other_ref):
-            for j in range(0, ref.shape[1], 128):
-                part = ref[i * tile : (i + 1) * tile, j : j + 128].astype(f32)
-                squares += part * part
-        high = squares.astype(bf16)
-        low = (squares - high.astype(f32)).astype(bf16)
-        ones = jnp.ones((8, 128), bf16)
-        norm = lax.dot_general(ones, high, NT, preferred_element_type=f32)
-        norm_ref[:, i * tile : (i + 1) * tile] = norm + lax.dot_general(ones, low, NT, preferred_element_type=f32)
+        norm_ref[:, i * tile : (i + 1) * tile] = squared_norms(i, mine_ref, other_ref)
 
 
 def stage(hop, embeddings, received, through):
@@ -143,7 +154,7 @@
             shape(through.shape, through.dtype),
         ],
         scratch_shapes=[pltpu.SemaphoreType.DMA((6,))],
-        compiler_params=params(52),
+        compiler_params=params(50),
         cost_estimate=cost(0, 4 * pack * dims),
         name="stage_%d" % hop,
     )(embeddings, received, through)
@@ -153,7 +164,7 @@
     y = lax.rem(lax.axis_index("rows"), Y)
     group = s0.shape[0]
     for j, ref in enumerate((s0, s1, s2, s3)):
-        g = pl.multiple_of(lax.rem(y + (Y - j), Y) * group, 16)
+        g = pl.multiple_of(lax.bitwise_xor(y, j) * group, 16)
         out_ref[pl.ds(g, group), :] = ref[...]
 
 
@@ -170,7 +181,7 @@
     )(*groups)
 
 
-def gram_kernel(mine_ref, other_ref, full_ref, half_ref, keep_ref):
+def gram_kernel(mine_ref, other_ref, token_ref, full_ref, half_ref, keep_ref):
     mine, other = mine_ref[...], other_ref[...]
     gram = lax.dot_general(mine, mine, NT, preferred_element_type=f32)
     gram += lax.dot_general(other, other, NT, preferred_element_type=f32)
@@ -184,24 +195,24 @@
     keep_ref[:128, :], keep_ref[128:, :] = jnp.where(core == 0, a, 0.0), jnp.where(core == 0, b, 0.0)
 
 
-def picks_gram(mine, other):
+def picks_gram(mine, other, token):
     total, dims = mine.shape
     return pl.pallas_call(
         gram_kernel,
-        in_specs=[VMEM] * 2,
+        in_specs=[VMEM] * 3,
         out_specs=[VMEM] * 3,
         out_shape=[shape((256, 128), f32), shape((128, 128), f32), shape((256, 128), f32)],
         compiler_params=params(16),
         cost_estimate=cost(4 * total * total * dims, 4 * total * dims),
         name="gram",
-    )(mine, other)
+    )(mine, other, token)
 
 
 panel, together = 64, 8
 
 
-def factor_kernel(sum_ref, swapped_ref, inverse_ref, m_ref):
-    n = inverse_ref.shape[0]
+def factor_kernel(sum_ref, swapped_ref, high_ref, low_ref, m_ref):
+    n = high_ref.shape[0]
     core = lax.rem(lax.axis_index("dim"), 2)
     a = sum_ref[:128, :] + swapped_ref[128:, :]
     b = sum_ref[128:, :] + swapped_ref[:128, :]
@@ -236,7 +247,10 @@
                 tiles = [t - factors * y for t, y in zip(tiles, heads[i])]
         pivots = jnp.sum(jnp.where(at == off, tiles[0], 0.0), axis=1, keepdims=True)
         rows = jnp.concatenate(tiles, axis=1) * (1.0 / jnp.sqrt(pivots))
-        inverse_ref[low : low + panel, :] = rows[:, n - left :]
+        inverse = rows[:, n - left :]
+        high = inverse.astype(bf16)
+        high_ref[low : low + panel, :] = high
+        low_ref[low : low + panel, :] = (inverse - high.astype(f32)).astype(bf16)
         if low + panel < n:
             update = lax.dot_general(rows[:, : n - left], rows, TN, precision=HIGHEST, preferred_element_type=f32)
             m_ref[low + panel :, left:] -= update[low + panel - left :, :]
@@ -246,8 +260,8 @@
     return pl.pallas_call(
         factor_kernel,
         in_specs=[VMEM] * 2,
-        out_specs=VMEM,
-        out_shape=shape((n, n), f32),
+        out_specs=[VMEM] * 2,
+        out_shape=[shape((n, n), bf16)] * 2,
         scratch_shapes=[pltpu.VMEM((n, 2 * n), f32)],
         compiler_params=params(16),
         cost_estimate=cost(1e6, 1 << 16),
@@ -270,65 +284,134 @@
     return part + lax.dot_general(other_ref[...], r_ref[at, :], NT, preferred_element_type=f32)
 
 
-def send_kernel(e_ref, r_ref, norm_ref, mine_ref, other_ref, through_ref, out_ref, passed_ref):
+def coded(part, norm):
+    norm_high, norm_low = split(norm)
+    top_high, top_low = split(jnp.max(jnp.abs(part), axis=0, keepdims=True))
+    scale = join(top_high, top_low + 1.0)
+    whole = jnp.floor(part * (levels / scale) + 0.5)
+    row = lax.broadcasted_iota(i32, (8, part.shape[1]), 0)
+    extra = jnp.where(row == 0, norm_high, jnp.where(row == 1, norm_low, jnp.where(row == 2, top_high, top_low)))
+    return jnp.concatenate([whole, extra], axis=0).astype(i32).astype(i16)
+
+
+def decoded(ref, at, total):
+    got = ref[:, at].astype(i32).astype(f32)
+    scale = join(got[total + 2 : total + 3], got[total + 3 : total + 4] + 1.0)
+    norm = join(got[total : total + 1], got[total + 1 : total + 2] + 0.5)
+    return got[:total] * (scale * (1.0 / levels)), norm
+
+
+cut = 640
+spans = ((0, 384), (384, 256), (640, 512))
+
+
+def far_kernel(e_ref, r_ref, norm_ref, mine_ref, other_ref, low_ref, high_ref, token_ref):
+    for low, width in spans:
+        at = pl.ds(low, width)
+        part = block_products(at, e_ref, r_ref, mine_ref, other_ref)
+        out = coded(part, norm_ref[:1, at])
+        if low < cut:
+            low_ref[:, at] = out
+        else:
+            high_ref[:, low - cut : low - cut + width] = out
+    token_ref[...] = jnp.zeros_like(token_ref)
+
+
+def both_kernel(e_next, r_next, e_last, r_last, mine_ref, other_ref, through_ref, next_ref, last_ref, passed_ref):
+    passed_ref[...] = through_ref[...]
+    for low, width in spans:
+        at = pl.ds(low, width)
+        next_ref[:, at] = block_products(at, e_next, r_next, mine_ref, other_ref)
+        last_ref[:, at] = block_products(at, e_last, r_last, mine_ref, other_ref)
+
+
+def near_kernel(begin, end, part_ref, norm_ref, got_ref, through_ref, out_ref, passed_ref):
+    total = part_ref.shape[0]
+    passed_ref[...] = through_ref[...]
+    for low, width in spans:
+        at = pl.ds(low, width)
+        part, norm = part_ref[:, at], norm_ref[:1, at]
+        if begin <= low < end:
+            more, more_norm = decoded(got_ref, pl.ds(low - begin, width), total)
+            part, norm = part + more, norm + more_norm
+        out_ref[:, at] = coded(part, norm)
+
+
+def own_kernel(
+    picks_ref, e_ref, r_ref, mine_ref, other_ref, through_ref, out_ref, norm_ref, passed_ref, e_here, r_here, arrived
+):
+    copies = fetch_rows(0, e_ref, r_ref, e_here, r_here, arrived)
+    passed_ref[...] = through_ref[...]
+    rounds, count = picks_ref.shape
+    first_row = (lax.axis_index("rows") * (2 * X) + lax.axis_index("dim")) * pack
+    chosen = jnp.concatenate([as_column(picks_ref[r : r + 1, :]) for r in range(rounds)], axis=0) - first_row
     tile = pack // 3
-    passed_ref[...] = through_ref[...]
-    for low in range(0, pack, tile):
-        at = pl.ds(low, tile)
-        part = block_products(at, e_ref, r_ref, mine_ref, other_ref)
-        norm_high, norm_low = split(norm_ref[:1, at])
-        top_high, top_low = split(jnp.max(jnp.abs(part), axis=0, keepdims=True))
-        scale = join(top_high, top_low + 1.0)
-        coded = jnp.floor(part * (levels / scale) + 0.5)
-        row = lax.broadcasted_iota(i32, (8, tile), 0)
-        extra = jnp.where(row == 0, norm_high, jnp.where(row == 1, norm_low, jnp.where(row == 2, top_high, top_low)))
-        out_ref[:, at] = jnp.concatenate([coded, extra], axis=0).astype(i32).astype(i16)
-
-
-def keep_kernel(e_ref, r_ref, mine_ref, other_ref, out_ref):
-    tile = pack // 3
-    for low in range(0, pack, tile):
-        out_ref[:, low : low + tile] = block_products(pl.ds(low, tile), e_ref, r_ref, mine_ref, other_ref)
-
-
-def products(hop, staged, mine, other, through=None):
-    total, dims = mine.shape
-    if hop:
-        operands = (*staged, mine, other, through)
-        out_shape = [shape((total + 8, pack), i16), shape(through.shape, through.dtype)]
-    else:
-        operands = (*staged[:2], mine, other)
-        out_shape = [shape((total, pack), f32)]
-    return pl.pallas_call(
-        send_kernel if hop else keep_kernel,
-        in_specs=[VMEM] * len(operands),
+    for i in range(3):
+        for copy in copies[i]:
+            copy.wait()
+        at = slice(i * tile, (i + 1) * tile)
+        norm_ref[:, at] = squared_norms(i, e_here, r_here)
+        part = block_products(pl.ds(i * tile, tile), e_here, r_here, mine_ref, other_ref)
+        lane = lax.broadcasted_iota(i32, part.shape, 1) + i * tile
+        out_ref[:, at] = jnp.where(chosen == lane, part + ridge_term, part)
+
+
+def quick(kernel, name, in_specs, out_shape, mib=16, scratch=(), flops=1e6):
+    return pl.pallas_call(
+        kernel,
+        in_specs=in_specs,
         out_specs=[VMEM] * len(out_shape),
         out_shape=out_shape,
-        compiler_params=params(16),
-        cost_estimate=cost(1e6, 1 << 16),
-        name="products_%d" % hop,
-    )(*operands)
-
-
-def finish_kernel(picks_ref, quality_ref, own_ref, norm_ref, g1, g2, g3, inverse_ref, out_ref, resid_ref, stage_ref, sent):
+        scratch_shapes=scratch,
+        compiler_params=params(mib),
+        cost_estimate=cost(flops, 1 << 16),
+        name=name,
+    )
+
+
+def far_products(staged, mine, other):
+    total = mine.shape[0]
+    out_shape = [shape((total + 8, cut), i16), shape((total + 8, pack - cut), i16), shape((8, 128), f32)]
+    return quick(far_kernel, "products_far", [VMEM] * 5, out_shape)(*staged, mine, other)
+
+
+def both_products(following, last, mine, other, through):
+    total = mine.shape[0]
+    out_shape = [shape((total, pack), f32)] * 2 + [shape(through.shape, through.dtype)]
+    return quick(both_kernel, "products_both", [VMEM] * 7, out_shape)(*following[:2], *last[:2], mine, other, through)
+
+
+def near_block(begin, end, part, norm, got, through):
+    out_shape = [shape((part.shape[0] + 8, pack), i16), shape(through.shape, through.dtype)]
+    kernel = functools.partial(near_kernel, begin, end)
+    return quick(kernel, "near_%d" % begin, [VMEM] * 4, out_shape)(part, norm, got, through)
+
+
+def own_products(picks, embeddings, received, mine, other, through):
+    total, dims = mine.shape
+    out_shape = [shape((total, pack), f32), shape((8, pack), f32), shape(through.shape, through.dtype)]
+    scratch = [pltpu.VMEM((pack, dims), bf16), pltpu.VMEM((pack, dims), bf16), pltpu.SemaphoreType.DMA((6,))]
+    in_specs = [VMEM, ANY, ANY, VMEM, VMEM, VMEM]
+    call = quick(own_kernel, "products_own", in_specs, out_shape, 46, scratch)
+    return call(picks, embeddings, received, mine, other, through)
+
+
+def finish_kernel(quality_ref, own_ref, norm_ref, g1, g2, inv_high, inv_low, out_ref, resid_ref, stage_ref, sent):
     total, width = own_ref.shape
-    rounds, count = picks_ref.shape
-    first_row = (lax.axis_index("rows") * (2 * X) + lax.axis_index("dim")) * width
-    chosen = jnp.concatenate([as_column(picks_ref[r : r + 1, :]) for r in range(rounds)], axis=0) - first_row
-    inverse = inverse_ref[...]
+    inverse_high, inverse_low = inv_high[...], inv_low[...]
     tile = width // 3
     copies = []
     for i in range(3):
         here = pl.ds(i * tile, tile)
         values, norm = own_ref[:, here], norm_ref[:1, here]
-        for ref in (g1, g2, g3):
-            got = ref[:, here].astype(i32).astype(f32)
-            scale = join(got[total + 2 : total + 3], got[total + 3 : total + 4] + 1.0)
-            values = values + got[:total] * (scale * (1.0 / levels))
-            norm = norm + join(got[total : total + 1], got[total + 1 : total + 2] + 0.5)
-        lane = lax.broadcasted_iota(i32, (total, tile), 1) + i * tile
-        values = jnp.where(chosen == lane, values + ridge_term, values)
-        columns = jnp.dot(inverse, values, precision=HIGHEST, preferred_element_type=f32)
+        for ref in (g1, g2):
+            more, more_norm = decoded(ref, here, total)
+            values, norm = values + more, norm + more_norm
+        high = values.astype(bf16)
+        low = (values - high.astype(f32)).astype(bf16)
+        columns = jnp.dot(inverse_high, high, preferred_element_type=f32)
+        columns += jnp.dot(inverse_high, low, preferred_element_type=f32)
+        columns += jnp.dot(inverse_low, high, preferred_element_type=f32)
         score = quality_ref[here].reshape(1, tile)
         stage_ref[:, here] = columns * score
         copies.append(pltpu.make_async_copy(stage_ref.at[:, here], out_ref.at[:, here], sent.at[i]))
@@ -339,22 +422,22 @@
         copy.wait()
 
 
-def finish(picks, quality, own, norm, got, inverse):
+def finish(quality, own, norm, got, inverse):
     total, width = own.shape
     return pl.pallas_call(
         finish_kernel,
-        in_specs=[VMEM] * 8,
+        in_specs=[VMEM] * 7,
         out_specs=[ANY, VMEM],
         out_shape=[shape((total, width), f32), shape((width,), f32)],
         scratch_shapes=[pltpu.VMEM((total, width), f32), pltpu.SemaphoreType.DMA((3,))],
         compiler_params=params(16),
         cost_estimate=cost(12 * total * total * width, 4 << 20),
         name="finish",
-    )(picks, quality, own, norm, *got, inverse)
+    )(quality, own, norm, *got, *inverse)
 
 
 def along_y(k):
-    return [(r, r // Y * Y + (r % Y + k) % Y) for r in range(Y * Z)]
+    return [(r, r ^ k) for r in range(Y * Z)]
 
 
 def along_z(partner):
@@ -384,31 +467,33 @@
         arrived = lax.ppermute(mine, "rows", along_z(lambda z: z ^ 2))
         *staged[2], mine = stage(2, embeddings, received, mine)
         mine = mine + arrived
-        arrived = lax.ppermute(mine, "rows", along_z(lambda z: Z - 1 - z))
+        arrived = lax.ppermute(mine, "rows", along_z(lambda z: z ^ 6))
         *staged[1], mine = stage(1, embeddings, received, mine)
         mine = mine + arrived
         groups = [mine] + [lax.ppermute(mine, "rows", along_y(k)) for k in range(1, Y)]
         *staged[3], mine = stage(3, embeddings, received, mine)
-        *staged[0], mine = stage(0, embeddings, received, mine)
         groups[0] = mine
         pick_mine = in_order(groups)
         pick_other = lax.ppermute(pick_mine, "dim", swap)
 
-    full, half, keep = picks_gram(pick_mine, pick_other)
-    got = {}
+    with jax.named_scope("sum_products"):
+        to_next, to_last, token = far_products(staged[2], pick_mine, pick_other)
+        from_last = lax.ppermute(to_next, "dim", along_x(1))
+        from_next = lax.ppermute(to_last, "dim", along_x(3))
+        full, half, keep = picks_gram(pick_mine, pick_other, token)
+        gram_near = lax.ppermute(full, "dim", both_ways)
+        gram_far = lax.ppermute(half, "dim", along_x(2))
+        for_next, for_last, keep = both_products(staged[1], staged[3], pick_mine, pick_other, keep)
+        onward, keep = near_block(0, cut, for_next, staged[1][2], from_last, keep)
+        got_last = lax.ppermute(onward, "dim", along_x(1))
+        onward, keep = near_block(cut, pack, for_last, staged[3][2], from_next, keep)
+        got_next = lax.ppermute(onward, "dim", along_x(3))
     with jax.named_scope("sum_gram"):
-        near = lax.ppermute(full, "dim", both_ways)
-        far = lax.ppermute(half, "dim", along_x(2))
-        for hop in (2, 1):
-            coded, keep = products(hop, staged[hop], pick_mine, pick_other, keep)
-            got[hop] = lax.ppermute(coded, "dim", along_x(hop))
-        gram = jnp.concatenate([keep[:128] + near[:128] + far, keep[128:] + near[128:]], axis=0)
+        gram = jnp.concatenate([keep[:128] + gram_near[:128] + gram_far, keep[128:] + gram_near[128:]], axis=0)
         gram_other = lax.ppermute(gram, "dim", swap)
-        coded, gram = products(3, staged[3], pick_mine, pick_other, gram)
-        got[3] = lax.ppermute(coded, "dim", along_x(3))
+    own, norm, gram = own_products(picked_rows, embeddings, received, pick_mine, pick_other, gram)
     inverse = factor_inverse(gram, gram_other, total)
-    own = products(0, staged[0], pick_mine, pick_other)[0]
-    columns, residual = finish(picked_rows, quality, own, staged[0][2], [got[k] for k in (2, 1, 3)], inverse)
+    columns, residual = finish(quality, own, norm, [got_last, got_next], inverse)
     return columns.T, residual
 
 

time: 78.9 us -> 69.7 us (0.88)
  the two profiles are of different devices: /device:TPU:11 before, /device:TPU:1 now
where the time goes in v3:
time: 69.7 us; the launch traced here: 69.4 us
  starting transfers between devices  34.9 us (50%)
  Pallas kernels  24.8 us (36%)
  waiting for transfers between devices  7.89 us (11%)
  between operations  1.01 us (1%)
    pallas_call x1, Pallas kernels, factor_inverse(): pl.pallas_call(factor_kernel, in_specs=[VMEM] * 2, out_specs=[VMEM] * 2,...  6.62 us
    pallas_call x3, Pallas kernels, stage(): pl.pallas_call(functools.partial(stage_kernel, hop), in_specs=[ANY, ANY,...  6.43 us
    ppermute x1, starting transfers between devices, per_device(): pick_other = lax.ppermute(pick_mine, 'dim', swap)  5.64 us
    ppermute x1, starting transfers between devices, per_device(): arrived = lax.ppermute(mine, 'rows', along_z(lambda z: z ^ 6))  4.59 us
    ppermute x3, starting transfers between devices, per_device(): mine = mine + lax.ppermute(parts[k], 'rows', along_y(k))  3.95 us
    ppermute x3, starting transfers between devices, per_device(): lax.ppermute(mine, 'rows', along_y(k))  3.34 us
    ppermute x1, starting transfers between devices, per_device(): received = lax.ppermute(embeddings, 'dim', swap)  3.33 us
    ppermute x3, waiting for transfers between devices, per_device(): mine = mine + lax.ppermute(parts[k], 'rows', along_y(k))  3.24 us
  transfers between devices with their start and end apart: 18, of which 5 were waited for; matrix products, arithmetic and copies ran while one was open for 0% of the time, Pallas kernels for 31%

profile of v3, /device:TPU:1, one launch (start us, length us, event | category | flops | bytes accessed | tf_op | source)
XLA Modules:
  0.0 69.4 jit_solution(3627112248129683032)
XLA Ops:
  0.6 3.3 %collective-permute-start = (bf16[9216,512]{1,0:T(8,128)(2,1)}, bf16[9216,512]{1,0:T(8,128)(2,1)}, u32[]{:S(2)}, u32[]{:S(2)}) collective-permute-start(bf16[9216,512]{1,0:T(8,128)(2,1)} %e_ref.9), channel_id=1, source_target_pairs={{0,1},{1,0},{2,3},{3,2},{4,5},{5,4},{6,7},{7,6},{8,9},{9,8},{10,11... | collective-permute-start | bytes 28311560 | tf_op jit(solution)/shard_map/swap_rows/ppermute | solution.py:458
  4.0 0.0 copy-start.1
  4.0 0.7 copy-done.1
  4.6 3.0 %local_picks.1 = (bf16[48,512]{1,0:T(8,128)(2,1)S(1)}, bf16[48,512]{1,0:T(8,128)(2,1)S(1)}, bf16[48,512]{1,0:T(8,128)(2,1)S(1)}, bf16[48,512]{1,0:T(8,128)(2,1)S(1)}) custom-call(s32[3,64]{1,0:T(4,128)S(1)} %copy-done.1, bf16[9216,512]{1,0:T(8,128)(2,1)} %e_ref.9), custom_call_target="tpu_custom_call" | custom-call | bytes 10485760 | tf_op jit(solution)/shard_map/gather_picks/local_picks/pallas_call | solution.py:83
  7.6 0.4 collective-permute-start.1
  8.0 2.6 %collective-permute-start.2 = (bf16[48,512]{1,0:T(8,128)(2,1)S(1)}, bf16[48,512]{1,0:T(8,128)(2,1)S(1)}, u32[]{:S(2)}, u32[]{:S(2)}) collective-permute-start(bf16[48,512]{1,0:T(8,128)(2,1)S(1)} %get-tuple-element.40), channel_id=1, source_target_pairs={{0,16},{8,24},{16,0},{24,8},{32,48},{40,56},{48,32},{56,40},{64,80... | collective-permute-start | bytes 147464 | tf_op jit(solution)/shard_map/gather_picks/ppermute | solution.py:464
  10.6 0.9 %collective-permute-start.3 = (bf16[48,512]{1,0:T(8,128)(2,1)S(1)}, bf16[48,512]{1,0:T(8,128)(2,1)S(1)}, u32[]{:S(2)}, u32[]{:S(2)}) collective-permute-start(bf16[48,512]{1,0:T(8,128)(2,1)S(1)} %get-tuple-element.41), channel_id=1, source_target_pairs={{0,24},{8,16},{16,8},{24,0},{32,56},{40,48},{48,40},{56,32},{64,88... | collective-permute-start | bytes 147464 | tf_op jit(solution)/shard_map/gather_picks/ppermute | solution.py:464
  11.6 0.0 collective-permute-done.1
  11.6 2.0 %collective-permute-done.2 = bf16[48,512]{1,0:T(8,128)(2,1)S(1)} collective-permute-done((bf16[48,512]{1,0:T(8,128)(2,1)S(1)}, bf16[48,512]{1,0:T(8,128)(2,1)S(1)}, u32[]{:S(2)}, u32[]{:S(2)}) %collective-permute-start.2) | collective-permute-done | bytes 49184 | tf_op jit(solution)/shard_map/gather_picks/ppermute | solution.py:464
  13.6 1.2 %collective-permute-done.3 = bf16[48,512]{1,0:T(8,128)(2,1)S(1)} collective-permute-done((bf16[48,512]{1,0:T(8,128)(2,1)S(1)}, bf16[48,512]{1,0:T(8,128)(2,1)S(1)}, u32[]{:S(2)}, u32[]{:S(2)}) %collective-permute-start.3) | collective-permute-done | bytes 49184 | tf_op jit(solution)/shard_map/gather_picks/ppermute | solution.py:464
  14.8 1.8 %collective-permute-start.4 = (bf16[48,512]{1,0:T(8,128)(2,1)S(1)}, bf16[48,512]{1,0:T(8,128)(2,1)S(1)}, u32[]{:S(2)}, u32[]{:S(2)}) collective-permute-start(bf16[48,512]{1,0:T(8,128)(2,1)S(1)} %add_add_fusion), channel_id=1, source_target_pairs={{0,32},{8,40},{16,48},{24,56},{32,0},{40,8},{48,16},{56,24},{64,96... | collective-permute-start | bytes 147464 | tf_op jit(solution)/shard_map/gather_picks/ppermute | solution.py:466
  16.6 1.5 %collective-permute-done.4 = bf16[48,512]{1,0:T(8,128)(2,1)S(1)} collective-permute-done((bf16[48,512]{1,0:T(8,128)(2,1)S(1)}, bf16[48,512]{1,0:T(8,128)(2,1)S(1)}, u32[]{:S(2)}, u32[]{:S(2)}) %collective-permute-start.4) | collective-permute-done | bytes 49184 | tf_op jit(solution)/shard_map/gather_picks/ppermute | solution.py:466
  18.1 3.1 %collective-permute-start.5 = (bf16[48,512]{1,0:T(8,128)(2,1)S(1)}, bf16[48,512]{1,0:T(8,128)(2,1)S(1)}, u32[]{:S(2)}, u32[]{:S(2)}) collective-permute-start(bf16[48,512]{1,0:T(8,128)(2,1)S(1)} %add.30.through_ref), channel_id=1, source_target_pairs={{0,64},{8,72},{16,80},{24,88},{32,96},{40,104},{48,112},{56,120},{... | collective-permute-start | bytes 147464 | tf_op jit(solution)/shard_map/gather_picks/ppermute | solution.py:467
  21.2 0.0 collective-permute-done.r_ref
  21.2 2.1 %stage_2.1 = (bf16[1152,512]{1,0:T(8,128)(2,1)S(1)}, bf16[1152,512]{1,0:T(8,128)(2,1)S(1)}, f32[8,1152]{1,0:T(8,128)S(1)}, bf16[48,512]{1,0:T(8,128)(2,1)S(1)}) custom-call(bf16[9216,512]{1,0:T(8,128)(2,1)} %e_ref.9, bf16[9216,512]{1,0:T(8,128)(2,1)} %collective-permute-done.r_ref, bf16[48,512]{1,0:T(8,128)(2,1)S(1)} %add.30.through_ref), custom_call_target="tpu_custom_call" | custom-call | bytes 2359296 | tf_op jit(solution)/shard_map/gather_picks/stage_2/pallas_call | solution.py:146
  23.3 0.0 collective-permute-done.5
  23.4 4.6 %collective-permute-start.6 = (bf16[48,512]{1,0:T(8,128)(2,1)S(1)}, bf16[48,512]{1,0:T(8,128)(2,1)S(1)}, u32[]{:S(2)}, u32[]{:S(2)}) collective-permute-start(bf16[48,512]{1,0:T(8,128)(2,1)S(1)} %add.31.through_ref), channel_id=1, source_target_pairs={{0,192},{8,200},{16,208},{24,216},{32,224},{40,232},{48,240},{56,2... | collective-permute-start | bytes 147464 | tf_op jit(solution)/shard_map/gather_picks/ppermute | solution.py:470
  27.9 2.1 %stage_1.1 = (bf16[1152,512]{1,0:T(8,128)(2,1)S(1)}, bf16[1152,512]{1,0:T(8,128)(2,1)S(1)}, f32[8,1152]{1,0:T(8,128)S(1)}, bf16[48,512]{1,0:T(8,128)(2,1)S(1)}) custom-call(bf16[9216,512]{1,0:T(8,128)(2,1)} %e_ref.9, bf16[9216,512]{1,0:T(8,128)(2,1)} %collective-permute-done.r_ref, bf16[48,512]{1,0:T(8,128)(2,1)S(1)} %add.31.through_ref), custom_call_target="tpu_custom_call" | custom-call | bytes 2359296 | tf_op jit(solution)/shard_map/gather_picks/stage_1/pallas_call | solution.py:146
  30.1 0.0 collective-permute-done.6
  30.1 0.6 collective-permute-start.9
  30.7 0.9 %collective-permute-start.8 = (bf16[48,512]{1,0:T(8,128)(2,1)S(1)}, bf16[48,512]{1,0:T(8,128)(2,1)S(1)}, u32[]{:S(2)}, u32[]{:S(2)}) collective-permute-start(bf16[48,512]{1,0:T(8,128)(2,1)S(1)} %add.32.through_ref), channel_id=1, source_target_pairs={{0,16},{8,24},{16,0},{24,8},{32,48},{40,56},{48,32},{56,40},{64,80... | collective-permute-start | bytes 147464 | tf_op jit(solution)/shard_map/gather_picks/ppermute | solution.py:473
  31.6 1.8 %collective-permute-start.7 = (bf16[48,512]{1,0:T(8,128)(2,1)S(1)}, bf16[48,512]{1,0:T(8,128)(2,1)S(1)}, u32[]{:S(2)}, u32[]{:S(2)}) collective-permute-start(bf16[48,512]{1,0:T(8,128)(2,1)S(1)} %add.32.through_ref), channel_id=1, source_target_pairs={{0,8},{8,0},{16,24},{24,16},{32,40},{40,32},{48,56},{56,48},{64,72... | collective-permute-start | bytes 147464 | tf_op jit(solution)/shard_map/gather_picks/ppermute | solution.py:473
  33.5 2.1 %stage_3.1 = (bf16[1152,512]{1,0:T(8,128)(2,1)S(1)}, bf16[1152,512]{1,0:T(8,128)(2,1)S(1)}, f32[8,1152]{1,0:T(8,128)S(1)}, bf16[48,512]{1,0:T(8,128)(2,1)S(1)}) custom-call(bf16[9216,512]{1,0:T(8,128)(2,1)} %e_ref.9, bf16[9216,512]{1,0:T(8,128)(2,1)} %collective-permute-done.r_ref, bf16[48,512]{1,0:T(8,128)(2,1)S(1)} %add.32.through_ref), custom_call_target="tpu_custom_call" | custom-call | bytes 2359296 | tf_op jit(solution)/shard_map/gather_picks/stage_3/pallas_call | solution.py:146
  35.6 0.0 collective-permute-done.9.s3
  35.6 0.0 collective-permute-done.8.s2
  35.6 0.0 collective-permute-done.7.s1
  35.7 5.6 %collective-permute-start.10 = (bf16[192,512]{1,0:T(8,128)(2,1)S(1)}, bf16[192,512]{1,0:T(8,128)(2,1)S(1)}, u32[]{:S(2)}, u32[]{:S(2)}) collective-permute-start(bf16[192,512]{1,0:T(8,128)(2,1)S(1)} %order.1.mine_ref), channel_id=1, source_target_pairs={{0,1},{1,0},{2,3},{3,2},{4,5},{5,4},{6,7},{7,6},{8,9},{9,8},{10,11... | collective-permute-start | bytes 589832 | tf_op jit(solution)/shard_map/gather_picks/ppermute | solution.py:477
  41.3 1.1 %collective-permute-done.10.other_ref = bf16[192,512]{1,0:T(8,128)(2,1)S(1)} collective-permute-done((bf16[192,512]{1,0:T(8,128)(2,1)S(1)}, bf16[192,512]{1,0:T(8,128)(2,1)S(1)}, u32[]{:S(2)}, u32[]{:S(2)}) %collective-permute-start.10) | collective-permute-done | bytes 196640 | tf_op jit(solution)/shard_map/gather_picks/ppermute | solution.py:477
  42.4 1.0 %products_far.1 = (s16[200,640]{1,0:T(8,128)(2,1)S(1)}, s16[200,512]{1,0:T(8,128)(2,1)S(1)}, f32[8,128]{1,0:T(8,128)S(1)}) custom-call(bf16[1152,512]{1,0:T(8,128)(2,1)S(1)} %get-tuple-element.49.e_ref, bf16[1152,512]{1,0:T(8,128)(2,1)S(1)} %get-tuple-element.50.r_ref, f32[8,1152]{1,0:T(8,128)S(1)} %get-tuple-element.51.norm_ref, ...), custom_call_target="tpu_custom_call" | custom-call | flops 1000000 | bytes 65536 | tf_op jit(solution)/shard_map/sum_products/products_far/pallas_call | solution.py:375
  43.4 1.3 %collective-permute-start.12 = (s16[200,640]{1,0:T(8,128)(2,1)S(1)}, s16[200,640]{1,0:T(8,128)(2,1)S(1)}, u32[]{:S(2)}, u32[]{:S(2)}) collective-permute-start(s16[200,640]{1,0:T(8,128)(2,1)S(1)} %get-tuple-element.59), channel_id=1, source_target_pairs={{0,2},{1,3},{2,4},{3,5},{4,6},{5,7},{6,0},{7,1},{8,10},{9,11},{10,... | collective-permute-start | bytes 768008 | tf_op jit(solution)/shard_map/sum_products/ppermute | solution.py:481
  44.7 1.5 %collective-permute-start.11 = (s16[200,512]{1,0:T(8,128)(2,1)S(1)}, s16[200,512]{1,0:T(8,128)(2,1)S(1)}, u32[]{:S(2)}, u32[]{:S(2)}) collective-permute-start(s16[200,512]{1,0:T(8,128)(2,1)S(1)} %get-tuple-element.56), channel_id=1, source_target_pairs={{0,6},{1,7},{2,0},{3,1},{4,2},{5,3},{6,4},{7,5},{8,14},{9,15},{10,... | collective-permute-start | bytes 614408 | tf_op jit(solution)/shard_map/sum_products/ppermute | solution.py:482
  46.2 0.3 gram.1
  46.5 1.5 %collective-permute-start.13 = (f32[256,128]{1,0:T(8,128)S(1)}, f32[256,128]{1,0:T(8,128)S(1)}, u32[]{:S(2)}, u32[]{:S(2)}) collective-permute-start(f32[256,128]{1,0:T(8,128)S(1)} %get-tuple-element.63), channel_id=1, source_target_pairs={{0,2},{1,7},{2,4},{3,1},{4,6},{5,3},{6,0},{7,5},{8,10},{9,15},{10,... | collective-permute-start | bytes 393224 | tf_op jit(solution)/shard_map/sum_products/ppermute | solution.py:484
  48.0 0.5 collective-permute-start.14
  48.5 1.5 %products_both.1 = (f32[192,1152]{1,0:T(8,128)S(1)}, f32[192,1152]{1,0:T(8,128)S(1)}, f32[256,128]{1,0:T(8,128)S(1)}) custom-call(bf16[1152,512]{1,0:T(8,128)(2,1)S(1)} %get-tuple-element.45.e_next, bf16[1152,512]{1,0:T(8,128)(2,1)S(1)} %get-tuple-element.46.r_next, bf16[1152,512]{1,0:T(8,128)(2,1)S(1)} %get-tuple-element.47.e_last, ...), custom_call_target="tpu_custom_call" | custom-call | flops 1000000 | bytes 65536 | tf_op jit(solution)/shard_map/sum_products/products_both/pallas_call | solution.py:381
  50.0 2.1 %collective-permute-done.12.got_ref = s16[200,640]{1,0:T(8,128)(2,1)S(1)} collective-permute-done((s16[200,640]{1,0:T(8,128)(2,1)S(1)}, s16[200,640]{1,0:T(8,128)(2,1)S(1)}, u32[]{:S(2)}, u32[]{:S(2)}) %collective-permute-start.12) | collective-permute-done | bytes 256032 | tf_op jit(solution)/shard_map/sum_products/ppermute | solution.py:481
  52.1 0.3 near_0.1
  52.4 0.0 copy-start.2
  52.4 0.0 collective-permute-done.11.got_ref
  52.5 0.3 near_640.1
  52.8 1.3 %collective-permute-start.16 = (s16[200,1152]{1,0:T(8,128)(2,1)S(1)}, s16[200,1152]{1,0:T(8,128)(2,1)S(1)}, u32[]{:S(2)}, u32[]{:S(2)}) collective-permute-start(s16[200,1152]{1,0:T(8,128)(2,1)S(1)} %get-tuple-element.68), channel_id=1, source_target_pairs={{0,6},{1,7},{2,0},{3,1},{4,2},{5,3},{6,4},{7,5},{8,14},{9,15},{10,... | collective-permute-start | bytes 1382408 | tf_op jit(solution)/shard_map/sum_products/ppermute | solution.py:490
  54.1 0.2 collective-permute-start.15
  54.3 0.0 collective-permute-done.14
  54.3 0.0 collective-permute-done.13
  54.4 0.0 copy-start
  54.4 2.9 %collective-permute-start.17 = (f32[256,128]{1,0:T(8,128)S(1)}, f32[256,128]{1,0:T(8,128)S(1)}, u32[]{:S(2)}, u32[]{:S(2)}) collective-permute-start(f32[256,128]{1,0:T(8,128)S(1)} %pad_maximum_fusion.through_ref), channel_id=1, source_target_pairs={{0,1},{1,0},{2,3},{3,2},{4,5},{5,4},{6,7},{7,6},{8,9},{9,8},{10,11... | collective-permute-start | bytes 393224 | tf_op jit(solution)/shard_map/sum_gram/ppermute | solution.py:493
  57.3 0.0 copy-done.2
  57.3 3.2 %products_own.1 = (f32[192,1152]{1,0:T(8,128)S(1)}, f32[8,1152]{1,0:T(8,128)S(1)}, f32[256,128]{1,0:T(8,128)S(1)}) custom-call(s32[3,64]{1,0:T(4,128)S(1)} %copy-done.2, bf16[9216,512]{1,0:T(8,128)(2,1)} %e_ref.9, bf16[9216,512]{1,0:T(8,128)(2,1)} %collective-permute-done.r_ref, bf16[192,512]{1,0:T(8,128)(2,1)S(1)} %order.1.mine_ref, ...), custom_call_target="tpu_custom_call" | custom-call | flops 1000000 | bytes 65536 | tf_op jit(solution)/shard_map/products_own/pallas_call | solution.py:396
  60.4 0.0 collective-permute-done.17.swapped_ref
  60.4 6.6 %factor.1 = (bf16[192,192]{1,0:T(8,128)(2,1)S(1)}, bf16[192,192]{1,0:T(8,128)(2,1)S(1)}) custom-call(f32[256,128]{1,0:T(8,128)S(1)} %get-tuple-element.69.sum_ref, f32[256,128]{1,0:T(8,128)S(1)} %collective-permute-done.17.swapped_ref), custom_call_target="tpu_custom_call" | custom-call | flops 1000000 | bytes 65536 | tf_op jit(solution)/shard_map/factor/pallas_call | solution.py:260
  67.1 0.0 collective-permute-done.16.g2
  67.1 0.0 collective-permute-done.15.g1
  67.1 0.0 copy-done
  67.1 2.1 %finish.1 = (f32[192,1152]{1,0:T(8,128)}, f32[1152]{0:T(1024)}) custom-call(f32[1152]{0:T(1024)S(1)} %copy-done, f32[192,1152]{1,0:T(8,128)S(1)} %get-tuple-element.65.own_ref, f32[8,1152]{1,0:T(8,128)S(1)} %get-tuple-element.66.norm_ref, s16[200,1152]{1,0:T(8,128)(2,1)S(1)} %collective-permute-done.15.g1, s16[200,1152]{1,0:T(8,128)(2,1)S(1)} %collective-permute-done.16.g2, ...), custom_call_target="tpu_custom_call" | custom-call | flops 509607936 | bytes 4194304 | tf_op jit(solution)/shard_map/finish/pallas_call | solution.py:427
  (7 shorter events, 0.1 us)
Async XLA Ops:
  0.6 20.5 %collective-permute-start = (bf16[9216,512]{1,0:T(8,128)(2,1)}, bf16[9216,512]{1,0:T(8,128)(2,1)}, u32[]{:S(2)}, u32[]{:S(2)}) collective-permute-start(bf16[9216,512]{1,0:T(8,128)(2,1)} %e_ref.9), channel_id=1, source_target_pairs={{0,1},{1,0},{2,3},{3,2},{4,5},{5,4},{6,7},{7,6},{8,9},{9,8},{10,11... | collective-permute-start | bytes 28311560 | tf_op jit(solution)/shard_map/swap_rows/ppermute | solution.py:458
  4.0 0.7 copy-start.1
  7.6 3.9 %collective-permute-start.1 = (bf16[48,512]{1,0:T(8,128)(2,1)S(1)}, bf16[48,512]{1,0:T(8,128)(2,1)S(1)}, u32[]{:S(2)}, u32[]{:S(2)}) collective-permute-start(bf16[48,512]{1,0:T(8,128)(2,1)S(1)} %get-tuple-element.39), channel_id=1, source_target_pairs={{0,8},{8,0},{16,24},{24,16},{32,40},{40,32},{48,56},{56,48},{64,72... | collective-permute-start | bytes 147464 | tf_op jit(solution)/shard_map/gather_picks/ppermute | solution.py:464
  8.0 5.6 %collective-permute-start.2 = (bf16[48,512]{1,0:T(8,128)(2,1)S(1)}, bf16[48,512]{1,0:T(8,128)(2,1)S(1)}, u32[]{:S(2)}, u32[]{:S(2)}) collective-permute-start(bf16[48,512]{1,0:T(8,128)(2,1)S(1)} %get-tuple-element.40), channel_id=1, source_target_pairs={{0,16},{8,24},{16,0},{24,8},{32,48},{40,56},{48,32},{56,40},{64,80... | collective-permute-start | bytes 147464 | tf_op jit(solution)/shard_map/gather_picks/ppermute | solution.py:464
  10.6 4.2 %collective-permute-start.3 = (bf16[48,512]{1,0:T(8,128)(2,1)S(1)}, bf16[48,512]{1,0:T(8,128)(2,1)S(1)}, u32[]{:S(2)}, u32[]{:S(2)}) collective-permute-start(bf16[48,512]{1,0:T(8,128)(2,1)S(1)} %get-tuple-element.41), channel_id=1, source_target_pairs={{0,24},{8,16},{16,8},{24,0},{32,56},{40,48},{48,40},{56,32},{64,88... | collective-permute-start | bytes 147464 | tf_op jit(solution)/shard_map/gather_picks/ppermute | solution.py:464
  14.8 3.2 %collective-permute-start.4 = (bf16[48,512]{1,0:T(8,128)(2,1)S(1)}, bf16[48,512]{1,0:T(8,128)(2,1)S(1)}, u32[]{:S(2)}, u32[]{:S(2)}) collective-permute-start(bf16[48,512]{1,0:T(8,128)(2,1)S(1)} %add_add_fusion), channel_id=1, source_target_pairs={{0,32},{8,40},{16,48},{24,56},{32,0},{40,8},{48,16},{56,24},{64,96... | collective-permute-start | bytes 147464 | tf_op jit(solution)/shard_map/gather_picks/ppermute | solution.py:466
  18.1 5.3 %collective-permute-start.5 = (bf16[48,512]{1,0:T(8,128)(2,1)S(1)}, bf16[48,512]{1,0:T(8,128)(2,1)S(1)}, u32[]{:S(2)}, u32[]{:S(2)}) collective-permute-start(bf16[48,512]{1,0:T(8,128)(2,1)S(1)} %add.30.through_ref), channel_id=1, source_target_pairs={{0,64},{8,72},{16,80},{24,88},{32,96},{40,104},{48,112},{56,120},{... | collective-permute-start | bytes 147464 | tf_op jit(solution)/shard_map/gather_picks/ppermute | solution.py:467
  23.4 6.7 %collective-permute-start.6 = (bf16[48,512]{1,0:T(8,128)(2,1)S(1)}, bf16[48,512]{1,0:T(8,128)(2,1)S(1)}, u32[]{:S(2)}, u32[]{:S(2)}) collective-permute-start(bf16[48,512]{1,0:T(8,128)(2,1)S(1)} %add.31.through_ref), channel_id=1, source_target_pairs={{0,192},{8,200},{16,208},{24,216},{32,224},{40,232},{48,240},{56,2... | collective-permute-start | bytes 147464 | tf_op jit(solution)/shard_map/gather_picks/ppermute | solution.py:470
  30.1 5.5 %collective-permute-start.9 = (bf16[48,512]{1,0:T(8,128)(2,1)S(1)}, bf16[48,512]{1,0:T(8,128)(2,1)S(1)}, u32[]{:S(2)}, u32[]{:S(2)}) collective-permute-start(bf16[48,512]{1,0:T(8,128)(2,1)S(1)} %add.32.through_ref), channel_id=1, source_target_pairs={{0,24},{8,16},{16,8},{24,0},{32,56},{40,48},{48,40},{56,32},{64,88... | collective-permute-start | bytes 147464 | tf_op jit(solution)/shard_map/gather_picks/ppermute | solution.py:473
  30.7 4.9 %collective-permute-start.8 = (bf16[48,512]{1,0:T(8,128)(2,1)S(1)}, bf16[48,512]{1,0:T(8,128)(2,1)S(1)}, u32[]{:S(2)}, u32[]{:S(2)}) collective-permute-start(bf16[48,512]{1,0:T(8,128)(2,1)S(1)} %add.32.through_ref), channel_id=1, source_target_pairs={{0,16},{8,24},{16,0},{24,8},{32,48},{40,56},{48,32},{56,40},{64,80... | collective-permute-start | bytes 147464 | tf_op jit(solution)/shard_map/gather_picks/ppermute | solution.py:473
  31.6 4.0 %collective-permute-start.7 = (bf16[48,512]{1,0:T(8,128)(2,1)S(1)}, bf16[48,512]{1,0:T(8,128)(2,1)S(1)}, u32[]{:S(2)}, u32[]{:S(2)}) collective-permute-start(bf16[48,512]{1,0:T(8,128)(2,1)S(1)} %add.32.through_ref), channel_id=1, source_target_pairs={{0,8},{8,0},{16,24},{24,16},{32,40},{40,32},{48,56},{56,48},{64,72... | collective-permute-start | bytes 147464 | tf_op jit(solution)/shard_map/gather_picks/ppermute | solution.py:473
  35.7 6.7 %collective-permute-start.10 = (bf16[192,512]{1,0:T(8,128)(2,1)S(1)}, bf16[192,512]{1,0:T(8,128)(2,1)S(1)}, u32[]{:S(2)}, u32[]{:S(2)}) collective-permute-start(bf16[192,512]{1,0:T(8,128)(2,1)S(1)} %order.1.mine_ref), channel_id=1, source_target_pairs={{0,1},{1,0},{2,3},{3,2},{4,5},{5,4},{6,7},{7,6},{8,9},{9,8},{10,11... | collective-permute-start | bytes 589832 | tf_op jit(solution)/shard_map/gather_picks/ppermute | solution.py:477
  43.4 8.7 %collective-permute-start.12 = (s16[200,640]{1,0:T(8,128)(2,1)S(1)}, s16[200,640]{1,0:T(8,128)(2,1)S(1)}, u32[]{:S(2)}, u32[]{:S(2)}) collective-permute-start(s16[200,640]{1,0:T(8,128)(2,1)S(1)} %get-tuple-element.59), channel_id=1, source_target_pairs={{0,2},{1,3},{2,4},{3,5},{4,6},{5,7},{6,0},{7,1},{8,10},{9,11},{10,... | collective-permute-start | bytes 768008 | tf_op jit(solution)/shard_map/sum_products/ppermute | solution.py:481
  44.7 7.7 %collective-permute-start.11 = (s16[200,512]{1,0:T(8,128)(2,1)S(1)}, s16[200,512]{1,0:T(8,128)(2,1)S(1)}, u32[]{:S(2)}, u32[]{:S(2)}) collective-permute-start(s16[200,512]{1,0:T(8,128)(2,1)S(1)} %get-tuple-element.56), channel_id=1, source_target_pairs={{0,6},{1,7},{2,0},{3,1},{4,2},{5,3},{6,4},{7,5},{8,14},{9,15},{10,... | collective-permute-start | bytes 614408 | tf_op jit(solution)/shard_map/sum_products/ppermute | solution.py:482
  46.5 7.8 %collective-permute-start.13 = (f32[256,128]{1,0:T(8,128)S(1)}, f32[256,128]{1,0:T(8,128)S(1)}, u32[]{:S(2)}, u32[]{:S(2)}) collective-permute-start(f32[256,128]{1,0:T(8,128)S(1)} %get-tuple-element.63), channel_id=1, source_target_pairs={{0,2},{1,7},{2,4},{3,1},{4,6},{5,3},{6,0},{7,5},{8,10},{9,15},{10,... | collective-permute-start | bytes 393224 | tf_op jit(solution)/shard_map/sum_products/ppermute | solution.py:484
  48.0 6.3 %collective-permute-start.14 = (f32[128,128]{1,0:T(8,128)S(1)}, f32[128,128]{1,0:T(8,128)S(1)}, u32[]{:S(2)}, u32[]{:S(2)}) collective-permute-start(f32[128,128]{1,0:T(8,128)S(1)} %get-tuple-element.64), channel_id=1, source_target_pairs={{0,4},{1,5},{2,6},{3,7},{4,0},{5,1},{6,2},{7,3},{8,12},{9,13},{10,... | collective-permute-start | bytes 196616 | tf_op jit(solution)/shard_map/sum_products/ppermute | solution.py:485
  52.4 4.8 %copy-start.2 = (s32[3,64]{1,0:T(4,128)S(1)}, s32[3,64]{1,0:T(4,128)}, u32[]{:S(2)}) copy-start(s32[3,64]{1,0:T(4,128)} %picks_ref.3) | copy-start | bytes 2308
  52.8 14.3 %collective-permute-start.16 = (s16[200,1152]{1,0:T(8,128)(2,1)S(1)}, s16[200,1152]{1,0:T(8,128)(2,1)S(1)}, u32[]{:S(2)}, u32[]{:S(2)}) collective-permute-start(s16[200,1152]{1,0:T(8,128)(2,1)S(1)} %get-tuple-element.68), channel_id=1, source_target_pairs={{0,6},{1,7},{2,0},{3,1},{4,2},{5,3},{6,4},{7,5},{8,14},{9,15},{10,... | collective-permute-start | bytes 1382408 | tf_op jit(solution)/shard_map/sum_products/ppermute | solution.py:490
  54.1 13.0 %collective-permute-start.15 = (s16[200,1152]{1,0:T(8,128)(2,1)S(1)}, s16[200,1152]{1,0:T(8,128)(2,1)S(1)}, u32[]{:S(2)}, u32[]{:S(2)}) collective-permute-start(s16[200,1152]{1,0:T(8,128)(2,1)S(1)} %get-tuple-element.67), channel_id=1, source_target_pairs={{0,2},{1,3},{2,4},{3,5},{4,6},{5,7},{6,0},{7,1},{8,10},{9,11},{10,... | collective-permute-start | bytes 1382408 | tf_op jit(solution)/shard_map/sum_products/ppermute | solution.py:488
  54.4 12.7 %copy-start = (f32[1152]{0:T(1024)S(1)}, f32[1152]{0:T(1024)}, u32[]{:S(2)}) copy-start(f32[1152]{0:T(1024)} %quality_ref.1) | copy-start | bytes 13828
  54.4 6.1 %collective-permute-start.17 = (f32[256,128]{1,0:T(8,128)S(1)}, f32[256,128]{1,0:T(8,128)S(1)}, u32[]{:S(2)}, u32[]{:S(2)}) collective-permute-start(f32[256,128]{1,0:T(8,128)S(1)} %pad_maximum_fusion.through_ref), channel_id=1, source_target_pairs={{0,1},{1,0},{2,3},{3,2},{4,5},{5,4},{6,7},{7,6},{8,9},{9,8},{10,11... | collective-permute-start | bytes 393224 | tf_op jit(solution)/shard_map/sum_gram/ppermute | solution.py:493

commit v4 on v3

--- a/solution.py
+++ b/solution.py
@@ -460,14 +460,14 @@
     with jax.named_scope("gather_picks"):
         parts = local_picks(picked_rows, embeddings)
         mine = parts[0]
-        for k in range(1, Y):
+        for k in (3, 2, 1):
             mine = mine + lax.ppermute(parts[k], "rows", along_y(k))
         staged = {}
         mine = mine + lax.ppermute(mine, "rows", along_z(lambda z: z ^ 1))
         arrived = lax.ppermute(mine, "rows", along_z(lambda z: z ^ 2))
         *staged[2], mine = stage(2, embeddings, received, mine)
         mine = mine + arrived
-        arrived = lax.ppermute(mine, "rows", along_z(lambda z: z ^ 6))
+        arrived = lax.ppermute(mine, "rows", along_z(lambda z: z ^ 7))
         *staged[1], mine = stage(1, embeddings, received, mine)
         mine = mine + arrived
         groups = [mine] + [lax.ppermute(mine, "rows", along_y(k)) for k in range(1, Y)]

time: 69.7 us -> 68.9 us (0.989)
  starting transfers between devices: 34.9 us -> 33.7 us
  Pallas kernels: 24.8 us -> 25.5 us
    pallas_call x1, Pallas kernels: 2.96 us -> 3.67 us  [local_picks(): pl.pallas_call(pick_kernel, in_specs=[pl.BlockSpec(memory_space=pltpu.SME...]
  transfers between devices with their start and end apart: 18 -> 18, of which waited for: 5 -> 7; matrix products, arithmetic and copies ran while one was open for 0% -> 0% of each run, Pallas kernels for 31% -> 32%
where the time goes in v4:
time: 68.9 us; the launch traced here: 69 us
  starting transfers between devices  33.7 us (49%)
  Pallas kernels  25.5 us (37%)
  waiting for transfers between devices  8.08 us (12%)
  between operations  0.99 us (1%)
  local copies, waits for them, and re-layouts  0.69 us (1%)
    pallas_call x1, Pallas kernels, factor_inverse(): pl.pallas_call(factor_kernel, in_specs=[VMEM] * 2, out_specs=[VMEM] * 2,...  6.62 us
    pallas_call x3, Pallas kernels, stage(): pl.pallas_call(functools.partial(stage_kernel, hop), in_specs=[ANY, ANY,...  6.43 us
    ppermute x1, starting transfers between devices, per_device(): pick_other = lax.ppermute(pick_mine, 'dim', swap)  5.5 us
    ppermute x1, starting transfers between devices, per_device(): arrived = lax.ppermute(mine, 'rows', along_z(lambda z: z ^ 7))  4.63 us
    pallas_call x1, Pallas kernels, local_picks(): pl.pallas_call(pick_kernel, in_specs=[pl.BlockSpec(memory_space=pltpu.SME...  3.67 us
    ppermute x3, starting transfers between devices, per_device(): mine = mine + lax.ppermute(parts[k], 'rows', along_y(k))  3.34 us
    ppermute x3, starting transfers between devices, per_device(): lax.ppermute(mine, 'rows', along_y(k))  3.34 us
    ppermute x1, starting transfers between devices, per_device(): received = lax.ppermute(embeddings, 'dim', swap)  3.33 us
  transfers between devices with their start and end apart: 18, of which 7 were waited for; matrix products, arithmetic and copies ran while one was open for 0% of the time, Pallas kernels for 32%

profile of v4, /device:TPU:1, one launch (start us, length us, event | category | flops | bytes accessed | tf_op | source)
XLA Modules:
  0.0 69.0 jit_solution(11039512817617016443)
XLA Ops:
  0.6 3.3 %collective-permute-start = (bf16[9216,512]{1,0:T(8,128)(2,1)}, bf16[9216,512]{1,0:T(8,128)(2,1)}, u32[]{:S(2)}, u32[]{:S(2)}) collective-permute-start(bf16[9216,512]{1,0:T(8,128)(2,1)} %e_ref.9), channel_id=1, source_target_pairs={{0,1},{1,0},{2,3},{3,2},{4,5},{5,4},{6,7},{7,6},{8,9},{9,8},{10,11... | collective-permute-start | bytes 28311560 | tf_op jit(solution)/shard_map/swap_rows/ppermute | solution.py:458
  4.0 0.0 copy-start.1
  4.0 0.7 copy-done.1
  4.6 3.7 %local_picks.1 = (bf16[48,512]{1,0:T(8,128)(2,1)S(1)}, bf16[48,512]{1,0:T(8,128)(2,1)S(1)}, bf16[48,512]{1,0:T(8,128)(2,1)S(1)}, bf16[48,512]{1,0:T(8,128)(2,1)S(1)}) custom-call(s32[3,64]{1,0:T(4,128)S(1)} %copy-done.1, bf16[9216,512]{1,0:T(8,128)(2,1)} %e_ref.9), custom_call_target="tpu_custom_call" | custom-call | bytes 10485760 | tf_op jit(solution)/shard_map/gather_picks/local_picks/pallas_call | solution.py:83
  8.3 1.2 %collective-permute-start.1 = (bf16[48,512]{1,0:T(8,128)(2,1)S(1)}, bf16[48,512]{1,0:T(8,128)(2,1)S(1)}, u32[]{:S(2)}, u32[]{:S(2)}) collective-permute-start(bf16[48,512]{1,0:T(8,128)(2,1)S(1)} %get-tuple-element.39), channel_id=1, source_target_pairs={{0,24},{8,16},{16,8},{24,0},{32,56},{40,48},{48,40},{56,32},{64,88... | collective-permute-start | bytes 147464 | tf_op jit(solution)/shard_map/gather_picks/ppermute | solution.py:464
  9.5 0.3 collective-permute-start.2
  9.8 1.8 %collective-permute-start.3 = (bf16[48,512]{1,0:T(8,128)(2,1)S(1)}, bf16[48,512]{1,0:T(8,128)(2,1)S(1)}, u32[]{:S(2)}, u32[]{:S(2)}) collective-permute-start(bf16[48,512]{1,0:T(8,128)(2,1)S(1)} %get-tuple-element.41), channel_id=1, source_target_pairs={{0,8},{8,0},{16,24},{24,16},{32,40},{40,32},{48,56},{56,48},{64,72... | collective-permute-start | bytes 147464 | tf_op jit(solution)/shard_map/gather_picks/ppermute | solution.py:464
  11.7 1.3 %collective-permute-done.1 = bf16[48,512]{1,0:T(8,128)(2,1)S(1)} collective-permute-done((bf16[48,512]{1,0:T(8,128)(2,1)S(1)}, bf16[48,512]{1,0:T(8,128)(2,1)S(1)}, u32[]{:S(2)}, u32[]{:S(2)}) %collective-permute-start.1) | collective-permute-done | bytes 49184 | tf_op jit(solution)/shard_map/gather_picks/ppermute | solution.py:464
  13.0 1.0 %collective-permute-done.2 = bf16[48,512]{1,0:T(8,128)(2,1)S(1)} collective-permute-done((bf16[48,512]{1,0:T(8,128)(2,1)S(1)}, bf16[48,512]{1,0:T(8,128)(2,1)S(1)}, u32[]{:S(2)}, u32[]{:S(2)}) %collective-permute-start.2) | collective-permute-done | bytes 49184 | tf_op jit(solution)/shard_map/gather_picks/ppermute | solution.py:464
  13.9 0.3 collective-permute-done.3
  14.3 1.3 %collective-permute-start.4 = (bf16[48,512]{1,0:T(8,128)(2,1)S(1)}, bf16[48,512]{1,0:T(8,128)(2,1)S(1)}, u32[]{:S(2)}, u32[]{:S(2)}) collective-permute-start(bf16[48,512]{1,0:T(8,128)(2,1)S(1)} %add_add_fusion), channel_id=1, source_target_pairs={{0,32},{8,40},{16,48},{24,56},{32,0},{40,8},{48,16},{56,24},{64,96... | collective-permute-start | bytes 147464 | tf_op jit(solution)/shard_map/gather_picks/ppermute | solution.py:466
  15.6 1.7 %collective-permute-done.4 = bf16[48,512]{1,0:T(8,128)(2,1)S(1)} collective-permute-done((bf16[48,512]{1,0:T(8,128)(2,1)S(1)}, bf16[48,512]{1,0:T(8,128)(2,1)S(1)}, u32[]{:S(2)}, u32[]{:S(2)}) %collective-permute-start.4) | collective-permute-done | bytes 49184 | tf_op jit(solution)/shard_map/gather_picks/ppermute | solution.py:466
  17.3 3.0 %collective-permute-start.5 = (bf16[48,512]{1,0:T(8,128)(2,1)S(1)}, bf16[48,512]{1,0:T(8,128)(2,1)S(1)}, u32[]{:S(2)}, u32[]{:S(2)}) collective-permute-start(bf16[48,512]{1,0:T(8,128)(2,1)S(1)} %add.30.through_ref), channel_id=1, source_target_pairs={{0,64},{8,72},{16,80},{24,88},{32,96},{40,104},{48,112},{56,120},{... | collective-permute-start | bytes 147464 | tf_op jit(solution)/shard_map/gather_picks/ppermute | solution.py:467
  20.3 0.0 collective-permute-done.r_ref
  20.3 2.1 %stage_2.1 = (bf16[1152,512]{1,0:T(8,128)(2,1)S(1)}, bf16[1152,512]{1,0:T(8,128)(2,1)S(1)}, f32[8,1152]{1,0:T(8,128)S(1)}, bf16[48,512]{1,0:T(8,128)(2,1)S(1)}) custom-call(bf16[9216,512]{1,0:T(8,128)(2,1)} %e_ref.9, bf16[9216,512]{1,0:T(8,128)(2,1)} %collective-permute-done.r_ref, bf16[48,512]{1,0:T(8,128)(2,1)S(1)} %add.30.through_ref), custom_call_target="tpu_custom_call" | custom-call | bytes 2359296 | tf_op jit(solution)/shard_map/gather_picks/stage_2/pallas_call | solution.py:146
  22.5 0.0 collective-permute-done.5
  22.5 4.6 %collective-permute-start.6 = (bf16[48,512]{1,0:T(8,128)(2,1)S(1)}, bf16[48,512]{1,0:T(8,128)(2,1)S(1)}, u32[]{:S(2)}, u32[]{:S(2)}) collective-permute-start(bf16[48,512]{1,0:T(8,128)(2,1)S(1)} %add.31.through_ref), channel_id=1, source_target_pairs={{0,224},{8,232},{16,240},{24,248},{32,192},{40,200},{48,208},{56,2... | collective-permute-start | bytes 147464 | tf_op jit(solution)/shard_map/gather_picks/ppermute | solution.py:470
  27.1 2.1 %stage_1.1 = (bf16[1152,512]{1,0:T(8,128)(2,1)S(1)}, bf16[1152,512]{1,0:T(8,128)(2,1)S(1)}, f32[8,1152]{1,0:T(8,128)S(1)}, bf16[48,512]{1,0:T(8,128)(2,1)S(1)}) custom-call(bf16[9216,512]{1,0:T(8,128)(2,1)} %e_ref.9, bf16[9216,512]{1,0:T(8,128)(2,1)} %collective-permute-done.r_ref, bf16[48,512]{1,0:T(8,128)(2,1)S(1)} %add.31.through_ref), custom_call_target="tpu_custom_call" | custom-call | bytes 2359296 | tf_op jit(solution)/shard_map/gather_picks/stage_1/pallas_call | solution.py:146
  29.3 0.0 collective-permute-done.6
  29.3 1.7 %collective-permute-start.9 = (bf16[48,512]{1,0:T(8,128)(2,1)S(1)}, bf16[48,512]{1,0:T(8,128)(2,1)S(1)}, u32[]{:S(2)}, u32[]{:S(2)}) collective-permute-start(bf16[48,512]{1,0:T(8,128)(2,1)S(1)} %add.32.through_ref), channel_id=1, source_target_pairs={{0,24},{8,16},{16,8},{24,0},{32,56},{40,48},{48,40},{56,32},{64,88... | collective-permute-start | bytes 147464 | tf_op jit(solution)/shard_map/gather_picks/ppermute | solution.py:473
  31.0 0.0 collective-permute-start.8
  31.0 1.7 %collective-permute-start.7 = (bf16[48,512]{1,0:T(8,128)(2,1)S(1)}, bf16[48,512]{1,0:T(8,128)(2,1)S(1)}, u32[]{:S(2)}, u32[]{:S(2)}) collective-permute-start(bf16[48,512]{1,0:T(8,128)(2,1)S(1)} %add.32.through_ref), channel_id=1, source_target_pairs={{0,8},{8,0},{16,24},{24,16},{32,40},{40,32},{48,56},{56,48},{64,72... | collective-permute-start | bytes 147464 | tf_op jit(solution)/shard_map/gather_picks/ppermute | solution.py:473
  32.7 2.1 %stage_3.1 = (bf16[1152,512]{1,0:T(8,128)(2,1)S(1)}, bf16[1152,512]{1,0:T(8,128)(2,1)S(1)}, f32[8,1152]{1,0:T(8,128)S(1)}, bf16[48,512]{1,0:T(8,128)(2,1)S(1)}) custom-call(bf16[9216,512]{1,0:T(8,128)(2,1)} %e_ref.9, bf16[9216,512]{1,0:T(8,128)(2,1)} %collective-permute-done.r_ref, bf16[48,512]{1,0:T(8,128)(2,1)S(1)} %add.32.through_ref), custom_call_target="tpu_custom_call" | custom-call | bytes 2359296 | tf_op jit(solution)/shard_map/gather_picks/stage_3/pallas_call | solution.py:146
  34.8 0.0 collective-permute-done.9.s3
  34.8 0.6 collective-permute-done.8.s2
  35.4 0.0 collective-permute-done.7.s1
  35.5 5.5 %collective-permute-start.10 = (bf16[192,512]{1,0:T(8,128)(2,1)S(1)}, bf16[192,512]{1,0:T(8,128)(2,1)S(1)}, u32[]{:S(2)}, u32[]{:S(2)}) collective-permute-start(bf16[192,512]{1,0:T(8,128)(2,1)S(1)} %order.1.mine_ref), channel_id=1, source_target_pairs={{0,1},{1,0},{2,3},{3,2},{4,5},{5,4},{6,7},{7,6},{8,9},{9,8},{10,11... | collective-permute-start | bytes 589832 | tf_op jit(solution)/shard_map/gather_picks/ppermute | solution.py:477
  41.0 1.1 %collective-permute-done.10.other_ref = bf16[192,512]{1,0:T(8,128)(2,1)S(1)} collective-permute-done((bf16[192,512]{1,0:T(8,128)(2,1)S(1)}, bf16[192,512]{1,0:T(8,128)(2,1)S(1)}, u32[]{:S(2)}, u32[]{:S(2)}) %collective-permute-start.10) | collective-permute-done | bytes 196640 | tf_op jit(solution)/shard_map/gather_picks/ppermute | solution.py:477
  42.0 1.0 %products_far.1 = (s16[200,640]{1,0:T(8,128)(2,1)S(1)}, s16[200,512]{1,0:T(8,128)(2,1)S(1)}, f32[8,128]{1,0:T(8,128)S(1)}) custom-call(bf16[1152,512]{1,0:T(8,128)(2,1)S(1)} %get-tuple-element.49.e_ref, bf16[1152,512]{1,0:T(8,128)(2,1)S(1)} %get-tuple-element.50.r_ref, f32[8,1152]{1,0:T(8,128)S(1)} %get-tuple-element.51.norm_ref, ...), custom_call_target="tpu_custom_call" | custom-call | flops 1000000 | bytes 65536 | tf_op jit(solution)/shard_map/sum_products/products_far/pallas_call | solution.py:375
  43.1 1.3 %collective-permute-start.12 = (s16[200,640]{1,0:T(8,128)(2,1)S(1)}, s16[200,640]{1,0:T(8,128)(2,1)S(1)}, u32[]{:S(2)}, u32[]{:S(2)}) collective-permute-start(s16[200,640]{1,0:T(8,128)(2,1)S(1)} %get-tuple-element.59), channel_id=1, source_target_pairs={{0,2},{1,3},{2,4},{3,5},{4,6},{5,7},{6,0},{7,1},{8,10},{9,11},{10,... | collective-permute-start | bytes 768008 | tf_op jit(solution)/shard_map/sum_products/ppermute | solution.py:481
  44.4 1.5 %collective-permute-start.11 = (s16[200,512]{1,0:T(8,128)(2,1)S(1)}, s16[200,512]{1,0:T(8,128)(2,1)S(1)}, u32[]{:S(2)}, u32[]{:S(2)}) collective-permute-start(s16[200,512]{1,0:T(8,128)(2,1)S(1)} %get-tuple-element.56), channel_id=1, source_target_pairs={{0,6},{1,7},{2,0},{3,1},{4,2},{5,3},{6,4},{7,5},{8,14},{9,15},{10,... | collective-permute-start | bytes 614408 | tf_op jit(solution)/shard_map/sum_products/ppermute | solution.py:482
  45.8 0.3 gram.1
  46.1 1.5 %collective-permute-start.13 = (f32[256,128]{1,0:T(8,128)S(1)}, f32[256,128]{1,0:T(8,128)S(1)}, u32[]{:S(2)}, u32[]{:S(2)}) collective-permute-start(f32[256,128]{1,0:T(8,128)S(1)} %get-tuple-element.63), channel_id=1, source_target_pairs={{0,2},{1,7},{2,4},{3,1},{4,6},{5,3},{6,0},{7,5},{8,10},{9,15},{10,... | collective-permute-start | bytes 393224 | tf_op jit(solution)/shard_map/sum_products/ppermute | solution.py:484
  47.6 0.5 collective-permute-start.14
  48.2 1.5 %products_both.1 = (f32[192,1152]{1,0:T(8,128)S(1)}, f32[192,1152]{1,0:T(8,128)S(1)}, f32[256,128]{1,0:T(8,128)S(1)}) custom-call(bf16[1152,512]{1,0:T(8,128)(2,1)S(1)} %get-tuple-element.45.e_next, bf16[1152,512]{1,0:T(8,128)(2,1)S(1)} %get-tuple-element.46.r_next, bf16[1152,512]{1,0:T(8,128)(2,1)S(1)} %get-tuple-element.47.e_last, ...), custom_call_target="tpu_custom_call" | custom-call | flops 1000000 | bytes 65536 | tf_op jit(solution)/shard_map/sum_products/products_both/pallas_call | solution.py:381
  49.7 2.1 %collective-permute-done.12.got_ref = s16[200,640]{1,0:T(8,128)(2,1)S(1)} collective-permute-done((s16[200,640]{1,0:T(8,128)(2,1)S(1)}, s16[200,640]{1,0:T(8,128)(2,1)S(1)}, u32[]{:S(2)}, u32[]{:S(2)}) %collective-permute-start.12) | collective-permute-done | bytes 256032 | tf_op jit(solution)/shard_map/sum_products/ppermute | solution.py:481
  51.7 0.3 near_0.1
  52.1 0.0 copy-start.2
  52.1 0.0 collective-permute-done.11.got_ref
  52.1 0.3 near_640.1
  52.4 1.3 %collective-permute-start.16 = (s16[200,1152]{1,0:T(8,128)(2,1)S(1)}, s16[200,1152]{1,0:T(8,128)(2,1)S(1)}, u32[]{:S(2)}, u32[]{:S(2)}) collective-permute-start(s16[200,1152]{1,0:T(8,128)(2,1)S(1)} %get-tuple-element.68), channel_id=1, source_target_pairs={{0,6},{1,7},{2,0},{3,1},{4,2},{5,3},{6,4},{7,5},{8,14},{9,15},{10,... | collective-permute-start | bytes 1382408 | tf_op jit(solution)/shard_map/sum_products/ppermute | solution.py:490
  53.7 0.2 collective-permute-start.15
  53.9 0.0 collective-permute-done.14
  53.9 0.0 collective-permute-done.13
  54.0 0.0 copy-start
  54.0 2.9 %collective-permute-start.17 = (f32[256,128]{1,0:T(8,128)S(1)}, f32[256,128]{1,0:T(8,128)S(1)}, u32[]{:S(2)}, u32[]{:S(2)}) collective-permute-start(f32[256,128]{1,0:T(8,128)S(1)} %pad_maximum_fusion.through_ref), channel_id=1, source_target_pairs={{0,1},{1,0},{2,3},{3,2},{4,5},{5,4},{6,7},{7,6},{8,9},{9,8},{10,11... | collective-permute-start | bytes 393224 | tf_op jit(solution)/shard_map/sum_gram/ppermute | solution.py:493
  56.9 0.0 copy-done.2
  56.9 3.2 %products_own.1 = (f32[192,1152]{1,0:T(8,128)S(1)}, f32[8,1152]{1,0:T(8,128)S(1)}, f32[256,128]{1,0:T(8,128)S(1)}) custom-call(s32[3,64]{1,0:T(4,128)S(1)} %copy-done.2, bf16[9216,512]{1,0:T(8,128)(2,1)} %e_ref.9, bf16[9216,512]{1,0:T(8,128)(2,1)} %collective-permute-done.r_ref, bf16[192,512]{1,0:T(8,128)(2,1)S(1)} %order.1.mine_ref, ...), custom_call_target="tpu_custom_call" | custom-call | flops 1000000 | bytes 65536 | tf_op jit(solution)/shard_map/products_own/pallas_call | solution.py:396
  60.1 0.0 collective-permute-done.17.swapped_ref
  60.1 6.6 %factor.1 = (bf16[192,192]{1,0:T(8,128)(2,1)S(1)}, bf16[192,192]{1,0:T(8,128)(2,1)S(1)}) custom-call(f32[256,128]{1,0:T(8,128)S(1)} %get-tuple-element.69.sum_ref, f32[256,128]{1,0:T(8,128)S(1)} %collective-permute-done.17.swapped_ref), custom_call_target="tpu_custom_call" | custom-call | flops 1000000 | bytes 65536 | tf_op jit(solution)/shard_map/factor/pallas_call | solution.py:260
  66.7 0.0 collective-permute-done.16.g2
  66.7 0.0 collective-permute-done.15.g1
  66.7 0.0 copy-done
  66.7 2.1 %finish.1 = (f32[192,1152]{1,0:T(8,128)}, f32[1152]{0:T(1024)}) custom-call(f32[1152]{0:T(1024)S(1)} %copy-done, f32[192,1152]{1,0:T(8,128)S(1)} %get-tuple-element.65.own_ref, f32[8,1152]{1,0:T(8,128)S(1)} %get-tuple-element.66.norm_ref, s16[200,1152]{1,0:T(8,128)(2,1)S(1)} %collective-permute-done.15.g1, s16[200,1152]{1,0:T(8,128)(2,1)S(1)} %collective-permute-done.16.g2, ...), custom_call_target="tpu_custom_call" | custom-call | flops 509607936 | bytes 4194304 | tf_op jit(solution)/shard_map/finish/pallas_call | solution.py:427
  (7 shorter events, 0.1 us)
Async XLA Ops:
  0.6 19.7 %collective-permute-start = (bf16[9216,512]{1,0:T(8,128)(2,1)}, bf16[9216,512]{1,0:T(8,128)(2,1)}, u32[]{:S(2)}, u32[]{:S(2)}) collective-permute-start(bf16[9216,512]{1,0:T(8,128)(2,1)} %e_ref.9), channel_id=1, source_target_pairs={{0,1},{1,0},{2,3},{3,2},{4,5},{5,4},{6,7},{7,6},{8,9},{9,8},{10,11... | collective-permute-start | bytes 28311560 | tf_op jit(solution)/shard_map/swap_rows/ppermute | solution.py:458
  4.0 0.7 copy-start.1
  8.3 4.7 %collective-permute-start.1 = (bf16[48,512]{1,0:T(8,128)(2,1)S(1)}, bf16[48,512]{1,0:T(8,128)(2,1)S(1)}, u32[]{:S(2)}, u32[]{:S(2)}) collective-permute-start(bf16[48,512]{1,0:T(8,128)(2,1)S(1)} %get-tuple-element.39), channel_id=1, source_target_pairs={{0,24},{8,16},{16,8},{24,0},{32,56},{40,48},{48,40},{56,32},{64,88... | collective-permute-start | bytes 147464 | tf_op jit(solution)/shard_map/gather_picks/ppermute | solution.py:464
  9.5 4.4 %collective-permute-start.2 = (bf16[48,512]{1,0:T(8,128)(2,1)S(1)}, bf16[48,512]{1,0:T(8,128)(2,1)S(1)}, u32[]{:S(2)}, u32[]{:S(2)}) collective-permute-start(bf16[48,512]{1,0:T(8,128)(2,1)S(1)} %get-tuple-element.40), channel_id=1, source_target_pairs={{0,16},{8,24},{16,0},{24,8},{32,48},{40,56},{48,32},{56,40},{64,80... | collective-permute-start | bytes 147464 | tf_op jit(solution)/shard_map/gather_picks/ppermute | solution.py:464
  9.8 4.5 %collective-permute-start.3 = (bf16[48,512]{1,0:T(8,128)(2,1)S(1)}, bf16[48,512]{1,0:T(8,128)(2,1)S(1)}, u32[]{:S(2)}, u32[]{:S(2)}) collective-permute-start(bf16[48,512]{1,0:T(8,128)(2,1)S(1)} %get-tuple-element.41), channel_id=1, source_target_pairs={{0,8},{8,0},{16,24},{24,16},{32,40},{40,32},{48,56},{56,48},{64,72... | collective-permute-start | bytes 147464 | tf_op jit(solution)/shard_map/gather_picks/ppermute | solution.py:464
  14.3 3.0 %collective-permute-start.4 = (bf16[48,512]{1,0:T(8,128)(2,1)S(1)}, bf16[48,512]{1,0:T(8,128)(2,1)S(1)}, u32[]{:S(2)}, u32[]{:S(2)}) collective-permute-start(bf16[48,512]{1,0:T(8,128)(2,1)S(1)} %add_add_fusion), channel_id=1, source_target_pairs={{0,32},{8,40},{16,48},{24,56},{32,0},{40,8},{48,16},{56,24},{64,96... | collective-permute-start | bytes 147464 | tf_op jit(solution)/shard_map/gather_picks/ppermute | solution.py:466
  17.3 5.1 %collective-permute-start.5 = (bf16[48,512]{1,0:T(8,128)(2,1)S(1)}, bf16[48,512]{1,0:T(8,128)(2,1)S(1)}, u32[]{:S(2)}, u32[]{:S(2)}) collective-permute-start(bf16[48,512]{1,0:T(8,128)(2,1)S(1)} %add.30.through_ref), channel_id=1, source_target_pairs={{0,64},{8,72},{16,80},{24,88},{32,96},{40,104},{48,112},{56,120},{... | collective-permute-start | bytes 147464 | tf_op jit(solution)/shard_map/gather_picks/ppermute | solution.py:467
  22.5 6.8 %collective-permute-start.6 = (bf16[48,512]{1,0:T(8,128)(2,1)S(1)}, bf16[48,512]{1,0:T(8,128)(2,1)S(1)}, u32[]{:S(2)}, u32[]{:S(2)}) collective-permute-start(bf16[48,512]{1,0:T(8,128)(2,1)S(1)} %add.31.through_ref), channel_id=1, source_target_pairs={{0,224},{8,232},{16,240},{24,248},{32,192},{40,200},{48,208},{56,2... | collective-permute-start | bytes 147464 | tf_op jit(solution)/shard_map/gather_picks/ppermute | solution.py:470
  29.3 5.5 %collective-permute-start.9 = (bf16[48,512]{1,0:T(8,128)(2,1)S(1)}, bf16[48,512]{1,0:T(8,128)(2,1)S(1)}, u32[]{:S(2)}, u32[]{:S(2)}) collective-permute-start(bf16[48,512]{1,0:T(8,128)(2,1)S(1)} %add.32.through_ref), channel_id=1, source_target_pairs={{0,24},{8,16},{16,8},{24,0},{32,56},{40,48},{48,40},{56,32},{64,88... | collective-permute-start | bytes 147464 | tf_op jit(solution)/shard_map/gather_picks/ppermute | solution.py:473
  31.0 4.4 %collective-permute-start.8 = (bf16[48,512]{1,0:T(8,128)(2,1)S(1)}, bf16[48,512]{1,0:T(8,128)(2,1)S(1)}, u32[]{:S(2)}, u32[]{:S(2)}) collective-permute-start(bf16[48,512]{1,0:T(8,128)(2,1)S(1)} %add.32.through_ref), channel_id=1, source_target_pairs={{0,16},{8,24},{16,0},{24,8},{32,48},{40,56},{48,32},{56,40},{64,80... | collective-permute-start | bytes 147464 | tf_op jit(solution)/shard_map/gather_picks/ppermute | solution.py:473
  31.0 4.4 %collective-permute-start.7 = (bf16[48,512]{1,0:T(8,128)(2,1)S(1)}, bf16[48,512]{1,0:T(8,128)(2,1)S(1)}, u32[]{:S(2)}, u32[]{:S(2)}) collective-permute-start(bf16[48,512]{1,0:T(8,128)(2,1)S(1)} %add.32.through_ref), channel_id=1, source_target_pairs={{0,8},{8,0},{16,24},{24,16},{32,40},{40,32},{48,56},{56,48},{64,72... | collective-permute-start | bytes 147464 | tf_op jit(solution)/shard_map/gather_picks/ppermute | solution.py:473
  35.5 6.6 %collective-permute-start.10 = (bf16[192,512]{1,0:T(8,128)(2,1)S(1)}, bf16[192,512]{1,0:T(8,128)(2,1)S(1)}, u32[]{:S(2)}, u32[]{:S(2)}) collective-permute-start(bf16[192,512]{1,0:T(8,128)(2,1)S(1)} %order.1.mine_ref), channel_id=1, source_target_pairs={{0,1},{1,0},{2,3},{3,2},{4,5},{5,4},{6,7},{7,6},{8,9},{9,8},{10,11... | collective-permute-start | bytes 589832 | tf_op jit(solution)/shard_map/gather_picks/ppermute | solution.py:477
  43.1 8.7 %collective-permute-start.12 = (s16[200,640]{1,0:T(8,128)(2,1)S(1)}, s16[200,640]{1,0:T(8,128)(2,1)S(1)}, u32[]{:S(2)}, u32[]{:S(2)}) collective-permute-start(s16[200,640]{1,0:T(8,128)(2,1)S(1)} %get-tuple-element.59), channel_id=1, source_target_pairs={{0,2},{1,3},{2,4},{3,5},{4,6},{5,7},{6,0},{7,1},{8,10},{9,11},{10,... | collective-permute-start | bytes 768008 | tf_op jit(solution)/shard_map/sum_products/ppermute | solution.py:481
  44.4 7.7 %collective-permute-start.11 = (s16[200,512]{1,0:T(8,128)(2,1)S(1)}, s16[200,512]{1,0:T(8,128)(2,1)S(1)}, u32[]{:S(2)}, u32[]{:S(2)}) collective-permute-start(s16[200,512]{1,0:T(8,128)(2,1)S(1)} %get-tuple-element.56), channel_id=1, source_target_pairs={{0,6},{1,7},{2,0},{3,1},{4,2},{5,3},{6,4},{7,5},{8,14},{9,15},{10,... | collective-permute-start | bytes 614408 | tf_op jit(solution)/shard_map/sum_products/ppermute | solution.py:482
  46.1 7.8 %collective-permute-start.13 = (f32[256,128]{1,0:T(8,128)S(1)}, f32[256,128]{1,0:T(8,128)S(1)}, u32[]{:S(2)}, u32[]{:S(2)}) collective-permute-start(f32[256,128]{1,0:T(8,128)S(1)} %get-tuple-element.63), channel_id=1, source_target_pairs={{0,2},{1,7},{2,4},{3,1},{4,6},{5,3},{6,0},{7,5},{8,10},{9,15},{10,... | collective-permute-start | bytes 393224 | tf_op jit(solution)/shard_map/sum_products/ppermute | solution.py:484
  47.6 6.3 %collective-permute-start.14 = (f32[128,128]{1,0:T(8,128)S(1)}, f32[128,128]{1,0:T(8,128)S(1)}, u32[]{:S(2)}, u32[]{:S(2)}) collective-permute-start(f32[128,128]{1,0:T(8,128)S(1)} %get-tuple-element.64), channel_id=1, source_target_pairs={{0,4},{1,5},{2,6},{3,7},{4,0},{5,1},{6,2},{7,3},{8,12},{9,13},{10,... | collective-permute-start | bytes 196616 | tf_op jit(solution)/shard_map/sum_products/ppermute | solution.py:485
  52.1 4.8 %copy-start.2 = (s32[3,64]{1,0:T(4,128)S(1)}, s32[3,64]{1,0:T(4,128)}, u32[]{:S(2)}) copy-start(s32[3,64]{1,0:T(4,128)} %picks_ref.3) | copy-start | bytes 2308
  52.4 14.3 %collective-permute-start.16 = (s16[200,1152]{1,0:T(8,128)(2,1)S(1)}, s16[200,1152]{1,0:T(8,128)(2,1)S(1)}, u32[]{:S(2)}, u32[]{:S(2)}) collective-permute-start(s16[200,1152]{1,0:T(8,128)(2,1)S(1)} %get-tuple-element.68), channel_id=1, source_target_pairs={{0,6},{1,7},{2,0},{3,1},{4,2},{5,3},{6,4},{7,5},{8,14},{9,15},{10,... | collective-permute-start | bytes 1382408 | tf_op jit(solution)/shard_map/sum_products/ppermute | solution.py:490
  53.7 13.0 %collective-permute-start.15 = (s16[200,1152]{1,0:T(8,128)(2,1)S(1)}, s16[200,1152]{1,0:T(8,128)(2,1)S(1)}, u32[]{:S(2)}, u32[]{:S(2)}) collective-permute-start(s16[200,1152]{1,0:T(8,128)(2,1)S(1)} %get-tuple-element.67), channel_id=1, source_target_pairs={{0,2},{1,3},{2,4},{3,5},{4,6},{5,7},{6,0},{7,1},{8,10},{9,11},{10,... | collective-permute-start | bytes 1382408 | tf_op jit(solution)/shard_map/sum_products/ppermute | solution.py:488
  54.0 12.7 %copy-start = (f32[1152]{0:T(1024)S(1)}, f32[1152]{0:T(1024)}, u32[]{:S(2)}) copy-start(f32[1152]{0:T(1024)} %quality_ref.1) | copy-start | bytes 13828
  54.0 6.1 %collective-permute-start.17 = (f32[256,128]{1,0:T(8,128)S(1)}, f32[256,128]{1,0:T(8,128)S(1)}, u32[]{:S(2)}, u32[]{:S(2)}) collective-permute-start(f32[256,128]{1,0:T(8,128)S(1)} %pad_maximum_fusion.through_ref), channel_id=1, source_target_pairs={{0,1},{1,0},{2,3},{3,2},{4,5},{5,4},{6,7},{7,6},{8,9},{9,8},{10,11... | collective-permute-start | bytes 393224 | tf_op jit(solution)/shard_map/sum_gram/ppermute | solution.py:493

commit v5 on v4

--- a/solution.py
+++ b/solution.py
@@ -233,18 +233,23 @@
         left = low // 128 * 128
         off = low - left
         tiles = [m_ref[low : low + panel, j : j + 128] for j in range(left, width, 128)]
+        done = []
         for g in range(0, panel, together):
+            height = panel - g
             cols = [
-                jnp.broadcast_to(tiles[0][:, off + g + i : off + g + i + 1], (panel, 128)) for i in range(together)
+                jnp.broadcast_to(tiles[0][:, off + g + i : off + g + i + 1], (height, 128)) for i in range(together)
             ]
-            heads = [[t[g + i : g + i + 1, :] for t in tiles] for i in range(together)]
+            heads = [[t[i : i + 1, :] for t in tiles] for i in range(together)]
             for i in range(together):
-                factors = jnp.where(below > g + i, cols[i] * (1.0 / cols[i][g + i : g + i + 1, :]), 0.0)
+                factors = jnp.where(below[:height] > i, cols[i] * (1.0 / cols[i][i : i + 1, :]), 0.0)
                 for j in range(i + 1, together):
-                    cols[j] = cols[j] - factors * cols[j][g + i : g + i + 1, :]
-                    by = factors[g + j : g + j + 1, :]
+                    cols[j] = cols[j] - factors * cols[j][i : i + 1, :]
+                    by = factors[j : j + 1, :]
                     heads[j] = [x - by * y for x, y in zip(heads[j], heads[i])]
                 tiles = [t - factors * y for t, y in zip(tiles, heads[i])]
+            done.append([t[:together, :] for t in tiles])
+            tiles = [t[together:, :] for t in tiles]
+        tiles = [jnp.concatenate(pieces, axis=0) for pieces in zip(*done)]
         pivots = jnp.sum(jnp.where(at == off, tiles[0], 0.0), axis=1, keepdims=True)
         rows = jnp.concatenate(tiles, axis=1) * (1.0 / jnp.sqrt(pivots))
         inverse = rows[:, n - left :]
@@ -270,13 +275,13 @@
 
 
 def split(value):
-    scaled = value * 16.0
+    scaled = value * 8.0
     high = jnp.floor(scaled)
     return high, jnp.floor((scaled - high) * 32768.0)
 
 
 def join(high, low):
-    return (high + low * (1.0 / 32768.0)) * (1.0 / 16.0)
+    return (high + low * (1.0 / 32768.0)) * (1.0 / 8.0)
 
 
 def block_products(at, e_ref, r_ref, mine_ref, other_ref):
@@ -399,10 +404,9 @@
 def finish_kernel(quality_ref, own_ref, norm_ref, g1, g2, inv_high, inv_low, out_ref, resid_ref, stage_ref, sent):
     total, width = own_ref.shape
     inverse_high, inverse_low = inv_high[...], inv_low[...]
-    tile = width // 3
     copies = []
-    for i in range(3):
-        here = pl.ds(i * tile, tile)
+    for i, (start, tile) in enumerate(((0, 512), (512, 384), (896, 256))):
+        here = pl.ds(start, tile)
         values, norm = own_ref[:, here], norm_ref[:1, here]
         for ref in (g1, g2):
             more, more_norm = decoded(ref, here, total)

time: 68.9 us -> 68.7 us (level)
  transfers between devices with their start and end apart: 18 -> 18, of which waited for: 7 -> 7; matrix products, arithmetic and copies ran while one was open for 0% -> 0% of each run, Pallas kernels for 32% -> 33%
where the time goes in v5:
time: 68.7 us; the launch traced here: 68.1 us
  starting transfers between devices  33.1 us (48%)
  Pallas kernels  25.3 us (37%)
  waiting for transfers between devices  7.92 us (12%)
  between operations  0.99 us (1%)
  local copies, waits for them, and re-layouts  0.69 us (1%)
    pallas_call x3, Pallas kernels, stage(): pl.pallas_call(functools.partial(stage_kernel, hop), in_specs=[ANY, ANY,...  6.43 us
    pallas_call x1, Pallas kernels, factor_inverse(): pl.pallas_call(factor_kernel, in_specs=[VMEM] * 2, out_specs=[VMEM] * 2,...  6.42 us
    ppermute x1, starting transfers between devices, per_device(): pick_other = lax.ppermute(pick_mine, 'dim', swap)  5.57 us
    ppermute x1, starting transfers between devices, per_device(): arrived = lax.ppermute(mine, 'rows', along_z(lambda z: z ^ 7))  4.12 us
    pallas_call x1, Pallas kernels, local_picks(): pl.pallas_call(pick_kernel, in_specs=[pl.BlockSpec(memory_space=pltpu.SME...  3.72 us
    ppermute x3, starting transfers between devices, per_device(): mine = mine + lax.ppermute(parts[k], 'rows', along_y(k))  3.34 us
    ppermute x3, starting transfers between devices, per_device(): lax.ppermute(mine, 'rows', along_y(k))  3.34 us
    ppermute x1, starting transfers between devices, per_device(): received = lax.ppermute(embeddings, 'dim', swap)  3.33 us
  transfers between devices with their start and end apart: 18, of which 7 were waited for; matrix products, arithmetic and copies ran while one was open for 0% of the time, Pallas kernels for 33%

profile of v5, /device:TPU:1, one launch (start us, length us, event | category | flops | bytes accessed | tf_op | source)
XLA Modules:
  0.0 68.1 jit_solution(6554514647344375744)
XLA Ops:
  0.6 3.3 %collective-permute-start = (bf16[9216,512]{1,0:T(8,128)(2,1)}, bf16[9216,512]{1,0:T(8,128)(2,1)}, u32[]{:S(2)}, u32[]{:S(2)}) collective-permute-start(bf16[9216,512]{1,0:T(8,128)(2,1)} %e_ref.9), channel_id=1, source_target_pairs={{0,1},{1,0},{2,3},{3,2},{4,5},{5,4},{6,7},{7,6},{8,9},{9,8},{10,11... | collective-permute-start | bytes 28311560 | tf_op jit(solution)/shard_map/swap_rows/ppermute | solution.py:462
  4.0 0.0 copy-start.1
  4.0 0.7 copy-done.1
  4.6 3.7 %local_picks.1 = (bf16[48,512]{1,0:T(8,128)(2,1)S(1)}, bf16[48,512]{1,0:T(8,128)(2,1)S(1)}, bf16[48,512]{1,0:T(8,128)(2,1)S(1)}, bf16[48,512]{1,0:T(8,128)(2,1)S(1)}) custom-call(s32[3,64]{1,0:T(4,128)S(1)} %copy-done.1, bf16[9216,512]{1,0:T(8,128)(2,1)} %e_ref.9), custom_call_target="tpu_custom_call" | custom-call | bytes 10485760 | tf_op jit(solution)/shard_map/gather_picks/local_picks/pallas_call | solution.py:83
  8.4 1.2 %collective-permute-start.1 = (bf16[48,512]{1,0:T(8,128)(2,1)S(1)}, bf16[48,512]{1,0:T(8,128)(2,1)S(1)}, u32[]{:S(2)}, u32[]{:S(2)}) collective-permute-start(bf16[48,512]{1,0:T(8,128)(2,1)S(1)} %get-tuple-element.39), channel_id=1, source_target_pairs={{0,24},{8,16},{16,8},{24,0},{32,56},{40,48},{48,40},{56,32},{64,88... | collective-permute-start | bytes 147464 | tf_op jit(solution)/shard_map/gather_picks/ppermute | solution.py:468
  9.6 0.4 collective-permute-start.2
  10.0 1.7 %collective-permute-start.3 = (bf16[48,512]{1,0:T(8,128)(2,1)S(1)}, bf16[48,512]{1,0:T(8,128)(2,1)S(1)}, u32[]{:S(2)}, u32[]{:S(2)}) collective-permute-start(bf16[48,512]{1,0:T(8,128)(2,1)S(1)} %get-tuple-element.41), channel_id=1, source_target_pairs={{0,8},{8,0},{16,24},{24,16},{32,40},{40,32},{48,56},{56,48},{64,72... | collective-permute-start | bytes 147464 | tf_op jit(solution)/shard_map/gather_picks/ppermute | solution.py:468
  11.7 1.3 %collective-permute-done.1 = bf16[48,512]{1,0:T(8,128)(2,1)S(1)} collective-permute-done((bf16[48,512]{1,0:T(8,128)(2,1)S(1)}, bf16[48,512]{1,0:T(8,128)(2,1)S(1)}, u32[]{:S(2)}, u32[]{:S(2)}) %collective-permute-start.1) | collective-permute-done | bytes 49184 | tf_op jit(solution)/shard_map/gather_picks/ppermute | solution.py:468
  13.0 1.0 %collective-permute-done.2 = bf16[48,512]{1,0:T(8,128)(2,1)S(1)} collective-permute-done((bf16[48,512]{1,0:T(8,128)(2,1)S(1)}, bf16[48,512]{1,0:T(8,128)(2,1)S(1)}, u32[]{:S(2)}, u32[]{:S(2)}) %collective-permute-start.2) | collective-permute-done | bytes 49184 | tf_op jit(solution)/shard_map/gather_picks/ppermute | solution.py:468
  14.0 0.3 collective-permute-done.3
  14.4 1.4 %collective-permute-start.4 = (bf16[48,512]{1,0:T(8,128)(2,1)S(1)}, bf16[48,512]{1,0:T(8,128)(2,1)S(1)}, u32[]{:S(2)}, u32[]{:S(2)}) collective-permute-start(bf16[48,512]{1,0:T(8,128)(2,1)S(1)} %add_add_fusion), channel_id=1, source_target_pairs={{0,32},{8,40},{16,48},{24,56},{32,0},{40,8},{48,16},{56,24},{64,96... | collective-permute-start | bytes 147464 | tf_op jit(solution)/shard_map/gather_picks/ppermute | solution.py:470
  15.7 1.6 %collective-permute-done.4 = bf16[48,512]{1,0:T(8,128)(2,1)S(1)} collective-permute-done((bf16[48,512]{1,0:T(8,128)(2,1)S(1)}, bf16[48,512]{1,0:T(8,128)(2,1)S(1)}, u32[]{:S(2)}, u32[]{:S(2)}) %collective-permute-start.4) | collective-permute-done | bytes 49184 | tf_op jit(solution)/shard_map/gather_picks/ppermute | solution.py:470
  17.4 2.8 %collective-permute-start.5 = (bf16[48,512]{1,0:T(8,128)(2,1)S(1)}, bf16[48,512]{1,0:T(8,128)(2,1)S(1)}, u32[]{:S(2)}, u32[]{:S(2)}) collective-permute-start(bf16[48,512]{1,0:T(8,128)(2,1)S(1)} %add.30.through_ref), channel_id=1, source_target_pairs={{0,64},{8,72},{16,80},{24,88},{32,96},{40,104},{48,112},{56,120},{... | collective-permute-start | bytes 147464 | tf_op jit(solution)/shard_map/gather_picks/ppermute | solution.py:471
  20.2 0.0 collective-permute-done.r_ref
  20.2 2.1 %stage_2.1 = (bf16[1152,512]{1,0:T(8,128)(2,1)S(1)}, bf16[1152,512]{1,0:T(8,128)(2,1)S(1)}, f32[8,1152]{1,0:T(8,128)S(1)}, bf16[48,512]{1,0:T(8,128)(2,1)S(1)}) custom-call(bf16[9216,512]{1,0:T(8,128)(2,1)} %e_ref.9, bf16[9216,512]{1,0:T(8,128)(2,1)} %collective-permute-done.r_ref, bf16[48,512]{1,0:T(8,128)(2,1)S(1)} %add.30.through_ref), custom_call_target="tpu_custom_call" | custom-call | bytes 2359296 | tf_op jit(solution)/shard_map/gather_picks/stage_2/pallas_call | solution.py:146
  22.4 0.0 collective-permute-done.5
  22.4 4.1 %collective-permute-start.6 = (bf16[48,512]{1,0:T(8,128)(2,1)S(1)}, bf16[48,512]{1,0:T(8,128)(2,1)S(1)}, u32[]{:S(2)}, u32[]{:S(2)}) collective-permute-start(bf16[48,512]{1,0:T(8,128)(2,1)S(1)} %add.31.through_ref), channel_id=1, source_target_pairs={{0,224},{8,232},{16,240},{24,248},{32,192},{40,200},{48,208},{56,2... | collective-permute-start | bytes 147464 | tf_op jit(solution)/shard_map/gather_picks/ppermute | solution.py:474
  26.5 2.1 %stage_1.1 = (bf16[1152,512]{1,0:T(8,128)(2,1)S(1)}, bf16[1152,512]{1,0:T(8,128)(2,1)S(1)}, f32[8,1152]{1,0:T(8,128)S(1)}, bf16[48,512]{1,0:T(8,128)(2,1)S(1)}) custom-call(bf16[9216,512]{1,0:T(8,128)(2,1)} %e_ref.9, bf16[9216,512]{1,0:T(8,128)(2,1)} %collective-permute-done.r_ref, bf16[48,512]{1,0:T(8,128)(2,1)S(1)} %add.31.through_ref), custom_call_target="tpu_custom_call" | custom-call | bytes 2359296 | tf_op jit(solution)/shard_map/gather_picks/stage_1/pallas_call | solution.py:146
  28.7 0.0 collective-permute-done.6
  28.7 1.6 %collective-permute-start.9 = (bf16[48,512]{1,0:T(8,128)(2,1)S(1)}, bf16[48,512]{1,0:T(8,128)(2,1)S(1)}, u32[]{:S(2)}, u32[]{:S(2)}) collective-permute-start(bf16[48,512]{1,0:T(8,128)(2,1)S(1)} %add.32.through_ref), channel_id=1, source_target_pairs={{0,24},{8,16},{16,8},{24,0},{32,56},{40,48},{48,40},{56,32},{64,88... | collective-permute-start | bytes 147464 | tf_op jit(solution)/shard_map/gather_picks/ppermute | solution.py:477
  30.3 1.2 %collective-permute-start.8 = (bf16[48,512]{1,0:T(8,128)(2,1)S(1)}, bf16[48,512]{1,0:T(8,128)(2,1)S(1)}, u32[]{:S(2)}, u32[]{:S(2)}) collective-permute-start(bf16[48,512]{1,0:T(8,128)(2,1)S(1)} %add.32.through_ref), channel_id=1, source_target_pairs={{0,16},{8,24},{16,0},{24,8},{32,48},{40,56},{48,32},{56,40},{64,80... | collective-permute-start | bytes 147464 | tf_op jit(solution)/shard_map/gather_picks/ppermute | solution.py:477
  31.4 0.6 collective-permute-start.7
  32.1 2.1 %stage_3.1 = (bf16[1152,512]{1,0:T(8,128)(2,1)S(1)}, bf16[1152,512]{1,0:T(8,128)(2,1)S(1)}, f32[8,1152]{1,0:T(8,128)S(1)}, bf16[48,512]{1,0:T(8,128)(2,1)S(1)}) custom-call(bf16[9216,512]{1,0:T(8,128)(2,1)} %e_ref.9, bf16[9216,512]{1,0:T(8,128)(2,1)} %collective-permute-done.r_ref, bf16[48,512]{1,0:T(8,128)(2,1)S(1)} %add.32.through_ref), custom_call_target="tpu_custom_call" | custom-call | bytes 2359296 | tf_op jit(solution)/shard_map/gather_picks/stage_3/pallas_call | solution.py:146
  34.2 0.0 collective-permute-done.9.s3
  34.2 0.5 collective-permute-done.8.s2
  34.7 0.0 collective-permute-done.7.s1
  34.8 5.6 %collective-permute-start.10 = (bf16[192,512]{1,0:T(8,128)(2,1)S(1)}, bf16[192,512]{1,0:T(8,128)(2,1)S(1)}, u32[]{:S(2)}, u32[]{:S(2)}) collective-permute-start(bf16[192,512]{1,0:T(8,128)(2,1)S(1)} %order.1.mine_ref), channel_id=1, source_target_pairs={{0,1},{1,0},{2,3},{3,2},{4,5},{5,4},{6,7},{7,6},{8,9},{9,8},{10,11... | collective-permute-start | bytes 589832 | tf_op jit(solution)/shard_map/gather_picks/ppermute | solution.py:481
  40.3 1.1 %collective-permute-done.10.other_ref = bf16[192,512]{1,0:T(8,128)(2,1)S(1)} collective-permute-done((bf16[192,512]{1,0:T(8,128)(2,1)S(1)}, bf16[192,512]{1,0:T(8,128)(2,1)S(1)}, u32[]{:S(2)}, u32[]{:S(2)}) %collective-permute-start.10) | collective-permute-done | bytes 196640 | tf_op jit(solution)/shard_map/gather_picks/ppermute | solution.py:481
  41.4 1.0 %products_far.1 = (s16[200,640]{1,0:T(8,128)(2,1)S(1)}, s16[200,512]{1,0:T(8,128)(2,1)S(1)}, f32[8,128]{1,0:T(8,128)S(1)}) custom-call(bf16[1152,512]{1,0:T(8,128)(2,1)S(1)} %get-tuple-element.49.e_ref, bf16[1152,512]{1,0:T(8,128)(2,1)S(1)} %get-tuple-element.50.r_ref, f32[8,1152]{1,0:T(8,128)S(1)} %get-tuple-element.51.norm_ref, ...), custom_call_target="tpu_custom_call" | custom-call | flops 1000000 | bytes 65536 | tf_op jit(solution)/shard_map/sum_products/products_far/pallas_call | solution.py:380
  42.4 1.3 %collective-permute-start.12 = (s16[200,640]{1,0:T(8,128)(2,1)S(1)}, s16[200,640]{1,0:T(8,128)(2,1)S(1)}, u32[]{:S(2)}, u32[]{:S(2)}) collective-permute-start(s16[200,640]{1,0:T(8,128)(2,1)S(1)} %get-tuple-element.59), channel_id=1, source_target_pairs={{0,2},{1,3},{2,4},{3,5},{4,6},{5,7},{6,0},{7,1},{8,10},{9,11},{10,... | collective-permute-start | bytes 768008 | tf_op jit(solution)/shard_map/sum_products/ppermute | solution.py:485
  43.7 1.5 %collective-permute-start.11 = (s16[200,512]{1,0:T(8,128)(2,1)S(1)}, s16[200,512]{1,0:T(8,128)(2,1)S(1)}, u32[]{:S(2)}, u32[]{:S(2)}) collective-permute-start(s16[200,512]{1,0:T(8,128)(2,1)S(1)} %get-tuple-element.56), channel_id=1, source_target_pairs={{0,6},{1,7},{2,0},{3,1},{4,2},{5,3},{6,4},{7,5},{8,14},{9,15},{10,... | collective-permute-start | bytes 614408 | tf_op jit(solution)/shard_map/sum_products/ppermute | solution.py:486
  45.2 0.3 gram.1
  45.5 1.5 %collective-permute-start.13 = (f32[256,128]{1,0:T(8,128)S(1)}, f32[256,128]{1,0:T(8,128)S(1)}, u32[]{:S(2)}, u32[]{:S(2)}) collective-permute-start(f32[256,128]{1,0:T(8,128)S(1)} %get-tuple-element.63), channel_id=1, source_target_pairs={{0,2},{1,7},{2,4},{3,1},{4,6},{5,3},{6,0},{7,5},{8,10},{9,15},{10,... | collective-permute-start | bytes 393224 | tf_op jit(solution)/shard_map/sum_products/ppermute | solution.py:488
  47.0 0.5 collective-permute-start.14
  47.5 1.5 %products_both.1 = (f32[192,1152]{1,0:T(8,128)S(1)}, f32[192,1152]{1,0:T(8,128)S(1)}, f32[256,128]{1,0:T(8,128)S(1)}) custom-call(bf16[1152,512]{1,0:T(8,128)(2,1)S(1)} %get-tuple-element.45.e_next, bf16[1152,512]{1,0:T(8,128)(2,1)S(1)} %get-tuple-element.46.r_next, bf16[1152,512]{1,0:T(8,128)(2,1)S(1)} %get-tuple-element.47.e_last, ...), custom_call_target="tpu_custom_call" | custom-call | flops 1000000 | bytes 65536 | tf_op jit(solution)/shard_map/sum_products/products_both/pallas_call | solution.py:386
  49.0 2.1 %collective-permute-done.12.got_ref = s16[200,640]{1,0:T(8,128)(2,1)S(1)} collective-permute-done((s16[200,640]{1,0:T(8,128)(2,1)S(1)}, s16[200,640]{1,0:T(8,128)(2,1)S(1)}, u32[]{:S(2)}, u32[]{:S(2)}) %collective-permute-start.12) | collective-permute-done | bytes 256032 | tf_op jit(solution)/shard_map/sum_products/ppermute | solution.py:485
  51.1 0.3 near_0.1
  51.4 0.0 copy-start.2
  51.4 0.0 collective-permute-done.11.got_ref
  51.4 0.3 near_640.1
  51.8 1.3 %collective-permute-start.16 = (s16[200,1152]{1,0:T(8,128)(2,1)S(1)}, s16[200,1152]{1,0:T(8,128)(2,1)S(1)}, u32[]{:S(2)}, u32[]{:S(2)}) collective-permute-start(s16[200,1152]{1,0:T(8,128)(2,1)S(1)} %get-tuple-element.68), channel_id=1, source_target_pairs={{0,6},{1,7},{2,0},{3,1},{4,2},{5,3},{6,4},{7,5},{8,14},{9,15},{10,... | collective-permute-start | bytes 1382408 | tf_op jit(solution)/shard_map/sum_products/ppermute | solution.py:494
  53.1 0.2 collective-permute-start.15
  53.3 0.0 collective-permute-done.14
  53.3 0.0 collective-permute-done.13
  53.3 0.0 copy-start
  53.4 2.9 %collective-permute-start.17 = (f32[256,128]{1,0:T(8,128)S(1)}, f32[256,128]{1,0:T(8,128)S(1)}, u32[]{:S(2)}, u32[]{:S(2)}) collective-permute-start(f32[256,128]{1,0:T(8,128)S(1)} %pad_maximum_fusion.through_ref), channel_id=1, source_target_pairs={{0,1},{1,0},{2,3},{3,2},{4,5},{5,4},{6,7},{7,6},{8,9},{9,8},{10,11... | collective-permute-start | bytes 393224 | tf_op jit(solution)/shard_map/sum_gram/ppermute | solution.py:497
  56.2 0.0 copy-done.2
  56.2 3.2 %products_own.1 = (f32[192,1152]{1,0:T(8,128)S(1)}, f32[8,1152]{1,0:T(8,128)S(1)}, f32[256,128]{1,0:T(8,128)S(1)}) custom-call(s32[3,64]{1,0:T(4,128)S(1)} %copy-done.2, bf16[9216,512]{1,0:T(8,128)(2,1)} %e_ref.9, bf16[9216,512]{1,0:T(8,128)(2,1)} %collective-permute-done.r_ref, bf16[192,512]{1,0:T(8,128)(2,1)S(1)} %order.1.mine_ref, ...), custom_call_target="tpu_custom_call" | custom-call | flops 1000000 | bytes 65536 | tf_op jit(solution)/shard_map/products_own/pallas_call | solution.py:401
  59.4 0.0 collective-permute-done.17.swapped_ref
  59.4 6.4 %factor.1 = (bf16[192,192]{1,0:T(8,128)(2,1)S(1)}, bf16[192,192]{1,0:T(8,128)(2,1)S(1)}) custom-call(f32[256,128]{1,0:T(8,128)S(1)} %get-tuple-element.69.sum_ref, f32[256,128]{1,0:T(8,128)S(1)} %collective-permute-done.17.swapped_ref), custom_call_target="tpu_custom_call" | custom-call | flops 1000000 | bytes 65536 | tf_op jit(solution)/shard_map/factor/pallas_call | solution.py:265
  65.8 0.0 collective-permute-done.16.g2
  65.8 0.0 collective-permute-done.15.g1
  65.9 0.0 copy-done
  65.9 2.1 %finish.1 = (f32[192,1152]{1,0:T(8,128)}, f32[1152]{0:T(1024)}) custom-call(f32[1152]{0:T(1024)S(1)} %copy-done, f32[192,1152]{1,0:T(8,128)S(1)} %get-tuple-element.65.own_ref, f32[8,1152]{1,0:T(8,128)S(1)} %get-tuple-element.66.norm_ref, s16[200,1152]{1,0:T(8,128)(2,1)S(1)} %collective-permute-done.15.g1, s16[200,1152]{1,0:T(8,128)(2,1)S(1)} %collective-permute-done.16.g2, ...), custom_call_target="tpu_custom_call" | custom-call | flops 509607936 | bytes 4194304 | tf_op jit(solution)/shard_map/finish/pallas_call | solution.py:431
  (7 shorter events, 0.1 us)
Async XLA Ops:
  0.6 19.6 %collective-permute-start = (bf16[9216,512]{1,0:T(8,128)(2,1)}, bf16[9216,512]{1,0:T(8,128)(2,1)}, u32[]{:S(2)}, u32[]{:S(2)}) collective-permute-start(bf16[9216,512]{1,0:T(8,128)(2,1)} %e_ref.9), channel_id=1, source_target_pairs={{0,1},{1,0},{2,3},{3,2},{4,5},{5,4},{6,7},{7,6},{8,9},{9,8},{10,11... | collective-permute-start | bytes 28311560 | tf_op jit(solution)/shard_map/swap_rows/ppermute | solution.py:462
  4.0 0.7 %copy-start.1 = (s32[3,64]{1,0:T(4,128)S(1)}, s32[3,64]{1,0:T(4,128)}, u32[]{:S(2)}) copy-start(s32[3,64]{1,0:T(4,128)} %picks_ref.3) | copy-start | bytes 2308
  8.4 4.7 %collective-permute-start.1 = (bf16[48,512]{1,0:T(8,128)(2,1)S(1)}, bf16[48,512]{1,0:T(8,128)(2,1)S(1)}, u32[]{:S(2)}, u32[]{:S(2)}) collective-permute-start(bf16[48,512]{1,0:T(8,128)(2,1)S(1)} %get-tuple-element.39), channel_id=1, source_target_pairs={{0,24},{8,16},{16,8},{24,0},{32,56},{40,48},{48,40},{56,32},{64,88... | collective-permute-start | bytes 147464 | tf_op jit(solution)/shard_map/gather_picks/ppermute | solution.py:468
  9.6 4.4 %collective-permute-start.2 = (bf16[48,512]{1,0:T(8,128)(2,1)S(1)}, bf16[48,512]{1,0:T(8,128)(2,1)S(1)}, u32[]{:S(2)}, u32[]{:S(2)}) collective-permute-start(bf16[48,512]{1,0:T(8,128)(2,1)S(1)} %get-tuple-element.40), channel_id=1, source_target_pairs={{0,16},{8,24},{16,0},{24,8},{32,48},{40,56},{48,32},{56,40},{64,80... | collective-permute-start | bytes 147464 | tf_op jit(solution)/shard_map/gather_picks/ppermute | solution.py:468
  10.0 4.4 %collective-permute-start.3 = (bf16[48,512]{1,0:T(8,128)(2,1)S(1)}, bf16[48,512]{1,0:T(8,128)(2,1)S(1)}, u32[]{:S(2)}, u32[]{:S(2)}) collective-permute-start(bf16[48,512]{1,0:T(8,128)(2,1)S(1)} %get-tuple-element.41), channel_id=1, source_target_pairs={{0,8},{8,0},{16,24},{24,16},{32,40},{40,32},{48,56},{56,48},{64,72... | collective-permute-start | bytes 147464 | tf_op jit(solution)/shard_map/gather_picks/ppermute | solution.py:468
  14.4 3.0 %collective-permute-start.4 = (bf16[48,512]{1,0:T(8,128)(2,1)S(1)}, bf16[48,512]{1,0:T(8,128)(2,1)S(1)}, u32[]{:S(2)}, u32[]{:S(2)}) collective-permute-start(bf16[48,512]{1,0:T(8,128)(2,1)S(1)} %add_add_fusion), channel_id=1, source_target_pairs={{0,32},{8,40},{16,48},{24,56},{32,0},{40,8},{48,16},{56,24},{64,96... | collective-permute-start | bytes 147464 | tf_op jit(solution)/shard_map/gather_picks/ppermute | solution.py:470
  17.4 5.0 %collective-permute-start.5 = (bf16[48,512]{1,0:T(8,128)(2,1)S(1)}, bf16[48,512]{1,0:T(8,128)(2,1)S(1)}, u32[]{:S(2)}, u32[]{:S(2)}) collective-permute-start(bf16[48,512]{1,0:T(8,128)(2,1)S(1)} %add.30.through_ref), channel_id=1, source_target_pairs={{0,64},{8,72},{16,80},{24,88},{32,96},{40,104},{48,112},{56,120},{... | collective-permute-start | bytes 147464 | tf_op jit(solution)/shard_map/gather_picks/ppermute | solution.py:471
  22.4 6.3 %collective-permute-start.6 = (bf16[48,512]{1,0:T(8,128)(2,1)S(1)}, bf16[48,512]{1,0:T(8,128)(2,1)S(1)}, u32[]{:S(2)}, u32[]{:S(2)}) collective-permute-start(bf16[48,512]{1,0:T(8,128)(2,1)S(1)} %add.31.through_ref), channel_id=1, source_target_pairs={{0,224},{8,232},{16,240},{24,248},{32,192},{40,200},{48,208},{56,2... | collective-permute-start | bytes 147464 | tf_op jit(solution)/shard_map/gather_picks/ppermute | solution.py:474
  28.7 5.5 %collective-permute-start.9 = (bf16[48,512]{1,0:T(8,128)(2,1)S(1)}, bf16[48,512]{1,0:T(8,128)(2,1)S(1)}, u32[]{:S(2)}, u32[]{:S(2)}) collective-permute-start(bf16[48,512]{1,0:T(8,128)(2,1)S(1)} %add.32.through_ref), channel_id=1, source_target_pairs={{0,24},{8,16},{16,8},{24,0},{32,56},{40,48},{48,40},{56,32},{64,88... | collective-permute-start | bytes 147464 | tf_op jit(solution)/shard_map/gather_picks/ppermute | solution.py:477
  30.3 4.4 %collective-permute-start.8 = (bf16[48,512]{1,0:T(8,128)(2,1)S(1)}, bf16[48,512]{1,0:T(8,128)(2,1)S(1)}, u32[]{:S(2)}, u32[]{:S(2)}) collective-permute-start(bf16[48,512]{1,0:T(8,128)(2,1)S(1)} %add.32.through_ref), channel_id=1, source_target_pairs={{0,16},{8,24},{16,0},{24,8},{32,48},{40,56},{48,32},{56,40},{64,80... | collective-permute-start | bytes 147464 | tf_op jit(solution)/shard_map/gather_picks/ppermute | solution.py:477
  31.4 3.3 %collective-permute-start.7 = (bf16[48,512]{1,0:T(8,128)(2,1)S(1)}, bf16[48,512]{1,0:T(8,128)(2,1)S(1)}, u32[]{:S(2)}, u32[]{:S(2)}) collective-permute-start(bf16[48,512]{1,0:T(8,128)(2,1)S(1)} %add.32.through_ref), channel_id=1, source_target_pairs={{0,8},{8,0},{16,24},{24,16},{32,40},{40,32},{48,56},{56,48},{64,72... | collective-permute-start | bytes 147464 | tf_op jit(solution)/shard_map/gather_picks/ppermute | solution.py:477
  34.8 6.6 %collective-permute-start.10 = (bf16[192,512]{1,0:T(8,128)(2,1)S(1)}, bf16[192,512]{1,0:T(8,128)(2,1)S(1)}, u32[]{:S(2)}, u32[]{:S(2)}) collective-permute-start(bf16[192,512]{1,0:T(8,128)(2,1)S(1)} %order.1.mine_ref), channel_id=1, source_target_pairs={{0,1},{1,0},{2,3},{3,2},{4,5},{5,4},{6,7},{7,6},{8,9},{9,8},{10,11... | collective-permute-start | bytes 589832 | tf_op jit(solution)/shard_map/gather_picks/ppermute | solution.py:481
  42.4 8.7 %collective-permute-start.12 = (s16[200,640]{1,0:T(8,128)(2,1)S(1)}, s16[200,640]{1,0:T(8,128)(2,1)S(1)}, u32[]{:S(2)}, u32[]{:S(2)}) collective-permute-start(s16[200,640]{1,0:T(8,128)(2,1)S(1)} %get-tuple-element.59), channel_id=1, source_target_pairs={{0,2},{1,3},{2,4},{3,5},{4,6},{5,7},{6,0},{7,1},{8,10},{9,11},{10,... | collective-permute-start | bytes 768008 | tf_op jit(solution)/shard_map/sum_products/ppermute | solution.py:485
  43.7 7.7 %collective-permute-start.11 = (s16[200,512]{1,0:T(8,128)(2,1)S(1)}, s16[200,512]{1,0:T(8,128)(2,1)S(1)}, u32[]{:S(2)}, u32[]{:S(2)}) collective-permute-start(s16[200,512]{1,0:T(8,128)(2,1)S(1)} %get-tuple-element.56), channel_id=1, source_target_pairs={{0,6},{1,7},{2,0},{3,1},{4,2},{5,3},{6,4},{7,5},{8,14},{9,15},{10,... | collective-permute-start | bytes 614408 | tf_op jit(solution)/shard_map/sum_products/ppermute | solution.py:486
  45.5 7.8 %collective-permute-start.13 = (f32[256,128]{1,0:T(8,128)S(1)}, f32[256,128]{1,0:T(8,128)S(1)}, u32[]{:S(2)}, u32[]{:S(2)}) collective-permute-start(f32[256,128]{1,0:T(8,128)S(1)} %get-tuple-element.63), channel_id=1, source_target_pairs={{0,2},{1,7},{2,4},{3,1},{4,6},{5,3},{6,0},{7,5},{8,10},{9,15},{10,... | collective-permute-start | bytes 393224 | tf_op jit(solution)/shard_map/sum_products/ppermute | solution.py:488
  47.0 6.3 %collective-permute-start.14 = (f32[128,128]{1,0:T(8,128)S(1)}, f32[128,128]{1,0:T(8,128)S(1)}, u32[]{:S(2)}, u32[]{:S(2)}) collective-permute-start(f32[128,128]{1,0:T(8,128)S(1)} %get-tuple-element.64), channel_id=1, source_target_pairs={{0,4},{1,5},{2,6},{3,7},{4,0},{5,1},{6,2},{7,3},{8,12},{9,13},{10,... | collective-permute-start | bytes 196616 | tf_op jit(solution)/shard_map/sum_products/ppermute | solution.py:489
  51.4 4.8 %copy-start.2 = (s32[3,64]{1,0:T(4,128)S(1)}, s32[3,64]{1,0:T(4,128)}, u32[]{:S(2)}) copy-start(s32[3,64]{1,0:T(4,128)} %picks_ref.3) | copy-start | bytes 2308
  51.8 14.1 %collective-permute-start.16 = (s16[200,1152]{1,0:T(8,128)(2,1)S(1)}, s16[200,1152]{1,0:T(8,128)(2,1)S(1)}, u32[]{:S(2)}, u32[]{:S(2)}) collective-permute-start(s16[200,1152]{1,0:T(8,128)(2,1)S(1)} %get-tuple-element.68), channel_id=1, source_target_pairs={{0,6},{1,7},{2,0},{3,1},{4,2},{5,3},{6,4},{7,5},{8,14},{9,15},{10,... | collective-permute-start | bytes 1382408 | tf_op jit(solution)/shard_map/sum_products/ppermute | solution.py:494
  53.1 12.7 %collective-permute-start.15 = (s16[200,1152]{1,0:T(8,128)(2,1)S(1)}, s16[200,1152]{1,0:T(8,128)(2,1)S(1)}, u32[]{:S(2)}, u32[]{:S(2)}) collective-permute-start(s16[200,1152]{1,0:T(8,128)(2,1)S(1)} %get-tuple-element.67), channel_id=1, source_target_pairs={{0,2},{1,3},{2,4},{3,5},{4,6},{5,7},{6,0},{7,1},{8,10},{9,11},{10,... | collective-permute-start | bytes 1382408 | tf_op jit(solution)/shard_map/sum_products/ppermute | solution.py:492
  53.3 12.5 %copy-start = (f32[1152]{0:T(1024)S(1)}, f32[1152]{0:T(1024)}, u32[]{:S(2)}) copy-start(f32[1152]{0:T(1024)} %quality_ref.1) | copy-start | bytes 13828
  53.4 6.1 %collective-permute-start.17 = (f32[256,128]{1,0:T(8,128)S(1)}, f32[256,128]{1,0:T(8,128)S(1)}, u32[]{:S(2)}, u32[]{:S(2)}) collective-permute-start(f32[256,128]{1,0:T(8,128)S(1)} %pad_maximum_fusion.through_ref), channel_id=1, source_target_pairs={{0,1},{1,0},{2,3},{3,2},{4,5},{5,4},{6,7},{7,6},{8,9},{9,8},{10,11... | collective-permute-start | bytes 393224 | tf_op jit(solution)/shard_map/sum_gram/ppermute | solution.py:497
